TPU v7x, 32 devices: a whole 2x2x4 slice. The times are simulated.
32 devices in a mesh: tm: 8 (over z, core), pts: 4 (over y, x).
Axes of the slice: x: 2, y: 2, z: 4, core: 2. Of those that a mesh axis runs over, the one named last changes fastest.
Arguments:
- snapshots: float32 [1024, 16384], P('tm', 'pts'), may hold values from -110 to 110
- weights: float32 [16384], P(('pts', 'tm')), may hold values from 0.25 to 12, as said below
Outputs:
- modes: float32 [2, 33, 31, 16384], P(None, None, None, ('pts', 'tm'))
- triangle: float32 [2, 33, 31, 31], replicated
Inputs may be any that keep to these rules, and one draw needn't show every extreme that they name: Positive weights.
All inputs are finite; a program needn't handle non-finite values.
Results may differ from a plain program's by a relative error of at most 0.00065.
Values sent between devices are 32-bit elements; how exact they have to be, the bound alone decides.
No kernel may reach another device: no remote copies, remote signals or barrier semaphores. Data moves between devices by JAX's collectives and lax.ppermute only.
A program may use at most 128 MiB of HBM per device.

v0:
```python
import functools
import math

import jax
import jax.numpy as jnp
import numpy as np
from jax import lax
from jax.experimental import pallas as pl
from jax.experimental.pallas import tpu as pltpu
from jax.sharding import PartitionSpec as P

SEG = 64
HOP = 32
NF = 33
NT = 1024
NB = 31
SLOTS = 32
GROUPS = 8
SIDE = 4
CUTS = 4
VMEM_BYTES = 24 * 1024 * 1024


def fourier_table():
    sample = np.arange(SEG, dtype=np.float64)[:, None]
    column = np.arange(SEG)[None, :]
    frequency = np.where(column < NF, column, column - HOP).astype(np.float64)
    window = 0.5 - 0.5 * np.cos(2.0 * math.pi * sample / SEG)
    phase_angle = 2.0 * math.pi * frequency * sample / SEG
    waveform = np.where(column < NF, np.cos(phase_angle), -np.sin(phase_angle))
    return (waveform * window / math.sqrt(3 * SEG / 8)).astype(np.float32)


def slices_of(value, count):
    parts = []
    for number in range(count):
        part = value.astype(jnp.bfloat16)
        parts.append(part)
        if number + 1 < count:
            value = value - part.astype(jnp.float32)
    return parts


def two_sum(a, b):
    total = a + b
    rest = total - a
    return total, (a - (total - rest)) + (b - rest)


def pair_add(a, b):
    high, low = two_sum(a[0], b[0])
    low = low + (a[1] + b[1])
    total = high + low
    return total, low - (total - high)


def pair_tree(values):
    while len(values) > 1:
        values = [pair_add(values[i], values[i + 1]) for i in range(0, len(values), 2)]
    return values[0]


def halves(a):
    shifted = a * 4097.0
    high = shifted - (shifted - a)
    return high, a - high


def pair_product(a, a_halves, b, b_halves):
    product = a[0] * b[0]
    (ah, al), (bh, bl) = a_halves, b_halves
    error = ((ah * bh - product) + ah * bl + al * bh) + al * bl
    return product, error + (a[0] * b[1] + a[1] * b[0])


def spectrum_body(table_t, records, spec_ref):
    t1, t2, t3 = slices_of(table_t, 3)
    left = jnp.concatenate([t1, t1, t1, t2, t2, t3], axis=1)
    x1, x2, x3 = slices_of(records, 3)
    points = records.shape[1]
    for b in range(NB):
        at = slice(HOP * b, HOP * b + SEG)
        right = jnp.concatenate([x1[at], x2[at], x3[at], x1[at], x2[at], x1[at]], axis=0)
        spec_ref[:, b, :] = jnp.dot(left, right, preferred_element_type=jnp.float32)
    spec_ref[:, NB, :] = jnp.zeros((SEG, points), jnp.float32)


def cut_rows(real, imag):
    top = jnp.maximum(jnp.max(jnp.abs(real), axis=1, keepdims=True), jnp.max(jnp.abs(imag), axis=1, keepdims=True))
    grid = top * (1.5 * 2.0**17)
    cuts = []
    for _ in range(CUTS):
        cut = ((real + grid) - grid, (imag + grid) - grid)
        real, imag = real - cut[0], imag - cut[1]
        grid = grid * 2.0**-7
        cuts.append(cut)
    return cuts


def gram_slot(real, imag, two_real):
    left, right = [], []
    for r, i in cut_rows(real, imag):
        left.append(jnp.concatenate([r, i], axis=1).astype(jnp.bfloat16))
        if two_real is None:
            across, own = i, -r
        else:
            across, own = i * (1.0 - two_real), i * two_real - r * (1.0 - two_real)
        right.append(jnp.concatenate([r, across], axis=1).astype(jnp.bfloat16))
        right.append(jnp.concatenate([across, own], axis=1).astype(jnp.bfloat16))
    products = lax.dot_general(
        jnp.concatenate(left, axis=0),
        jnp.concatenate(right, axis=0),
        (((1,), (1,)), ((), ())),
        preferred_element_type=jnp.float32,
    )

    def block(row, column):
        return products[32 * row:32 * row + 32, 64 * column:64 * column + 64]

    low = None
    for order in reversed(range(2, 2 * CUTS - 1)):
        for row in range(CUTS):
            if 0 <= order - row < CUTS:
                part = block(row, order - row)
                low = part if low is None else low + part
    high, rest = two_sum(block(0, 0), block(0, 1))
    high, more = two_sum(high, block(1, 0))
    low = low + (rest + more)
    total = high + low
    return total, low - (total - high)


def spectrum_kernel(me_ref, table_ref, root_ref, *refs, tm):
    pieces, (spec_ref, keep_ref, send_ref, records_ref) = refs[:tm], refs[tm:]
    rows = pieces[0].shape[0]
    root = root_ref[...]
    for d in range(tm):
        start = pl.multiple_of((me_ref[0] ^ d) * rows, rows)
        records_ref[pl.ds(start, rows), :] = pieces[d][...] * root
    spectrum_body(table_ref[...], records_ref[...], spec_ref)
    core = me_ref[0] & 1
    row = lax.broadcasted_iota(jnp.int32, (32, 32), 0)
    column = lax.broadcasted_iota(jnp.int32, (32, 32), 1)
    for j, out_ref in ((1, send_ref), (0, keep_ref)):
        side = core ^ j
        for q in range(SIDE):
            packed = [[], []]
            for s in range(4):
                slot = (side * SIDE + q) * 4 + s
                special = q == 0 and s == 0
                two_real = jnp.where(side == 0, 1.0, 0.0) if special else None
                sums = gram_slot(spec_ref[slot], spec_ref[SLOTS + slot], two_real)
                for part in range(2):
                    real, imag = sums[part][:, :32], sums[part][:, 32:]
                    square = jnp.where(column >= row, real, imag)
                    diagonal = jnp.sum(jnp.where(column == row, imag, 0.0), axis=0, keepdims=True)
                    if special:
                        square = jnp.where(row == NB, diagonal, square)
                    packed[part].append(square)
            for part in range(2):
                out_ref[q, part] = jnp.concatenate(packed[part], axis=1)


def core_sum_kernel(me_ref, keep_ref, got_ref, *out_refs):
    for d in range(SIDE):
        q = (me_ref[1] & (SIDE - 1)) ^ d
        high, low = pair_add((keep_ref[q, 0], keep_ref[q, 1]), (got_ref[q, 0], got_ref[q, 1]))
        out_refs[d][0] = high
        out_refs[d][1] = low


def pair_sum_kernel(*refs):
    high, low = pair_tree([(ref[0], ref[1]) for ref in refs[:-1]])
    refs[-1][0] = high
    refs[-1][1] = low


def swap_squares(square):
    turned = square.T
    return jnp.concatenate([turned[32 * s:32 * s + 32] for s in range(4)], axis=1)


def factor_kernel(me_ref, *refs, scale):
    out_ref = refs[-1]
    high, low = pair_tree([(ref[0], ref[1]) for ref in refs[:-1]])
    shape = (32, 128)
    row = lax.broadcasted_iota(jnp.int32, shape, 0)
    lane = lax.broadcasted_iota(jnp.int32, shape, 1)
    column = lane % 32
    base = lane - column
    first = jnp.logical_and((me_ref[0] & 1) == 0, (me_ref[1] & (SIDE - 1)) == 0)
    two_real = jnp.logical_and(lane < 32, first)
    sign = jnp.where(two_real, 1.0, -1.0)
    real, imag = [], []
    for square in (high, low):
        turned = swap_squares(square)
        diagonal = jnp.where(two_real, square[NB:NB + 1], 0.0)
        real.append(jnp.where(column >= row, square, turned))
        imag.append(jnp.where(column < row, square, jnp.where(column == row, diagonal, turned * sign)))
    inside = jnp.logical_and(row < NB, column < NB)
    real = [jnp.where(inside, part * scale, 0.0) for part in real]
    imag = [jnp.where(inside, part * scale, 0.0) for part in imag]

    def spread(value, at):
        return jnp.take_along_axis(value, base + at, axis=1, mode="promise_in_bounds")

    def rows_of(value, at):
        return jnp.broadcast_to(value[at:at + 1], shape)

    def quotient(value, pivot, pivot_halves, inverse):
        first_part = value[0] * inverse
        product, error = pair_product(
            (first_part, 0.0), halves(first_part), (pivot[0], 0.0), pivot_halves
        )
        rest = ((value[0] - product) - error) + (value[1] - first_part * pivot[1])
        return first_part, rest * inverse

    def minus(value, products):
        high, low = value[0], value[1]
        for product in products:
            high, error = two_sum(high, -product[0])
            low = low + (error - product[1])
        total = high + low
        return [total, low - (total - high)]

    for k in range(NB):
        line_real = [rows_of(part, k) for part in real]
        line_imag = [rows_of(part, k) for part in imag]
        pivot_real = [spread(part, k) for part in line_real]
        pivot_imag = [jnp.where(two_real, spread(part, k), own) for part, own in zip(line_imag, pivot_real)]
        below = row > k
        here = column == k
        step_real = [jnp.where(below, spread(part, k), 0.0) for part in real]
        step_imag = [jnp.where(below, spread(part, k), 0.0) for part in imag]
        step_real = quotient(step_real, pivot_real, halves(pivot_real[0]), 1.0 / pivot_real[0])
        step_imag = quotient(step_imag, pivot_imag, halves(pivot_imag[0]), 1.0 / pivot_imag[0])
        cross = tuple(jnp.where(two_real, 0.0, part) for part in step_imag)
        own = tuple(jnp.where(two_real, b, a) for a, b in zip(step_real, step_imag))
        one = jnp.where(here, 1.0, 0.0)
        line_real = (jnp.where(here, 1.0, line_real[0]), jnp.where(here, 0.0, line_real[1]))
        line_imag = (
            jnp.where(here, jnp.where(two_real, 1.0, 0.0), line_imag[0]),
            jnp.where(here, 0.0, line_imag[1]),
        )
        clear = jnp.logical_and(below, here)
        real = [jnp.where(clear, 0.0, part) for part in real]
        imag = [jnp.where(clear, 0.0, part) for part in imag]
        line_real_halves, line_imag_halves = halves(line_real[0]), halves(line_imag[0])
        step_halves, cross_halves, own_halves = halves(step_real[0]), halves(cross[0]), halves(own[0])
        p = pair_product(step_real, step_halves, line_real, line_real_halves)
        q = pair_product(cross, cross_halves, line_imag, line_imag_halves)
        real = minus(real, [p, (-q[0], -q[1])])
        p = pair_product(own, own_halves, line_imag, line_imag_halves)
        q = pair_product(cross, cross_halves, line_real, line_real_halves)
        imag = minus(imag, [p, q])
    pivot_real = spread(real[0], row)
    pivot_imag = jnp.where(two_real, spread(imag[0], row), pivot_real)
    good = row < NB
    out_ref[0] = jnp.where(good, real[0] / jnp.sqrt(pivot_real), 0.0)
    out_ref[1] = jnp.where(good, imag[0] / jnp.sqrt(pivot_imag), 0.0)


def apply_kernel(me_ref, *refs):
    pieces, (spec_ref, modes_ref, triangle_ref) = refs[:GROUPS], refs[GROUPS:]
    points = spec_ref.shape[-1]
    tiles = points // 128
    shape = (32, 128)
    row = lax.broadcasted_iota(jnp.int32, shape, 0)
    lane = lax.broadcasted_iota(jnp.int32, shape, 1)
    column = lane % 32
    here = column == row
    zero = jnp.zeros((NB, 128), jnp.float32)

    def put(frequency, part, value):
        for tile in range(tiles):
            modes_ref[frequency, pl.ds(2 * tile + part, NB, stride=2 * tiles), :] = (
                value if value is zero else value[:, 128 * tile:128 * tile + 128]
            )

    put(0, 1, zero)
    put(SLOTS, 1, zero)
    for c in range(2):
        for d in range(SIDE):
            piece = pieces[SIDE * c + d]
            group = ((me_ref[0] & 1) ^ c) * SIDE + ((me_ref[1] & (SIDE - 1)) ^ d)
            is_first = group == 0
            two_real = jnp.logical_and(lane < 32, is_first)
            both_real, both_imag = piece[0], piece[1]
            upper_real = jnp.where(column >= row, both_real, 0.0)
            upper_imag = jnp.where(column >= row, both_imag, 0.0)
            for s in range(4):
                triangle_ref[0, 4 * group + s] = upper_real[:NB, 32 * s:32 * s + NB]
                if s:
                    triangle_ref[1, 4 * group + s] = upper_imag[:NB, 32 * s:32 * s + NB]
                else:
                    triangle_ref[1, 4 * group] = jnp.where(is_first, 0.0, upper_imag[:NB, :NB])
            low_real = jnp.where(column < row, both_real, jnp.where(here, 1.0 / both_real, 0.0))
            low_imag = jnp.where(
                column < row, both_imag, jnp.where(jnp.logical_and(here, two_real), 1.0 / both_imag, 0.0)
            )
            good = row < NB
            low_real = jnp.where(good, low_real, 0.0)
            low_imag = jnp.where(good, low_imag, 0.0)
            cross = jnp.where(two_real, 0.0, low_imag)
            own = jnp.where(two_real, low_imag, low_real)
            rows = []
            for s in range(4):
                mine = lane // 32 == s
                rows.append(jnp.concatenate([jnp.where(mine, low_real, 0.0), jnp.where(mine, cross, 0.0)], axis=1))
                rows.append(jnp.concatenate([jnp.where(mine, -cross, 0.0), jnp.where(mine, own, 0.0)], axis=1))
            left = slices_of(jnp.concatenate(rows, axis=0), 3)
            reals = spec_ref[pl.ds(4 * group, 4)].reshape(128, points)
            imags = spec_ref[pl.ds(SLOTS + 4 * group, 4)].reshape(128, points)
            right = slices_of(jnp.concatenate([reals, imags], axis=0), 3)
            total = None
            for order in reversed(range(3)):
                for number in range(order + 1):
                    part = jnp.dot(left[number], right[order - number], preferred_element_type=jnp.float32)
                    total = part if total is None else total + part
            for s in range(4):
                put(4 * group + s, 0, total[64 * s:64 * s + NB])
                if s:
                    put(4 * group + s, 1, total[64 * s + 32:64 * s + 32 + NB])

            @pl.when(is_first)
            def _(total=total, upper_imag=upper_imag):
                put(SLOTS, 0, total[32:32 + NB])
                triangle_ref[0, SLOTS] = upper_imag[:NB, :NB]
                triangle_ref[1, SLOTS] = jnp.zeros((NB, NB), jnp.float32)

            @pl.when(jnp.logical_not(is_first))
            def _(total=total, group=group):
                put(4 * group, 1, total[32:32 + NB])


def call(body, out_shape, scratch, operands):
    smem = pl.BlockSpec(memory_space=pltpu.SMEM)
    vmem = pl.BlockSpec(memory_space=pltpu.VMEM)
    return pl.pallas_call(
        body,
        out_shape=out_shape,
        in_specs=[smem] + [vmem] * (len(operands) - 1),
        out_specs=jax.tree.map(lambda _: vmem, out_shape),
        scratch_shapes=scratch,
        compiler_params=pltpu.CompilerParams(vmem_limit_bytes=VMEM_BYTES),
    )(*operands)


def f32(*shape):
    return jax.ShapeDtypeStruct(shape, jnp.float32)


def xor_pairs(size, difference):
    return [(i, i ^ difference) for i in range(size)]


def factor_over_devices(place, keep, send, scale):
    tm, pts = lax.axis_size("tm"), lax.axis_size("pts")
    part = f32(2, 32, 128)
    got = lax.ppermute(send, "tm", xor_pairs(tm, 1))
    parts = call(core_sum_kernel, (part,) * SIDE, [], [place, keep, got])
    parts = [parts[0]] + [lax.ppermute(parts[d], "pts", xor_pairs(pts, d)) for d in range(1, SIDE)]
    total = call(lambda _, *refs: pair_sum_kernel(*refs), part, [], [place] + parts)
    if pts > SIDE:
        parts = [total] + [lax.ppermute(total, "pts", xor_pairs(pts, d)) for d in range(SIDE, pts, SIDE)]
        total = call(lambda _, *refs: pair_sum_kernel(*refs), part, [], [place] + parts)
    parts = [total] + [lax.ppermute(total, "tm", xor_pairs(tm, d)) for d in range(2, tm, 2)]
    own = call(functools.partial(factor_kernel, scale=scale), part, [], [place] + parts)
    own = [own] + [lax.ppermute(own, "pts", xor_pairs(pts, d)) for d in range(1, SIDE)]
    return own + [lax.ppermute(piece, "tm", xor_pairs(tm, 1)) for piece in own]


def shards(snapshots, weights):
    tm, pts = lax.axis_size("tm"), lax.axis_size("pts")
    me = lax.axis_index("tm")
    points = weights.shape[0]
    scale = 1.0 / (points * tm * pts)
    pieces = []
    for d in range(tm):
        piece = lax.dynamic_slice_in_dim(snapshots, (me ^ d) * points, points, 1)
        pieces.append(piece if d == 0 else lax.ppermute(piece, "tm", xor_pairs(tm, d)))
    root = jnp.sqrt(weights)[None, :]
    table_t = jnp.asarray(fourier_table().T)
    place = jnp.stack([me, lax.axis_index("pts")]).astype(jnp.int32)
    half = f32(SIDE, 2, 32, 128)
    spec, keep, send = call(
        functools.partial(spectrum_kernel, tm=tm),
        (f32(SEG, 32, points), half, half),
        [pltpu.VMEM((NT, points), jnp.float32)],
        [place, table_t, root] + pieces,
    )
    factors = factor_over_devices(place, keep, send, scale)
    tiles = points // 128
    modes, triangle = call(
        apply_kernel,
        (f32(NF, NB * tiles * 2, 128), f32(2, NF, NB, NB)),
        [],
        [place] + factors + [spec],
    )
    modes = modes.reshape(NF, NB, tiles, 2, 128).transpose(3, 0, 1, 2, 4).reshape(2, NF, NB, points)
    return (modes, triangle)


def solution(mesh):
    placed = (P("tm", "pts"), P(("pts", "tm")))
    return jax.shard_map(
        shards,
        mesh=mesh,
        in_specs=placed,
        out_specs=(P(None, None, None, ("pts", "tm")), P()),
        check_vma=False,
    )
```

profile of v0, /device:TPU:0, one launch (start us, length us, event | category | flops | bytes accessed | tf_op | source)
XLA Modules:
  0.0 101.4 jit_solution(14290985843056265278)
XLA Ops:
  0.7 0.0 copy-start.1
  0.7 0.0 copy-start
  0.7 1.8 %constant_dynamic-slice_fusion = (f32[128,512]{1,0:T(8,128)S(1)}, f32[128,512]{1,0:T(8,128)S(1)}, f32[128,512]{1,0:T(8,128)S(1)}, f32[128,512]{1,0:T(8,128)S(1)}...) fusion(f32[128,4096]{1,0:T(8,128)} %param.3, ...), kind=kLoop, calls=%fused_computation | loop fusion | bytes 4194336 | tf_op jit(solution)/shard_map/dynamic_slice | solution.py:380
  2.5 4.6 %collective-permute-start.6 = (f32[128,512]{1,0:T(8,128)S(1)}, f32[128,512]{1,0:T(8,128)S(1)}, u32[]{:S(2)}, u32[]{:S(2)}) collective-permute-start(f32[128,512]{1,0:T(8,128)S(1)} %get-tuple-element.22), channel_id=1, source_target_pairs={{0,28},{4,24},{8,20},{12,16},{16,12},{20,8},{24,4},{28,0},{1,29},{... | collective-permute-start | bytes 786440 | tf_op jit(solution)/shard_map/ppermute | solution.py:381
  7.1 0.0 collective-permute-start.4
  7.1 3.2 %collective-permute-start.3 = (f32[128,512]{1,0:T(8,128)S(1)}, f32[128,512]{1,0:T(8,128)S(1)}, u32[]{:S(2)}, u32[]{:S(2)}) collective-permute-start(f32[128,512]{1,0:T(8,128)S(1)} %get-tuple-element.24), channel_id=1, source_target_pairs={{0,16},{4,20},{8,24},{12,28},{16,0},{20,4},{24,8},{28,12},{1,17},{... | collective-permute-start | bytes 786440 | tf_op jit(solution)/shard_map/ppermute | solution.py:381
  10.3 0.0 collective-permute-start.2
  10.3 1.2 %collective-permute-start.1 = (f32[128,512]{1,0:T(8,128)S(1)}, f32[128,512]{1,0:T(8,128)S(1)}, u32[]{:S(2)}, u32[]{:S(2)}) collective-permute-start(f32[128,512]{1,0:T(8,128)S(1)} %get-tuple-element.26), channel_id=1, source_target_pairs={{0,8},{4,12},{8,0},{12,4},{16,24},{20,28},{24,16},{28,20},{1,9},{5... | collective-permute-start | bytes 786440 | tf_op jit(solution)/shard_map/ppermute | solution.py:381
  11.5 2.4 %collective-permute-done.6.refs_7_ = f32[128,512]{1,0:T(8,128)S(1)} collective-permute-done((f32[128,512]{1,0:T(8,128)S(1)}, f32[128,512]{1,0:T(8,128)S(1)}, u32[]{:S(2)}, u32[]{:S(2)}) %collective-permute-start.6) | collective-permute-done | bytes 262176 | tf_op jit(solution)/shard_map/ppermute | solution.py:381
  13.9 0.8 collective-permute-start
  14.7 21.3 %collective-permute-done.4.refs_5_ = f32[128,512]{1,0:T(8,128)S(1)} collective-permute-done((f32[128,512]{1,0:T(8,128)S(1)}, f32[128,512]{1,0:T(8,128)S(1)}, u32[]{:S(2)}, u32[]{:S(2)}) %collective-permute-start.4) | collective-permute-done | bytes 262176 | tf_op jit(solution)/shard_map/ppermute | solution.py:381
  36.0 2.6 %collective-permute-start.5 = (f32[128,512]{1,0:T(8,128)S(1)}, f32[128,512]{1,0:T(8,128)S(1)}, u32[]{:S(2)}, u32[]{:S(2)}) collective-permute-start(f32[128,512]{1,0:T(8,128)S(1)} %get-tuple-element.29), channel_id=1, source_target_pairs={{0,24},{4,28},{8,16},{12,20},{16,8},{20,12},{24,0},{28,4},{1,25},{... | collective-permute-start | bytes 786440 | tf_op jit(solution)/shard_map/ppermute | solution.py:381
  38.6 0.0 copy-done.1
  38.6 0.1 pad_add_fusion.me_ref._
  38.7 8.8 %collective-permute-done.3.refs_4_ = f32[128,512]{1,0:T(8,128)S(1)} collective-permute-done((f32[128,512]{1,0:T(8,128)S(1)}, f32[128,512]{1,0:T(8,128)S(1)}, u32[]{:S(2)}, u32[]{:S(2)}) %collective-permute-start.3) | collective-permute-done | bytes 262176 | tf_op jit(solution)/shard_map/ppermute | solution.py:381
  47.5 0.0 collective-permute-done.2.refs_3_
  47.5 0.0 collective-permute-done.1.refs_2_
  47.5 0.0 collective-permute-done.refs_1_
  47.5 0.0 collective-permute-done.5.refs_6_
  47.5 0.0 copy-done
  47.5 10.3 %shard_map.50 = (f32[64,32,512]{2,1,0:T(8,128)S(1)}, f32[4,2,32,128]{3,2,1,0:T(8,128)S(1)}, f32[4,2,32,128]{3,2,1,0:T(8,128)S(1)}) custom-call(s32[2]{0:T(128)S(1)} %pad_add_fusion.me_ref._, f32[64,64]{1,0:T(8,128)S(1)} %copy-done, f32[1,512]{1,0:T(1,128)S(1)} %bitcast.8, f32[128,512]{1,0:T(8,128)S(1)} %get-tuple-element.28.refs_0_, ...), custom_call_target="tpu_custom_call" | custom-call | tf_op jit(solution)/shard_map/pallas_call | solution.py:339
  57.8 0.1 collective-permute-start.7
  57.9 1.3 %collective-permute-done.7.got_ref = f32[4,2,32,128]{3,2,1,0:T(8,128)S(1)} collective-permute-done((f32[4,2,32,128]{3,2,1,0:T(8,128)S(1)}, f32[4,2,32,128]{3,2,1,0:T(8,128)S(1)}, u32[]{:S(2)}, u32[]{:S(2)}) %collective-permute-start.7) | collective-permute-done | bytes 131104 | tf_op jit(solution)/shard_map/ppermute | solution.py:360
  59.2 0.6 shard_map.51
  59.8 1.6 %collective-permute-start.8 = (f32[2,32,128]{2,1,0:T(8,128)S(1)}, f32[2,32,128]{2,1,0:T(8,128)S(1)}, u32[]{:S(2)}, u32[]{:S(2)}) collective-permute-start(f32[2,32,128]{2,1,0:T(8,128)S(1)} %get-tuple-element.14), channel_id=1, source_target_pairs={{0,1},{1,0},{2,3},{3,2},{4,5},{5,4},{6,7},{7,6},{8,9},{9,8},{10,11... | collective-permute-start | bytes 98312 | tf_op jit(solution)/shard_map/ppermute | solution.py:362
  61.4 1.5 %collective-permute-start.9 = (f32[2,32,128]{2,1,0:T(8,128)S(1)}, f32[2,32,128]{2,1,0:T(8,128)S(1)}, u32[]{:S(2)}, u32[]{:S(2)}) collective-permute-start(f32[2,32,128]{2,1,0:T(8,128)S(1)} %get-tuple-element.15), channel_id=1, source_target_pairs={{0,2},{1,3},{2,0},{3,1},{4,6},{5,7},{6,4},{7,5},{8,10},{9,11},{10,... | collective-permute-start | bytes 98312 | tf_op jit(solution)/shard_map/ppermute | solution.py:362
  62.9 0.5 collective-permute-start.10
  63.4 0.4 collective-permute-done.8.refs_1_
  63.8 1.5 %collective-permute-done.9.refs_2_ = f32[2,32,128]{2,1,0:T(8,128)S(1)} collective-permute-done((f32[2,32,128]{2,1,0:T(8,128)S(1)}, f32[2,32,128]{2,1,0:T(8,128)S(1)}, u32[]{:S(2)}, u32[]{:S(2)}) %collective-permute-start.9) | collective-permute-done | bytes 32800 | tf_op jit(solution)/shard_map/ppermute | solution.py:362
  65.3 2.4 %collective-permute-done.10.refs_3_ = f32[2,32,128]{2,1,0:T(8,128)S(1)} collective-permute-done((f32[2,32,128]{2,1,0:T(8,128)S(1)}, f32[2,32,128]{2,1,0:T(8,128)S(1)}, u32[]{:S(2)}, u32[]{:S(2)}) %collective-permute-start.10) | collective-permute-done | bytes 32800 | tf_op jit(solution)/shard_map/ppermute | solution.py:362
  67.7 0.6 shard_map.52.refs_0_
  68.3 2.4 %collective-permute-start.13 = (f32[2,32,128]{2,1,0:T(8,128)S(1)}, f32[2,32,128]{2,1,0:T(8,128)S(1)}, u32[]{:S(2)}, u32[]{:S(2)}) collective-permute-start(f32[2,32,128]{2,1,0:T(8,128)S(1)} %shard_map.52.refs_0_), channel_id=1, source_target_pairs={{0,24},{4,28},{8,16},{12,20},{16,8},{20,12},{24,0},{28,4},{1,25},{... | collective-permute-start | bytes 98312 | tf_op jit(solution)/shard_map/ppermute | solution.py:367
  70.7 5.1 %collective-permute-start.12 = (f32[2,32,128]{2,1,0:T(8,128)S(1)}, f32[2,32,128]{2,1,0:T(8,128)S(1)}, u32[]{:S(2)}, u32[]{:S(2)}) collective-permute-start(f32[2,32,128]{2,1,0:T(8,128)S(1)} %shard_map.52.refs_0_), channel_id=1, source_target_pairs={{0,16},{4,20},{8,24},{12,28},{16,0},{20,4},{24,8},{28,12},{1,17},{... | collective-permute-start | bytes 98312 | tf_op jit(solution)/shard_map/ppermute | solution.py:367
  75.8 0.1 collective-permute-start.11
  75.9 0.0 collective-permute-done.13.refs_3_
  76.0 2.1 %collective-permute-done.12.refs_2_ = f32[2,32,128]{2,1,0:T(8,128)S(1)} collective-permute-done((f32[2,32,128]{2,1,0:T(8,128)S(1)}, f32[2,32,128]{2,1,0:T(8,128)S(1)}, u32[]{:S(2)}, u32[]{:S(2)}) %collective-permute-start.12) | collective-permute-done | bytes 32800 | tf_op jit(solution)/shard_map/ppermute | solution.py:367
  78.1 1.7 %collective-permute-done.11.refs_1_ = f32[2,32,128]{2,1,0:T(8,128)S(1)} collective-permute-done((f32[2,32,128]{2,1,0:T(8,128)S(1)}, f32[2,32,128]{2,1,0:T(8,128)S(1)}, u32[]{:S(2)}, u32[]{:S(2)}) %collective-permute-start.11) | collective-permute-done | bytes 32800 | tf_op jit(solution)/shard_map/ppermute | solution.py:367
  79.7 5.0 %shard_map.53.refs_0_ = f32[2,32,128]{2,1,0:T(8,128)S(1)} custom-call(s32[2]{0:T(128)S(1)} %pad_add_fusion.me_ref._, f32[2,32,128]{2,1,0:T(8,128)S(1)} %shard_map.52.refs_0_, f32[2,32,128]{2,1,0:T(8,128)S(1)} %collective-permute-done.11.refs_1_, f32[2,32,128]{2,1,0:T(8,128)S(1)} %collective-permute-done.12.refs_2_, ...), custom_call_target="tpu_custom_call" | custom-call | tf_op jit(solution)/shard_map/pallas_call | solution.py:339
  84.8 0.5 collective-permute-start.16
  85.3 1.5 %collective-permute-start.15 = (f32[2,32,128]{2,1,0:T(8,128)S(1)}, f32[2,32,128]{2,1,0:T(8,128)S(1)}, u32[]{:S(2)}, u32[]{:S(2)}) collective-permute-start(f32[2,32,128]{2,1,0:T(8,128)S(1)} %shard_map.53.refs_0_), channel_id=1, source_target_pairs={{0,2},{1,3},{2,0},{3,1},{4,6},{5,7},{6,4},{7,5},{8,10},{9,11},{10,... | collective-permute-start | bytes 98312 | tf_op jit(solution)/shard_map/ppermute | solution.py:369
  86.8 1.5 %collective-permute-start.14 = (f32[2,32,128]{2,1,0:T(8,128)S(1)}, f32[2,32,128]{2,1,0:T(8,128)S(1)}, u32[]{:S(2)}, u32[]{:S(2)}) collective-permute-start(f32[2,32,128]{2,1,0:T(8,128)S(1)} %shard_map.53.refs_0_), channel_id=1, source_target_pairs={{0,1},{1,0},{2,3},{3,2},{4,5},{5,4},{6,7},{7,6},{8,9},{9,8},{10,11... | collective-permute-start | bytes 98312 | tf_op jit(solution)/shard_map/ppermute | solution.py:369
  88.3 0.0 collective-permute-start.17
  88.3 1.3 %collective-permute-done.16.refs_3_ = f32[2,32,128]{2,1,0:T(8,128)S(1)} collective-permute-done((f32[2,32,128]{2,1,0:T(8,128)S(1)}, f32[2,32,128]{2,1,0:T(8,128)S(1)}, u32[]{:S(2)}, u32[]{:S(2)}) %collective-permute-start.16) | collective-permute-done | bytes 32800 | tf_op jit(solution)/shard_map/ppermute | solution.py:369
  89.7 0.0 collective-permute-start.20
  89.7 0.0 collective-permute-done.15.refs_2_
  89.7 0.5 collective-permute-start.19
  90.2 0.6 collective-permute-done.14.refs_1_
  90.8 0.0 collective-permute-start.18
  90.8 0.0 collective-permute-done.17.refs_4_
  90.8 0.1 collective-permute-done.20.refs_7_
  90.9 0.2 collective-permute-done.19.refs_6_
  91.0 0.9 collective-permute-done.18.refs_5_
  92.0 7.9 %shard_map.54 = (f32[33,248,128]{2,1,0:T(8,128)}, f32[2,33,31,31]{3,2,1,0:T(8,128)S(1)}) custom-call(s32[2]{0:T(128)S(1)} %pad_add_fusion.me_ref._, f32[2,32,128]{2,1,0:T(8,128)S(1)} %shard_map.53.refs_0_, f32[2,32,128]{2,1,0:T(8,128)S(1)} %collective-permute-done.14.refs_1_, f32[2,32,128]{2,1,0:T(8,128)S(1)} %collective-permute-done.15.refs_2_, ...), custom_call_target="tpu_custom_call" | custom-call | tf_op jit(solution)/shard_map/pallas_call | solution.py:339
  99.9 1.6 %copy.6 = f32[2,33,31,31]{1,0,3,2:T(2,128)} copy(f32[2,33,31,31]{3,2,1,0:T(8,128)S(1)} %get-tuple-element.21) | data formatting | bytes 507408
  (1 shorter events, 0.0 us)
Async XLA Ops:
  0.7 37.9 %copy-start.1 = (f32[512]{0:T(512)S(1)}, f32[512]{0:T(512)}, u32[]{:S(2)}) copy-start(f32[512]{0:T(512)} %param.4) | copy-start | bytes 6148
  0.7 46.8 %copy-start = (f32[64,64]{1,0:T(8,128)S(1)}, f32[64,64]{1,0:T(8,128)}, u32[]{:S(2)}) copy-start(f32[64,64]{1,0:T(8,128)} %constant.31.clone.table_ref) | copy-start | bytes 49156
  2.5 11.3 %collective-permute-start.6 = (f32[128,512]{1,0:T(8,128)S(1)}, f32[128,512]{1,0:T(8,128)S(1)}, u32[]{:S(2)}, u32[]{:S(2)}) collective-permute-start(f32[128,512]{1,0:T(8,128)S(1)} %get-tuple-element.22), channel_id=1, source_target_pairs={{0,28},{4,24},{8,20},{12,16},{16,12},{20,8},{24,4},{28,0},{1,29},{... | collective-permute-start | bytes 786440 | tf_op jit(solution)/shard_map/ppermute | solution.py:381
  7.1 28.9 %collective-permute-start.4 = (f32[128,512]{1,0:T(8,128)S(1)}, f32[128,512]{1,0:T(8,128)S(1)}, u32[]{:S(2)}, u32[]{:S(2)}) collective-permute-start(f32[128,512]{1,0:T(8,128)S(1)} %get-tuple-element.23), channel_id=1, source_target_pairs={{0,20},{4,16},{8,28},{12,24},{16,4},{20,0},{24,12},{28,8},{1,21},{... | collective-permute-start | bytes 786440 | tf_op jit(solution)/shard_map/ppermute | solution.py:381
  7.1 40.4 %collective-permute-start.3 = (f32[128,512]{1,0:T(8,128)S(1)}, f32[128,512]{1,0:T(8,128)S(1)}, u32[]{:S(2)}, u32[]{:S(2)}) collective-permute-start(f32[128,512]{1,0:T(8,128)S(1)} %get-tuple-element.24), channel_id=1, source_target_pairs={{0,16},{4,20},{8,24},{12,28},{16,0},{20,4},{24,8},{28,12},{1,17},{... | collective-permute-start | bytes 786440 | tf_op jit(solution)/shard_map/ppermute | solution.py:381
  10.3 37.2 %collective-permute-start.2 = (f32[128,512]{1,0:T(8,128)S(1)}, f32[128,512]{1,0:T(8,128)S(1)}, u32[]{:S(2)}, u32[]{:S(2)}) collective-permute-start(f32[128,512]{1,0:T(8,128)S(1)} %get-tuple-element.25), channel_id=1, source_target_pairs={{0,12},{4,8},{8,4},{12,0},{16,28},{20,24},{24,20},{28,16},{1,13},{... | collective-permute-start | bytes 786440 | tf_op jit(solution)/shard_map/ppermute | solution.py:381
  10.3 37.2 %collective-permute-start.1 = (f32[128,512]{1,0:T(8,128)S(1)}, f32[128,512]{1,0:T(8,128)S(1)}, u32[]{:S(2)}, u32[]{:S(2)}) collective-permute-start(f32[128,512]{1,0:T(8,128)S(1)} %get-tuple-element.26), channel_id=1, source_target_pairs={{0,8},{4,12},{8,0},{12,4},{16,24},{20,28},{24,16},{28,20},{1,9},{5... | collective-permute-start | bytes 786440 | tf_op jit(solution)/shard_map/ppermute | solution.py:381
  13.9 33.6 %collective-permute-start = (f32[128,512]{1,0:T(8,128)S(1)}, f32[128,512]{1,0:T(8,128)S(1)}, u32[]{:S(2)}, u32[]{:S(2)}) collective-permute-start(f32[128,512]{1,0:T(8,128)S(1)} %get-tuple-element.27), channel_id=1, source_target_pairs={{0,4},{4,0},{8,12},{12,8},{16,20},{20,16},{24,28},{28,24},{1,5},{5... | collective-permute-start | bytes 786440 | tf_op jit(solution)/shard_map/ppermute | solution.py:381
  36.0 11.5 %collective-permute-start.5 = (f32[128,512]{1,0:T(8,128)S(1)}, f32[128,512]{1,0:T(8,128)S(1)}, u32[]{:S(2)}, u32[]{:S(2)}) collective-permute-start(f32[128,512]{1,0:T(8,128)S(1)} %get-tuple-element.29), channel_id=1, source_target_pairs={{0,24},{4,28},{8,16},{12,20},{16,8},{20,12},{24,0},{28,4},{1,25},{... | collective-permute-start | bytes 786440 | tf_op jit(solution)/shard_map/ppermute | solution.py:381
  57.8 1.4 %collective-permute-start.7 = (f32[4,2,32,128]{3,2,1,0:T(8,128)S(1)}, f32[4,2,32,128]{3,2,1,0:T(8,128)S(1)}, u32[]{:S(2)}, u32[]{:S(2)}) collective-permute-start(f32[4,2,32,128]{3,2,1,0:T(8,128)S(1)} %get-tuple-element.12), channel_id=1, source_target_pairs={{0,4},{4,0},{8,12},{12,8},{16,20},{20,16},{24,28},{28,24},{1,5},{5... | collective-permute-start | bytes 393224 | tf_op jit(solution)/shard_map/ppermute | solution.py:360
  59.8 4.0 %collective-permute-start.8 = (f32[2,32,128]{2,1,0:T(8,128)S(1)}, f32[2,32,128]{2,1,0:T(8,128)S(1)}, u32[]{:S(2)}, u32[]{:S(2)}) collective-permute-start(f32[2,32,128]{2,1,0:T(8,128)S(1)} %get-tuple-element.14), channel_id=1, source_target_pairs={{0,1},{1,0},{2,3},{3,2},{4,5},{5,4},{6,7},{7,6},{8,9},{9,8},{10,11... | collective-permute-start | bytes 98312 | tf_op jit(solution)/shard_map/ppermute | solution.py:362
  61.4 3.9 %collective-permute-start.9 = (f32[2,32,128]{2,1,0:T(8,128)S(1)}, f32[2,32,128]{2,1,0:T(8,128)S(1)}, u32[]{:S(2)}, u32[]{:S(2)}) collective-permute-start(f32[2,32,128]{2,1,0:T(8,128)S(1)} %get-tuple-element.15), channel_id=1, source_target_pairs={{0,2},{1,3},{2,0},{3,1},{4,6},{5,7},{6,4},{7,5},{8,10},{9,11},{10,... | collective-permute-start | bytes 98312 | tf_op jit(solution)/shard_map/ppermute | solution.py:362
  62.9 4.8 %collective-permute-start.10 = (f32[2,32,128]{2,1,0:T(8,128)S(1)}, f32[2,32,128]{2,1,0:T(8,128)S(1)}, u32[]{:S(2)}, u32[]{:S(2)}) collective-permute-start(f32[2,32,128]{2,1,0:T(8,128)S(1)} %get-tuple-element.16), channel_id=1, source_target_pairs={{0,3},{1,2},{2,1},{3,0},{4,7},{5,6},{6,5},{7,4},{8,11},{9,10},{10,... | collective-permute-start | bytes 98312 | tf_op jit(solution)/shard_map/ppermute | solution.py:362
  68.3 7.7 %collective-permute-start.13 = (f32[2,32,128]{2,1,0:T(8,128)S(1)}, f32[2,32,128]{2,1,0:T(8,128)S(1)}, u32[]{:S(2)}, u32[]{:S(2)}) collective-permute-start(f32[2,32,128]{2,1,0:T(8,128)S(1)} %shard_map.52.refs_0_), channel_id=1, source_target_pairs={{0,24},{4,28},{8,16},{12,20},{16,8},{20,12},{24,0},{28,4},{1,25},{... | collective-permute-start | bytes 98312 | tf_op jit(solution)/shard_map/ppermute | solution.py:367
  70.7 7.4 %collective-permute-start.12 = (f32[2,32,128]{2,1,0:T(8,128)S(1)}, f32[2,32,128]{2,1,0:T(8,128)S(1)}, u32[]{:S(2)}, u32[]{:S(2)}) collective-permute-start(f32[2,32,128]{2,1,0:T(8,128)S(1)} %shard_map.52.refs_0_), channel_id=1, source_target_pairs={{0,16},{4,20},{8,24},{12,28},{16,0},{20,4},{24,8},{28,12},{1,17},{... | collective-permute-start | bytes 98312 | tf_op jit(solution)/shard_map/ppermute | solution.py:367
  75.8 3.9 %collective-permute-start.11 = (f32[2,32,128]{2,1,0:T(8,128)S(1)}, f32[2,32,128]{2,1,0:T(8,128)S(1)}, u32[]{:S(2)}, u32[]{:S(2)}) collective-permute-start(f32[2,32,128]{2,1,0:T(8,128)S(1)} %shard_map.52.refs_0_), channel_id=1, source_target_pairs={{0,8},{4,12},{8,0},{12,4},{16,24},{20,28},{24,16},{28,20},{1,9},{5... | collective-permute-start | bytes 98312 | tf_op jit(solution)/shard_map/ppermute | solution.py:367
  84.8 4.9 %collective-permute-start.16 = (f32[2,32,128]{2,1,0:T(8,128)S(1)}, f32[2,32,128]{2,1,0:T(8,128)S(1)}, u32[]{:S(2)}, u32[]{:S(2)}) collective-permute-start(f32[2,32,128]{2,1,0:T(8,128)S(1)} %shard_map.53.refs_0_), channel_id=1, source_target_pairs={{0,3},{1,2},{2,1},{3,0},{4,7},{5,6},{6,5},{7,4},{8,11},{9,10},{10,... | collective-permute-start | bytes 98312 | tf_op jit(solution)/shard_map/ppermute | solution.py:369
  85.3 4.3 %collective-permute-start.15 = (f32[2,32,128]{2,1,0:T(8,128)S(1)}, f32[2,32,128]{2,1,0:T(8,128)S(1)}, u32[]{:S(2)}, u32[]{:S(2)}) collective-permute-start(f32[2,32,128]{2,1,0:T(8,128)S(1)} %shard_map.53.refs_0_), channel_id=1, source_target_pairs={{0,2},{1,3},{2,0},{3,1},{4,6},{5,7},{6,4},{7,5},{8,10},{9,11},{10,... | collective-permute-start | bytes 98312 | tf_op jit(solution)/shard_map/ppermute | solution.py:369
  86.8 3.9 %collective-permute-start.14 = (f32[2,32,128]{2,1,0:T(8,128)S(1)}, f32[2,32,128]{2,1,0:T(8,128)S(1)}, u32[]{:S(2)}, u32[]{:S(2)}) collective-permute-start(f32[2,32,128]{2,1,0:T(8,128)S(1)} %shard_map.53.refs_0_), channel_id=1, source_target_pairs={{0,1},{1,0},{2,3},{3,2},{4,5},{5,4},{6,7},{7,6},{8,9},{9,8},{10,11... | collective-permute-start | bytes 98312 | tf_op jit(solution)/shard_map/ppermute | solution.py:369
  88.3 2.4 %collective-permute-start.17 = (f32[2,32,128]{2,1,0:T(8,128)S(1)}, f32[2,32,128]{2,1,0:T(8,128)S(1)}, u32[]{:S(2)}, u32[]{:S(2)}) collective-permute-start(f32[2,32,128]{2,1,0:T(8,128)S(1)} %shard_map.53.refs_0_), channel_id=1, source_target_pairs={{0,4},{4,0},{8,12},{12,8},{16,20},{20,16},{24,28},{28,24},{1,5},{5... | collective-permute-start | bytes 98312 | tf_op jit(solution)/shard_map/ppermute | solution.py:370
  89.7 1.2 %collective-permute-start.20 = (f32[2,32,128]{2,1,0:T(8,128)S(1)}, f32[2,32,128]{2,1,0:T(8,128)S(1)}, u32[]{:S(2)}, u32[]{:S(2)}) collective-permute-start(f32[2,32,128]{2,1,0:T(8,128)S(1)} %collective-permute-done.16.refs_3_), channel_id=1, source_target_pairs={{0,4},{4,0},{8,12},{12,8},{16,20},{20,16},{24,28},{28,24},{1,5},{5... | collective-permute-start | bytes 98312 | tf_op jit(solution)/shard_map/ppermute | solution.py:370
  89.7 1.4 %collective-permute-start.19 = (f32[2,32,128]{2,1,0:T(8,128)S(1)}, f32[2,32,128]{2,1,0:T(8,128)S(1)}, u32[]{:S(2)}, u32[]{:S(2)}) collective-permute-start(f32[2,32,128]{2,1,0:T(8,128)S(1)} %collective-permute-done.15.refs_2_), channel_id=1, source_target_pairs={{0,4},{4,0},{8,12},{12,8},{16,20},{20,16},{24,28},{28,24},{1,5},{5... | collective-permute-start | bytes 98312 | tf_op jit(solution)/shard_map/ppermute | solution.py:370
  90.8 1.2 %collective-permute-start.18 = (f32[2,32,128]{2,1,0:T(8,128)S(1)}, f32[2,32,128]{2,1,0:T(8,128)S(1)}, u32[]{:S(2)}, u32[]{:S(2)}) collective-permute-start(f32[2,32,128]{2,1,0:T(8,128)S(1)} %collective-permute-done.14.refs_1_), channel_id=1, source_target_pairs={{0,4},{4,0},{8,12},{12,8},{16,20},{20,16},{24,28},{28,24},{1,5},{5... | collective-permute-start | bytes 98312 | tf_op jit(solution)/shard_map/ppermute | solution.py:370
where the time goes:
time: 102 us; the launch traced here: 101 us
  waiting for transfers between devices  45.1 us (44%)
  starting transfers between devices  27.7 us (27%)
  Pallas kernels  24.4 us (24%)
  local copies, waits for them, and re-layouts  3.39 us (3%)
    ppermute x7, waiting for transfers between devices, shards(): lax.ppermute(piece, 'tm', xor_pairs(tm, d))  32.5 us
    pallas_call x5, Pallas kernels, call(): pl.pallas_call(body, out_shape=out_shape, in_specs=[smem] + [vmem] * (len...  24.4 us
    ppermute x7, starting transfers between devices, shards(): lax.ppermute(piece, 'tm', xor_pairs(tm, d))  12.4 us
    ppermute x3, starting transfers between devices, factor_over_devices(): lax.ppermute(total, 'tm', xor_pairs(tm, d))  7.67 us
    ppermute x3, waiting for transfers between devices, factor_over_devices(): lax.ppermute(parts[d], 'pts', xor_pairs(pts, d))  4.33 us
    ppermute x3, waiting for transfers between devices, factor_over_devices(): lax.ppermute(total, 'tm', xor_pairs(tm, d))  3.8 us
    ppermute x3, starting transfers between devices, factor_over_devices(): lax.ppermute(own, 'pts', xor_pairs(pts, d))  3.55 us
    ppermute x3, starting transfers between devices, factor_over_devices(): lax.ppermute(parts[d], 'pts', xor_pairs(pts, d))  3.55 us
  transfers between devices with their start and end apart: 21, of which 14 were waited for; matrix products, arithmetic and copies ran while one was open for 0% of the time, Pallas kernels for 0%

commit v1 on v0

--- a/solution.py
+++ b/solution.py
@@ -98,33 +98,32 @@
 
 
 def gram_slot(real, imag, two_real):
-    left, right = [], []
-    for r, i in cut_rows(real, imag):
-        left.append(jnp.concatenate([r, i], axis=1).astype(jnp.bfloat16))
+    rows = jnp.concatenate([part for cut in cut_rows(real, imag) for part in cut], axis=0).astype(jnp.bfloat16)
+    products = lax.dot_general(rows, rows, (((1,), (1,)), ((), ())), preferred_element_type=jnp.float32)
+    lane = lax.broadcasted_iota(jnp.int32, (32, 128), 1)
+    is_real = lane // 32 % 2 == 0
+    front = lane < 64
+
+    def block(number, half):
+        return products[32 * number:32 * number + 32, 128 * half:128 * half + 128]
+
+    def combine(from_real, from_imag):
+        swapped = jnp.take_along_axis(from_imag, lane ^ 32, axis=1, mode="promise_in_bounds")
+        result = from_real + jnp.where(is_real, swapped, -swapped)
         if two_real is None:
-            across, own = i, -r
-        else:
-            across, own = i * (1.0 - two_real), i * two_real - r * (1.0 - two_real)
-        right.append(jnp.concatenate([r, across], axis=1).astype(jnp.bfloat16))
-        right.append(jnp.concatenate([across, own], axis=1).astype(jnp.bfloat16))
-    products = lax.dot_general(
-        jnp.concatenate(left, axis=0),
-        jnp.concatenate(right, axis=0),
-        (((1,), (1,)), ((), ())),
-        preferred_element_type=jnp.float32,
+            return result
+        return jnp.where(two_real, jnp.where(is_real, from_real, from_imag), result)
+
+    first = combine(block(0, 0), block(1, 0))
+    second = combine(block(2, 0), block(3, 0))
+    rest_real, rest_imag = (
+        block(6 + part, 1) + (block(4 + part, 1) + block(6 + part, 0)) + (block(2 + part, 1) + block(4 + part, 0)) + block(part, 1)
+        for part in range(2)
     )
-
-    def block(row, column):
-        return products[32 * row:32 * row + 32, 64 * column:64 * column + 64]
-
-    low = None
-    for order in reversed(range(2, 2 * CUTS - 1)):
-        for row in range(CUTS):
-            if 0 <= order - row < CUTS:
-                part = block(row, order - row)
-                low = part if low is None else low + part
-    high, rest = two_sum(block(0, 0), block(0, 1))
-    high, more = two_sum(high, block(1, 0))
+    low = combine(rest_real, rest_imag) + jnp.where(front, 0.0, second)
+    low = low[:, :64] + low[:, 64:]
+    high, rest = two_sum(first[:, :64], first[:, 64:])
+    high, more = two_sum(high, second[:, :64])
     low = low + (rest + more)
     total = high + low
     return total, low - (total - high)
@@ -148,13 +147,13 @@
             for s in range(4):
                 slot = (side * SIDE + q) * 4 + s
                 special = q == 0 and s == 0
-                two_real = jnp.where(side == 0, 1.0, 0.0) if special else None
+                two_real = side == 0 if special else None
                 sums = gram_slot(spec_ref[slot], spec_ref[SLOTS + slot], two_real)
                 for part in range(2):
                     real, imag = sums[part][:, :32], sums[part][:, 32:]
                     square = jnp.where(column >= row, real, imag)
-                    diagonal = jnp.sum(jnp.where(column == row, imag, 0.0), axis=0, keepdims=True)
                     if special:
+                        diagonal = jnp.sum(jnp.where(column == row, imag, 0.0), axis=0, keepdims=True)
                         square = jnp.where(row == NB, diagonal, square)
                     packed[part].append(square)
             for part in range(2):
@@ -261,39 +260,40 @@
 
 
 def apply_kernel(me_ref, *refs):
-    pieces, (spec_ref, modes_ref, triangle_ref) = refs[:GROUPS], refs[GROUPS:]
+    pieces, (spec_ref, modes_ref, triangle_ref, tiles_ref, sent) = refs[:GROUPS], refs[GROUPS:]
     points = spec_ref.shape[-1]
-    tiles = points // 128
     shape = (32, 128)
     row = lax.broadcasted_iota(jnp.int32, shape, 0)
     lane = lax.broadcasted_iota(jnp.int32, shape, 1)
     column = lane % 32
     here = column == row
-    zero = jnp.zeros((NB, 128), jnp.float32)
-
-    def put(frequency, part, value):
-        for tile in range(tiles):
-            modes_ref[frequency, pl.ds(2 * tile + part, NB, stride=2 * tiles), :] = (
-                value if value is zero else value[:, 128 * tile:128 * tile + 128]
-            )
-
-    put(0, 1, zero)
-    put(SLOTS, 1, zero)
+    even = lane // 32 % 2 == 0
+    wide = lax.broadcasted_iota(jnp.int32, (64, 128), 1) < 64
+    nothing = jnp.zeros((32, 128), jnp.float32)
+    copies = []
+
+    def put(frequency, real, imag):
+        rows = []
+        for tile in range(points // 128):
+            at = slice(128 * tile, 128 * tile + 128)
+            rows += [real[:, at], nothing if imag is None else imag[:, at]]
+        number = len(copies)
+        tiles_ref[number] = jnp.swapaxes(jnp.stack(rows, axis=0), 0, 1)[:NB]
+        copy = pltpu.make_async_copy(tiles_ref.at[number], modes_ref.at[frequency], sent.at[number])
+        copy.start()
+        copies.append(copy)
+
+    last_real = jnp.zeros((32, points), jnp.float32)
+    last_triangle = jnp.zeros((NB, NB), jnp.float32)
     for c in range(2):
         for d in range(SIDE):
             piece = pieces[SIDE * c + d]
             group = ((me_ref[0] & 1) ^ c) * SIDE + ((me_ref[1] & (SIDE - 1)) ^ d)
             is_first = group == 0
-            two_real = jnp.logical_and(lane < 32, is_first)
             both_real, both_imag = piece[0], piece[1]
             upper_real = jnp.where(column >= row, both_real, 0.0)
             upper_imag = jnp.where(column >= row, both_imag, 0.0)
-            for s in range(4):
-                triangle_ref[0, 4 * group + s] = upper_real[:NB, 32 * s:32 * s + NB]
-                if s:
-                    triangle_ref[1, 4 * group + s] = upper_imag[:NB, 32 * s:32 * s + NB]
-                else:
-                    triangle_ref[1, 4 * group] = jnp.where(is_first, 0.0, upper_imag[:NB, :NB])
+            two_real = jnp.logical_and(lane < 32, is_first)
             low_real = jnp.where(column < row, both_real, jnp.where(here, 1.0 / both_real, 0.0))
             low_imag = jnp.where(
                 column < row, both_imag, jnp.where(jnp.logical_and(here, two_real), 1.0 / both_imag, 0.0)
@@ -303,44 +303,46 @@
             low_imag = jnp.where(good, low_imag, 0.0)
             cross = jnp.where(two_real, 0.0, low_imag)
             own = jnp.where(two_real, low_imag, low_real)
-            rows = []
             for s in range(4):
-                mine = lane // 32 == s
-                rows.append(jnp.concatenate([jnp.where(mine, low_real, 0.0), jnp.where(mine, cross, 0.0)], axis=1))
-                rows.append(jnp.concatenate([jnp.where(mine, -cross, 0.0), jnp.where(mine, own, 0.0)], axis=1))
-            left = slices_of(jnp.concatenate(rows, axis=0), 3)
-            reals = spec_ref[pl.ds(4 * group, 4)].reshape(128, points)
-            imags = spec_ref[pl.ds(SLOTS + 4 * group, 4)].reshape(128, points)
-            right = slices_of(jnp.concatenate([reals, imags], axis=0), 3)
-            total = None
-            for order in reversed(range(3)):
-                for number in range(order + 1):
-                    part = jnp.dot(left[number], right[order - number], preferred_element_type=jnp.float32)
-                    total = part if total is None else total + part
-            for s in range(4):
-                put(4 * group + s, 0, total[64 * s:64 * s + NB])
-                if s:
-                    put(4 * group + s, 1, total[64 * s + 32:64 * s + 32 + NB])
-
-            @pl.when(is_first)
-            def _(total=total, upper_imag=upper_imag):
-                put(SLOTS, 0, total[32:32 + NB])
-                triangle_ref[0, SLOTS] = upper_imag[:NB, :NB]
-                triangle_ref[1, SLOTS] = jnp.zeros((NB, NB), jnp.float32)
-
-            @pl.when(jnp.logical_not(is_first))
-            def _(total=total, group=group):
-                put(4 * group, 1, total[32:32 + NB])
-
-
-def call(body, out_shape, scratch, operands):
+                slot = 4 * group + s
+
+                def spread(value):
+                    return jnp.take_along_axis(value, 32 * s + column, axis=1, mode="promise_in_bounds")
+
+                wide_cross = spread(cross)
+                top = jnp.where(even, spread(low_real), wide_cross)
+                bottom = jnp.where(even, -wide_cross, spread(own))
+                l0, l1, l2 = (part.astype(jnp.float32) for part in slices_of(jnp.concatenate([top, bottom], axis=0), 3))
+                left = [l0, jnp.where(wide, l1, l0), jnp.where(wide, l1, l2)]
+                left = jnp.concatenate([part.astype(jnp.bfloat16) for part in left], axis=1)
+                r0, r1, r2 = slices_of(jnp.concatenate([spec_ref[slot], spec_ref[SLOTS + slot]], axis=0), 3)
+                right = jnp.concatenate([r0, r1, r0, r2, r1, r0], axis=0)
+                out = jnp.dot(left, right, preferred_element_type=jnp.float32)
+                real, imag = out[:32], out[32:]
+                square = upper_imag[:NB, 32 * s:32 * s + NB]
+                if s == 0:
+                    last_real = jnp.where(is_first, imag, last_real)
+                    last_triangle = jnp.where(is_first, square, last_triangle)
+                    imag = jnp.where(is_first, 0.0, imag)
+                    square = jnp.where(is_first, 0.0, square)
+                put(slot, real, imag)
+                triangle_ref[0, slot] = upper_real[:NB, 32 * s:32 * s + NB]
+                triangle_ref[1, slot] = square
+    put(SLOTS, last_real, None)
+    triangle_ref[0, SLOTS] = last_triangle
+    triangle_ref[1, SLOTS] = jnp.zeros((NB, NB), jnp.float32)
+    for copy in copies:
+        copy.wait()
+
+
+def call(body, out_shape, scratch, operands, out_spaces=None):
     smem = pl.BlockSpec(memory_space=pltpu.SMEM)
     vmem = pl.BlockSpec(memory_space=pltpu.VMEM)
     return pl.pallas_call(
         body,
         out_shape=out_shape,
         in_specs=[smem] + [vmem] * (len(operands) - 1),
-        out_specs=jax.tree.map(lambda _: vmem, out_shape),
+        out_specs=[pl.BlockSpec(memory_space=space) for space in out_spaces] if out_spaces else jax.tree.map(lambda _: vmem, out_shape),
         scratch_shapes=scratch,
         compiler_params=pltpu.CompilerParams(vmem_limit_bytes=VMEM_BYTES),
     )(*operands)
@@ -393,9 +395,10 @@
     tiles = points // 128
     modes, triangle = call(
         apply_kernel,
-        (f32(NF, NB * tiles * 2, 128), f32(2, NF, NB, NB)),
-        [],
+        (f32(NF, NB, tiles * 2, 128), f32(2, NF, NB, NB)),
+        [pltpu.VMEM((NF, NB, tiles * 2, 128), jnp.float32), pltpu.SemaphoreType.DMA((NF,))],
         [place] + factors + [spec],
+        [pl.ANY, pltpu.VMEM],
     )
     modes = modes.reshape(NF, NB, tiles, 2, 128).transpose(3, 0, 1, 2, 4).reshape(2, NF, NB, points)
     return (modes, triangle)

time: 102 us -> 95.5 us (0.936)
  Pallas kernels: 24.4 us -> 18.3 us
    pallas_call x5, Pallas kernels: 24.4 us -> 18.3 us  [call(): pl.pallas_call(body, out_shape=out_shape, in_specs=[smem] + [vmem] * (len...]
where the time goes in v1:
time: 95.5 us; the launch traced here: 95.3 us
  waiting for transfers between devices  45.1 us (47%)
  starting transfers between devices  27.7 us (29%)
  Pallas kernels  18.3 us (19%)
  local copies, waits for them, and re-layouts  3.4 us (4%)
    ppermute x7, waiting for transfers between devices, shards(): lax.ppermute(piece, 'tm', xor_pairs(tm, d))  32.5 us
    pallas_call x5, Pallas kernels, call(): pl.pallas_call(body, out_shape=out_shape, in_specs=[smem] + [vmem] * (len...  18.3 us
    ppermute x7, starting transfers between devices, shards(): lax.ppermute(piece, 'tm', xor_pairs(tm, d))  12.4 us
    ppermute x3, starting transfers between devices, factor_over_devices(): lax.ppermute(total, 'tm', xor_pairs(tm, d))  7.67 us
    ppermute x3, waiting for transfers between devices, factor_over_devices(): lax.ppermute(parts[d], 'pts', xor_pairs(pts, d))  4.33 us
    ppermute x3, waiting for transfers between devices, factor_over_devices(): lax.ppermute(total, 'tm', xor_pairs(tm, d))  3.8 us
    ppermute x3, starting transfers between devices, factor_over_devices(): lax.ppermute(own, 'pts', xor_pairs(pts, d))  3.55 us
    ppermute x3, starting transfers between devices, factor_over_devices(): lax.ppermute(parts[d], 'pts', xor_pairs(pts, d))  3.55 us
  transfers between devices with their start and end apart: 21, of which 14 were waited for; matrix products, arithmetic and copies ran while one was open for 0% of the time, Pallas kernels for 0%

profile of v1, /device:TPU:0, one launch (start us, length us, event | category | flops | bytes accessed | tf_op | source)
XLA Modules:
  0.0 95.3 jit_solution(1676456437090818429)
XLA Ops:
  0.7 0.0 copy-start.1
  0.7 0.0 copy-start
  0.7 1.8 %constant_dynamic-slice_fusion = (f32[128,512]{1,0:T(8,128)S(1)}, f32[128,512]{1,0:T(8,128)S(1)}, f32[128,512]{1,0:T(8,128)S(1)}, f32[128,512]{1,0:T(8,128)S(1)}...) fusion(f32[128,4096]{1,0:T(8,128)} %param.3, ...), kind=kLoop, calls=%fused_computation | loop fusion | bytes 4194336 | tf_op jit(solution)/shard_map/dynamic_slice | solution.py:382
  2.5 4.6 %collective-permute-start.6 = (f32[128,512]{1,0:T(8,128)S(1)}, f32[128,512]{1,0:T(8,128)S(1)}, u32[]{:S(2)}, u32[]{:S(2)}) collective-permute-start(f32[128,512]{1,0:T(8,128)S(1)} %get-tuple-element.22), channel_id=1, source_target_pairs={{0,28},{4,24},{8,20},{12,16},{16,12},{20,8},{24,4},{28,0},{1,29},{... | collective-permute-start | bytes 786440 | tf_op jit(solution)/shard_map/ppermute | solution.py:383
  7.1 0.0 collective-permute-start.4
  7.1 3.2 %collective-permute-start.3 = (f32[128,512]{1,0:T(8,128)S(1)}, f32[128,512]{1,0:T(8,128)S(1)}, u32[]{:S(2)}, u32[]{:S(2)}) collective-permute-start(f32[128,512]{1,0:T(8,128)S(1)} %get-tuple-element.24), channel_id=1, source_target_pairs={{0,16},{4,20},{8,24},{12,28},{16,0},{20,4},{24,8},{28,12},{1,17},{... | collective-permute-start | bytes 786440 | tf_op jit(solution)/shard_map/ppermute | solution.py:383
  10.3 0.0 collective-permute-start.2
  10.3 1.2 %collective-permute-start.1 = (f32[128,512]{1,0:T(8,128)S(1)}, f32[128,512]{1,0:T(8,128)S(1)}, u32[]{:S(2)}, u32[]{:S(2)}) collective-permute-start(f32[128,512]{1,0:T(8,128)S(1)} %get-tuple-element.26), channel_id=1, source_target_pairs={{0,8},{4,12},{8,0},{12,4},{16,24},{20,28},{24,16},{28,20},{1,9},{5... | collective-permute-start | bytes 786440 | tf_op jit(solution)/shard_map/ppermute | solution.py:383
  11.5 2.4 %collective-permute-done.6.refs_7_ = f32[128,512]{1,0:T(8,128)S(1)} collective-permute-done((f32[128,512]{1,0:T(8,128)S(1)}, f32[128,512]{1,0:T(8,128)S(1)}, u32[]{:S(2)}, u32[]{:S(2)}) %collective-permute-start.6) | collective-permute-done | bytes 262176 | tf_op jit(solution)/shard_map/ppermute | solution.py:383
  13.9 0.8 collective-permute-start
  14.7 21.3 %collective-permute-done.4.refs_5_ = f32[128,512]{1,0:T(8,128)S(1)} collective-permute-done((f32[128,512]{1,0:T(8,128)S(1)}, f32[128,512]{1,0:T(8,128)S(1)}, u32[]{:S(2)}, u32[]{:S(2)}) %collective-permute-start.4) | collective-permute-done | bytes 262176 | tf_op jit(solution)/shard_map/ppermute | solution.py:383
  36.0 2.6 %collective-permute-start.5 = (f32[128,512]{1,0:T(8,128)S(1)}, f32[128,512]{1,0:T(8,128)S(1)}, u32[]{:S(2)}, u32[]{:S(2)}) collective-permute-start(f32[128,512]{1,0:T(8,128)S(1)} %get-tuple-element.29), channel_id=1, source_target_pairs={{0,24},{4,28},{8,16},{12,20},{16,8},{20,12},{24,0},{28,4},{1,25},{... | collective-permute-start | bytes 786440 | tf_op jit(solution)/shard_map/ppermute | solution.py:383
  38.6 0.0 copy-done.1
  38.6 0.1 pad_add_fusion.me_ref._
  38.7 8.8 %collective-permute-done.3.refs_4_ = f32[128,512]{1,0:T(8,128)S(1)} collective-permute-done((f32[128,512]{1,0:T(8,128)S(1)}, f32[128,512]{1,0:T(8,128)S(1)}, u32[]{:S(2)}, u32[]{:S(2)}) %collective-permute-start.3) | collective-permute-done | bytes 262176 | tf_op jit(solution)/shard_map/ppermute | solution.py:383
  47.5 0.0 collective-permute-done.2.refs_3_
  47.5 0.0 collective-permute-done.1.refs_2_
  47.5 0.0 collective-permute-done.refs_1_
  47.5 0.0 collective-permute-done.5.refs_6_
  47.5 0.0 copy-done
  47.5 7.7 %shard_map.50 = (f32[64,32,512]{2,1,0:T(8,128)S(1)}, f32[4,2,32,128]{3,2,1,0:T(8,128)S(1)}, f32[4,2,32,128]{3,2,1,0:T(8,128)S(1)}) custom-call(s32[2]{0:T(128)S(1)} %pad_add_fusion.me_ref._, f32[64,64]{1,0:T(8,128)S(1)} %copy-done, f32[1,512]{1,0:T(1,128)S(1)} %bitcast.8, f32[128,512]{1,0:T(8,128)S(1)} %get-tuple-element.28.refs_0_, ...), custom_call_target="tpu_custom_call" | custom-call | tf_op jit(solution)/shard_map/pallas_call | solution.py:341
  55.2 0.1 collective-permute-start.7
  55.3 1.3 %collective-permute-done.7.got_ref = f32[4,2,32,128]{3,2,1,0:T(8,128)S(1)} collective-permute-done((f32[4,2,32,128]{3,2,1,0:T(8,128)S(1)}, f32[4,2,32,128]{3,2,1,0:T(8,128)S(1)}, u32[]{:S(2)}, u32[]{:S(2)}) %collective-permute-start.7) | collective-permute-done | bytes 131104 | tf_op jit(solution)/shard_map/ppermute | solution.py:362
  56.6 0.6 shard_map.51
  57.2 1.6 %collective-permute-start.8 = (f32[2,32,128]{2,1,0:T(8,128)S(1)}, f32[2,32,128]{2,1,0:T(8,128)S(1)}, u32[]{:S(2)}, u32[]{:S(2)}) collective-permute-start(f32[2,32,128]{2,1,0:T(8,128)S(1)} %get-tuple-element.14), channel_id=1, source_target_pairs={{0,1},{1,0},{2,3},{3,2},{4,5},{5,4},{6,7},{7,6},{8,9},{9,8},{10,11... | collective-permute-start | bytes 98312 | tf_op jit(solution)/shard_map/ppermute | solution.py:364
  58.8 1.5 %collective-permute-start.9 = (f32[2,32,128]{2,1,0:T(8,128)S(1)}, f32[2,32,128]{2,1,0:T(8,128)S(1)}, u32[]{:S(2)}, u32[]{:S(2)}) collective-permute-start(f32[2,32,128]{2,1,0:T(8,128)S(1)} %get-tuple-element.15), channel_id=1, source_target_pairs={{0,2},{1,3},{2,0},{3,1},{4,6},{5,7},{6,4},{7,5},{8,10},{9,11},{10,... | collective-permute-start | bytes 98312 | tf_op jit(solution)/shard_map/ppermute | solution.py:364
  60.3 0.5 collective-permute-start.10
  60.8 0.4 collective-permute-done.8.refs_1_
  61.2 1.5 %collective-permute-done.9.refs_2_ = f32[2,32,128]{2,1,0:T(8,128)S(1)} collective-permute-done((f32[2,32,128]{2,1,0:T(8,128)S(1)}, f32[2,32,128]{2,1,0:T(8,128)S(1)}, u32[]{:S(2)}, u32[]{:S(2)}) %collective-permute-start.9) | collective-permute-done | bytes 32800 | tf_op jit(solution)/shard_map/ppermute | solution.py:364
  62.7 2.4 %collective-permute-done.10.refs_3_ = f32[2,32,128]{2,1,0:T(8,128)S(1)} collective-permute-done((f32[2,32,128]{2,1,0:T(8,128)S(1)}, f32[2,32,128]{2,1,0:T(8,128)S(1)}, u32[]{:S(2)}, u32[]{:S(2)}) %collective-permute-start.10) | collective-permute-done | bytes 32800 | tf_op jit(solution)/shard_map/ppermute | solution.py:364
  65.1 0.6 shard_map.52.refs_0_
  65.7 2.4 %collective-permute-start.13 = (f32[2,32,128]{2,1,0:T(8,128)S(1)}, f32[2,32,128]{2,1,0:T(8,128)S(1)}, u32[]{:S(2)}, u32[]{:S(2)}) collective-permute-start(f32[2,32,128]{2,1,0:T(8,128)S(1)} %shard_map.52.refs_0_), channel_id=1, source_target_pairs={{0,24},{4,28},{8,16},{12,20},{16,8},{20,12},{24,0},{28,4},{1,25},{... | collective-permute-start | bytes 98312 | tf_op jit(solution)/shard_map/ppermute | solution.py:369
  68.1 5.1 %collective-permute-start.12 = (f32[2,32,128]{2,1,0:T(8,128)S(1)}, f32[2,32,128]{2,1,0:T(8,128)S(1)}, u32[]{:S(2)}, u32[]{:S(2)}) collective-permute-start(f32[2,32,128]{2,1,0:T(8,128)S(1)} %shard_map.52.refs_0_), channel_id=1, source_target_pairs={{0,16},{4,20},{8,24},{12,28},{16,0},{20,4},{24,8},{28,12},{1,17},{... | collective-permute-start | bytes 98312 | tf_op jit(solution)/shard_map/ppermute | solution.py:369
  73.2 0.1 collective-permute-start.11
  73.4 0.0 collective-permute-done.13.refs_3_
  73.4 2.1 %collective-permute-done.12.refs_2_ = f32[2,32,128]{2,1,0:T(8,128)S(1)} collective-permute-done((f32[2,32,128]{2,1,0:T(8,128)S(1)}, f32[2,32,128]{2,1,0:T(8,128)S(1)}, u32[]{:S(2)}, u32[]{:S(2)}) %collective-permute-start.12) | collective-permute-done | bytes 32800 | tf_op jit(solution)/shard_map/ppermute | solution.py:369
  75.5 1.7 %collective-permute-done.11.refs_1_ = f32[2,32,128]{2,1,0:T(8,128)S(1)} collective-permute-done((f32[2,32,128]{2,1,0:T(8,128)S(1)}, f32[2,32,128]{2,1,0:T(8,128)S(1)}, u32[]{:S(2)}, u32[]{:S(2)}) %collective-permute-start.11) | collective-permute-done | bytes 32800 | tf_op jit(solution)/shard_map/ppermute | solution.py:369
  77.2 4.8 %shard_map.53.refs_0_ = f32[2,32,128]{2,1,0:T(8,128)S(1)} custom-call(s32[2]{0:T(128)S(1)} %pad_add_fusion.me_ref._, f32[2,32,128]{2,1,0:T(8,128)S(1)} %shard_map.52.refs_0_, f32[2,32,128]{2,1,0:T(8,128)S(1)} %collective-permute-done.11.refs_1_, f32[2,32,128]{2,1,0:T(8,128)S(1)} %collective-permute-done.12.refs_2_, ...), custom_call_target="tpu_custom_call" | custom-call | tf_op jit(solution)/shard_map/pallas_call | solution.py:341
  82.0 0.5 collective-permute-start.16
  82.5 1.5 %collective-permute-start.15 = (f32[2,32,128]{2,1,0:T(8,128)S(1)}, f32[2,32,128]{2,1,0:T(8,128)S(1)}, u32[]{:S(2)}, u32[]{:S(2)}) collective-permute-start(f32[2,32,128]{2,1,0:T(8,128)S(1)} %shard_map.53.refs_0_), channel_id=1, source_target_pairs={{0,2},{1,3},{2,0},{3,1},{4,6},{5,7},{6,4},{7,5},{8,10},{9,11},{10,... | collective-permute-start | bytes 98312 | tf_op jit(solution)/shard_map/ppermute | solution.py:371
  84.1 1.5 %collective-permute-start.14 = (f32[2,32,128]{2,1,0:T(8,128)S(1)}, f32[2,32,128]{2,1,0:T(8,128)S(1)}, u32[]{:S(2)}, u32[]{:S(2)}) collective-permute-start(f32[2,32,128]{2,1,0:T(8,128)S(1)} %shard_map.53.refs_0_), channel_id=1, source_target_pairs={{0,1},{1,0},{2,3},{3,2},{4,5},{5,4},{6,7},{7,6},{8,9},{9,8},{10,11... | collective-permute-start | bytes 98312 | tf_op jit(solution)/shard_map/ppermute | solution.py:371
  85.6 0.0 collective-permute-start.17
  85.6 1.3 %collective-permute-done.16.refs_3_ = f32[2,32,128]{2,1,0:T(8,128)S(1)} collective-permute-done((f32[2,32,128]{2,1,0:T(8,128)S(1)}, f32[2,32,128]{2,1,0:T(8,128)S(1)}, u32[]{:S(2)}, u32[]{:S(2)}) %collective-permute-start.16) | collective-permute-done | bytes 32800 | tf_op jit(solution)/shard_map/ppermute | solution.py:371
  86.9 0.0 collective-permute-start.20
  86.9 0.0 collective-permute-done.15.refs_2_
  86.9 0.5 collective-permute-start.19
  87.4 0.6 collective-permute-done.14.refs_1_
  88.0 0.0 collective-permute-start.18
  88.0 0.0 collective-permute-done.17.refs_4_
  88.0 0.1 collective-permute-done.20.refs_7_
  88.1 0.2 collective-permute-done.19.refs_6_
  88.3 0.9 collective-permute-done.18.refs_5_
  89.2 4.6 %shard_map.54 = (f32[33,31,8,128]{3,2,1,0:T(8,128)}, f32[2,33,31,31]{3,2,1,0:T(8,128)S(1)}) custom-call(s32[2]{0:T(128)S(1)} %pad_add_fusion.me_ref._, f32[2,32,128]{2,1,0:T(8,128)S(1)} %shard_map.53.refs_0_, f32[2,32,128]{2,1,0:T(8,128)S(1)} %collective-permute-done.14.refs_1_, f32[2,32,128]{2,1,0:T(8,128)S(1)} %collective-permute-done.15.refs_2_, ...), custom_call_target="tpu_custom_call" | custom-call | tf_op jit(solution)/shard_map/pallas_call | solution.py:341
  93.8 1.6 %copy.6 = f32[2,33,31,31]{1,0,3,2:T(2,128)} copy(f32[2,33,31,31]{3,2,1,0:T(8,128)S(1)} %get-tuple-element.21) | data formatting | bytes 507408
  (1 shorter events, 0.0 us)
Async XLA Ops:
  0.7 37.9 %copy-start.1 = (f32[512]{0:T(512)S(1)}, f32[512]{0:T(512)}, u32[]{:S(2)}) copy-start(f32[512]{0:T(512)} %param.4) | copy-start | bytes 6148
  0.7 46.8 %copy-start = (f32[64,64]{1,0:T(8,128)S(1)}, f32[64,64]{1,0:T(8,128)}, u32[]{:S(2)}) copy-start(f32[64,64]{1,0:T(8,128)} %constant.31.clone.table_ref) | copy-start | bytes 49156
  2.5 11.3 %collective-permute-start.6 = (f32[128,512]{1,0:T(8,128)S(1)}, f32[128,512]{1,0:T(8,128)S(1)}, u32[]{:S(2)}, u32[]{:S(2)}) collective-permute-start(f32[128,512]{1,0:T(8,128)S(1)} %get-tuple-element.22), channel_id=1, source_target_pairs={{0,28},{4,24},{8,20},{12,16},{16,12},{20,8},{24,4},{28,0},{1,29},{... | collective-permute-start | bytes 786440 | tf_op jit(solution)/shard_map/ppermute | solution.py:383
  7.1 28.9 %collective-permute-start.4 = (f32[128,512]{1,0:T(8,128)S(1)}, f32[128,512]{1,0:T(8,128)S(1)}, u32[]{:S(2)}, u32[]{:S(2)}) collective-permute-start(f32[128,512]{1,0:T(8,128)S(1)} %get-tuple-element.23), channel_id=1, source_target_pairs={{0,20},{4,16},{8,28},{12,24},{16,4},{20,0},{24,12},{28,8},{1,21},{... | collective-permute-start | bytes 786440 | tf_op jit(solution)/shard_map/ppermute | solution.py:383
  7.1 40.4 %collective-permute-start.3 = (f32[128,512]{1,0:T(8,128)S(1)}, f32[128,512]{1,0:T(8,128)S(1)}, u32[]{:S(2)}, u32[]{:S(2)}) collective-permute-start(f32[128,512]{1,0:T(8,128)S(1)} %get-tuple-element.24), channel_id=1, source_target_pairs={{0,16},{4,20},{8,24},{12,28},{16,0},{20,4},{24,8},{28,12},{1,17},{... | collective-permute-start | bytes 786440 | tf_op jit(solution)/shard_map/ppermute | solution.py:383
  10.3 37.2 %collective-permute-start.2 = (f32[128,512]{1,0:T(8,128)S(1)}, f32[128,512]{1,0:T(8,128)S(1)}, u32[]{:S(2)}, u32[]{:S(2)}) collective-permute-start(f32[128,512]{1,0:T(8,128)S(1)} %get-tuple-element.25), channel_id=1, source_target_pairs={{0,12},{4,8},{8,4},{12,0},{16,28},{20,24},{24,20},{28,16},{1,13},{... | collective-permute-start | bytes 786440 | tf_op jit(solution)/shard_map/ppermute | solution.py:383
  10.3 37.2 %collective-permute-start.1 = (f32[128,512]{1,0:T(8,128)S(1)}, f32[128,512]{1,0:T(8,128)S(1)}, u32[]{:S(2)}, u32[]{:S(2)}) collective-permute-start(f32[128,512]{1,0:T(8,128)S(1)} %get-tuple-element.26), channel_id=1, source_target_pairs={{0,8},{4,12},{8,0},{12,4},{16,24},{20,28},{24,16},{28,20},{1,9},{5... | collective-permute-start | bytes 786440 | tf_op jit(solution)/shard_map/ppermute | solution.py:383
  13.9 33.6 %collective-permute-start = (f32[128,512]{1,0:T(8,128)S(1)}, f32[128,512]{1,0:T(8,128)S(1)}, u32[]{:S(2)}, u32[]{:S(2)}) collective-permute-start(f32[128,512]{1,0:T(8,128)S(1)} %get-tuple-element.27), channel_id=1, source_target_pairs={{0,4},{4,0},{8,12},{12,8},{16,20},{20,16},{24,28},{28,24},{1,5},{5... | collective-permute-start | bytes 786440 | tf_op jit(solution)/shard_map/ppermute | solution.py:383
  36.0 11.5 %collective-permute-start.5 = (f32[128,512]{1,0:T(8,128)S(1)}, f32[128,512]{1,0:T(8,128)S(1)}, u32[]{:S(2)}, u32[]{:S(2)}) collective-permute-start(f32[128,512]{1,0:T(8,128)S(1)} %get-tuple-element.29), channel_id=1, source_target_pairs={{0,24},{4,28},{8,16},{12,20},{16,8},{20,12},{24,0},{28,4},{1,25},{... | collective-permute-start | bytes 786440 | tf_op jit(solution)/shard_map/ppermute | solution.py:383
  55.2 1.4 %collective-permute-start.7 = (f32[4,2,32,128]{3,2,1,0:T(8,128)S(1)}, f32[4,2,32,128]{3,2,1,0:T(8,128)S(1)}, u32[]{:S(2)}, u32[]{:S(2)}) collective-permute-start(f32[4,2,32,128]{3,2,1,0:T(8,128)S(1)} %get-tuple-element.12), channel_id=1, source_target_pairs={{0,4},{4,0},{8,12},{12,8},{16,20},{20,16},{24,28},{28,24},{1,5},{5... | collective-permute-start | bytes 393224 | tf_op jit(solution)/shard_map/ppermute | solution.py:362
  57.2 4.0 %collective-permute-start.8 = (f32[2,32,128]{2,1,0:T(8,128)S(1)}, f32[2,32,128]{2,1,0:T(8,128)S(1)}, u32[]{:S(2)}, u32[]{:S(2)}) collective-permute-start(f32[2,32,128]{2,1,0:T(8,128)S(1)} %get-tuple-element.14), channel_id=1, source_target_pairs={{0,1},{1,0},{2,3},{3,2},{4,5},{5,4},{6,7},{7,6},{8,9},{9,8},{10,11... | collective-permute-start | bytes 98312 | tf_op jit(solution)/shard_map/ppermute | solution.py:364
  58.8 3.9 %collective-permute-start.9 = (f32[2,32,128]{2,1,0:T(8,128)S(1)}, f32[2,32,128]{2,1,0:T(8,128)S(1)}, u32[]{:S(2)}, u32[]{:S(2)}) collective-permute-start(f32[2,32,128]{2,1,0:T(8,128)S(1)} %get-tuple-element.15), channel_id=1, source_target_pairs={{0,2},{1,3},{2,0},{3,1},{4,6},{5,7},{6,4},{7,5},{8,10},{9,11},{10,... | collective-permute-start | bytes 98312 | tf_op jit(solution)/shard_map/ppermute | solution.py:364
  60.3 4.8 %collective-permute-start.10 = (f32[2,32,128]{2,1,0:T(8,128)S(1)}, f32[2,32,128]{2,1,0:T(8,128)S(1)}, u32[]{:S(2)}, u32[]{:S(2)}) collective-permute-start(f32[2,32,128]{2,1,0:T(8,128)S(1)} %get-tuple-element.16), channel_id=1, source_target_pairs={{0,3},{1,2},{2,1},{3,0},{4,7},{5,6},{6,5},{7,4},{8,11},{9,10},{10,... | collective-permute-start | bytes 98312 | tf_op jit(solution)/shard_map/ppermute | solution.py:364
  65.7 7.7 %collective-permute-start.13 = (f32[2,32,128]{2,1,0:T(8,128)S(1)}, f32[2,32,128]{2,1,0:T(8,128)S(1)}, u32[]{:S(2)}, u32[]{:S(2)}) collective-permute-start(f32[2,32,128]{2,1,0:T(8,128)S(1)} %shard_map.52.refs_0_), channel_id=1, source_target_pairs={{0,24},{4,28},{8,16},{12,20},{16,8},{20,12},{24,0},{28,4},{1,25},{... | collective-permute-start | bytes 98312 | tf_op jit(solution)/shard_map/ppermute | solution.py:369
  68.1 7.4 %collective-permute-start.12 = (f32[2,32,128]{2,1,0:T(8,128)S(1)}, f32[2,32,128]{2,1,0:T(8,128)S(1)}, u32[]{:S(2)}, u32[]{:S(2)}) collective-permute-start(f32[2,32,128]{2,1,0:T(8,128)S(1)} %shard_map.52.refs_0_), channel_id=1, source_target_pairs={{0,16},{4,20},{8,24},{12,28},{16,0},{20,4},{24,8},{28,12},{1,17},{... | collective-permute-start | bytes 98312 | tf_op jit(solution)/shard_map/ppermute | solution.py:369
  73.2 3.9 %collective-permute-start.11 = (f32[2,32,128]{2,1,0:T(8,128)S(1)}, f32[2,32,128]{2,1,0:T(8,128)S(1)}, u32[]{:S(2)}, u32[]{:S(2)}) collective-permute-start(f32[2,32,128]{2,1,0:T(8,128)S(1)} %shard_map.52.refs_0_), channel_id=1, source_target_pairs={{0,8},{4,12},{8,0},{12,4},{16,24},{20,28},{24,16},{28,20},{1,9},{5... | collective-permute-start | bytes 98312 | tf_op jit(solution)/shard_map/ppermute | solution.py:369
  82.0 4.9 %collective-permute-start.16 = (f32[2,32,128]{2,1,0:T(8,128)S(1)}, f32[2,32,128]{2,1,0:T(8,128)S(1)}, u32[]{:S(2)}, u32[]{:S(2)}) collective-permute-start(f32[2,32,128]{2,1,0:T(8,128)S(1)} %shard_map.53.refs_0_), channel_id=1, source_target_pairs={{0,3},{1,2},{2,1},{3,0},{4,7},{5,6},{6,5},{7,4},{8,11},{9,10},{10,... | collective-permute-start | bytes 98312 | tf_op jit(solution)/shard_map/ppermute | solution.py:371
  82.5 4.3 %collective-permute-start.15 = (f32[2,32,128]{2,1,0:T(8,128)S(1)}, f32[2,32,128]{2,1,0:T(8,128)S(1)}, u32[]{:S(2)}, u32[]{:S(2)}) collective-permute-start(f32[2,32,128]{2,1,0:T(8,128)S(1)} %shard_map.53.refs_0_), channel_id=1, source_target_pairs={{0,2},{1,3},{2,0},{3,1},{4,6},{5,7},{6,4},{7,5},{8,10},{9,11},{10,... | collective-permute-start | bytes 98312 | tf_op jit(solution)/shard_map/ppermute | solution.py:371
  84.1 3.9 %collective-permute-start.14 = (f32[2,32,128]{2,1,0:T(8,128)S(1)}, f32[2,32,128]{2,1,0:T(8,128)S(1)}, u32[]{:S(2)}, u32[]{:S(2)}) collective-permute-start(f32[2,32,128]{2,1,0:T(8,128)S(1)} %shard_map.53.refs_0_), channel_id=1, source_target_pairs={{0,1},{1,0},{2,3},{3,2},{4,5},{5,4},{6,7},{7,6},{8,9},{9,8},{10,11... | collective-permute-start | bytes 98312 | tf_op jit(solution)/shard_map/ppermute | solution.py:371
  85.6 2.4 %collective-permute-start.17 = (f32[2,32,128]{2,1,0:T(8,128)S(1)}, f32[2,32,128]{2,1,0:T(8,128)S(1)}, u32[]{:S(2)}, u32[]{:S(2)}) collective-permute-start(f32[2,32,128]{2,1,0:T(8,128)S(1)} %shard_map.53.refs_0_), channel_id=1, source_target_pairs={{0,4},{4,0},{8,12},{12,8},{16,20},{20,16},{24,28},{28,24},{1,5},{5... | collective-permute-start | bytes 98312 | tf_op jit(solution)/shard_map/ppermute | solution.py:372
  86.9 1.2 %collective-permute-start.20 = (f32[2,32,128]{2,1,0:T(8,128)S(1)}, f32[2,32,128]{2,1,0:T(8,128)S(1)}, u32[]{:S(2)}, u32[]{:S(2)}) collective-permute-start(f32[2,32,128]{2,1,0:T(8,128)S(1)} %collective-permute-done.16.refs_3_), channel_id=1, source_target_pairs={{0,4},{4,0},{8,12},{12,8},{16,20},{20,16},{24,28},{28,24},{1,5},{5... | collective-permute-start | bytes 98312 | tf_op jit(solution)/shard_map/ppermute | solution.py:372
  86.9 1.4 %collective-permute-start.19 = (f32[2,32,128]{2,1,0:T(8,128)S(1)}, f32[2,32,128]{2,1,0:T(8,128)S(1)}, u32[]{:S(2)}, u32[]{:S(2)}) collective-permute-start(f32[2,32,128]{2,1,0:T(8,128)S(1)} %collective-permute-done.15.refs_2_), channel_id=1, source_target_pairs={{0,4},{4,0},{8,12},{12,8},{16,20},{20,16},{24,28},{28,24},{1,5},{5... | collective-permute-start | bytes 98312 | tf_op jit(solution)/shard_map/ppermute | solution.py:372
  88.0 1.2 %collective-permute-start.18 = (f32[2,32,128]{2,1,0:T(8,128)S(1)}, f32[2,32,128]{2,1,0:T(8,128)S(1)}, u32[]{:S(2)}, u32[]{:S(2)}) collective-permute-start(f32[2,32,128]{2,1,0:T(8,128)S(1)} %collective-permute-done.14.refs_1_), channel_id=1, source_target_pairs={{0,4},{4,0},{8,12},{12,8},{16,20},{20,16},{24,28},{28,24},{1,5},{5... | collective-permute-start | bytes 98312 | tf_op jit(solution)/shard_map/ppermute | solution.py:372

commit v2 on v1

--- a/solution.py
+++ b/solution.py
@@ -74,15 +74,19 @@
 
 
 def spectrum_body(table_t, records, spec_ref):
-    t1, t2, t3 = slices_of(table_t, 3)
+    halves_t = jnp.concatenate([table_t[:, :HOP], table_t[:, HOP:]], axis=0)
+    t1, t2, t3 = slices_of(halves_t, 3)
     left = jnp.concatenate([t1, t1, t1, t2, t2, t3], axis=1)
     x1, x2, x3 = slices_of(records, 3)
-    points = records.shape[1]
-    for b in range(NB):
-        at = slice(HOP * b, HOP * b + SEG)
+    before = None
+    for hop in range(NT // HOP):
+        at = slice(HOP * hop, HOP * hop + HOP)
         right = jnp.concatenate([x1[at], x2[at], x3[at], x1[at], x2[at], x1[at]], axis=0)
-        spec_ref[:, b, :] = jnp.dot(left, right, preferred_element_type=jnp.float32)
-    spec_ref[:, NB, :] = jnp.zeros((SEG, points), jnp.float32)
+        out = jnp.dot(left, right, preferred_element_type=jnp.float32)
+        if hop:
+            spec_ref[:, hop - 1, :] = before + out[SEG:]
+        before = out[:SEG]
+    spec_ref[:, NB, :] = jnp.zeros((SEG, records.shape[1]), jnp.float32)
 
 
 def cut_rows(real, imag):
@@ -97,9 +101,12 @@
     return cuts
 
 
-def gram_slot(real, imag, two_real):
+def gram_products(real, imag):
     rows = jnp.concatenate([part for cut in cut_rows(real, imag) for part in cut], axis=0).astype(jnp.bfloat16)
-    products = lax.dot_general(rows, rows, (((1,), (1,)), ((), ())), preferred_element_type=jnp.float32)
+    return lax.dot_general(rows, rows, (((1,), (1,)), ((), ())), preferred_element_type=jnp.float32)
+
+
+def gram_pairs(products, two_real):
     lane = lax.broadcasted_iota(jnp.int32, (32, 128), 1)
     is_real = lane // 32 % 2 == 0
     front = lane < 64
@@ -129,35 +136,42 @@
     return total, low - (total - high)
 
 
-def spectrum_kernel(me_ref, table_ref, root_ref, *refs, tm):
-    pieces, (spec_ref, keep_ref, send_ref, records_ref) = refs[:tm], refs[tm:]
-    rows = pieces[0].shape[0]
-    root = root_ref[...]
-    for d in range(tm):
+def spectrum_kernel(me_ref, table_ref, root_ref, *refs, places):
+    pieces, (spec_ref, keep_ref, send_ref, records_ref) = refs[:len(places)], refs[len(places):]
+    for (d, first), piece in zip(places, pieces):
+        rows, size = piece.shape
         start = pl.multiple_of((me_ref[0] ^ d) * rows, rows)
-        records_ref[pl.ds(start, rows), :] = pieces[d][...] * root
+        at = slice(first, first + size)
+        records_ref[pl.ds(start, rows), at] = piece[...] * root_ref[:, at]
     spectrum_body(table_ref[...], records_ref[...], spec_ref)
     core = me_ref[0] & 1
     row = lax.broadcasted_iota(jnp.int32, (32, 32), 0)
     column = lax.broadcasted_iota(jnp.int32, (32, 32), 1)
-    for j, out_ref in ((1, send_ref), (0, keep_ref)):
-        side = core ^ j
-        for q in range(SIDE):
+    order = [(j, q, s) for j in (1, 0) for q in range(SIDE) for s in range(4)]
+
+    def products_of(step):
+        j, q, s = order[step]
+        slot = ((core ^ j) * SIDE + q) * 4 + s
+        return gram_products(spec_ref[slot], spec_ref[SLOTS + slot])
+
+    ahead = products_of(0)
+    for step, (j, q, s) in enumerate(order):
+        products = ahead
+        if step + 1 < len(order):
+            ahead = products_of(step + 1)
+        special = q == 0 and s == 0
+        if s == 0:
             packed = [[], []]
-            for s in range(4):
-                slot = (side * SIDE + q) * 4 + s
-                special = q == 0 and s == 0
-                two_real = side == 0 if special else None
-                sums = gram_slot(spec_ref[slot], spec_ref[SLOTS + slot], two_real)
-                for part in range(2):
-                    real, imag = sums[part][:, :32], sums[part][:, 32:]
-                    square = jnp.where(column >= row, real, imag)
-                    if special:
-                        diagonal = jnp.sum(jnp.where(column == row, imag, 0.0), axis=0, keepdims=True)
-                        square = jnp.where(row == NB, diagonal, square)
-                    packed[part].append(square)
-            for part in range(2):
-                out_ref[q, part] = jnp.concatenate(packed[part], axis=1)
+        sums = gram_pairs(products, (core ^ j) == 0 if special else None)
+        for part in range(2):
+            real, imag = sums[part][:, :32], sums[part][:, 32:]
+            square = jnp.where(column >= row, real, imag)
+            if special:
+                diagonal = jnp.sum(jnp.where(column == row, imag, 0.0), axis=0, keepdims=True)
+                square = jnp.where(row == NB, diagonal, square)
+            packed[part].append(square)
+            if s == 3:
+                (keep_ref, send_ref)[j][q, part] = jnp.concatenate(packed[part], axis=1)
 
 
 def core_sum_kernel(me_ref, keep_ref, got_ref, *out_refs):
@@ -186,7 +200,6 @@
     row = lax.broadcasted_iota(jnp.int32, shape, 0)
     lane = lax.broadcasted_iota(jnp.int32, shape, 1)
     column = lane % 32
-    base = lane - column
     first = jnp.logical_and((me_ref[0] & 1) == 0, (me_ref[1] & (SIDE - 1)) == 0)
     two_real = jnp.logical_and(lane < 32, first)
     sign = jnp.where(two_real, 1.0, -1.0)
@@ -200,17 +213,21 @@
     real = [jnp.where(inside, part * scale, 0.0) for part in real]
     imag = [jnp.where(inside, part * scale, 0.0) for part in imag]
 
+    shape = (8, 128)
+    row = lax.broadcasted_iota(jnp.int32, shape, 0)
+    lane = lax.broadcasted_iota(jnp.int32, shape, 1)
+    column = lane % 32
+    base = lane - column
+    two_real = jnp.logical_and(lane < 32, first)
+    real = [[part[8 * i:8 * i + 8] for part in real] for i in range(4)]
+    imag = [[part[8 * i:8 * i + 8] for part in imag] for i in range(4)]
+
     def spread(value, at):
         return jnp.take_along_axis(value, base + at, axis=1, mode="promise_in_bounds")
 
-    def rows_of(value, at):
-        return jnp.broadcast_to(value[at:at + 1], shape)
-
     def quotient(value, pivot, pivot_halves, inverse):
         first_part = value[0] * inverse
-        product, error = pair_product(
-            (first_part, 0.0), halves(first_part), (pivot[0], 0.0), pivot_halves
-        )
+        product, error = pair_product((first_part, 0.0), halves(first_part), (pivot[0], 0.0), pivot_halves)
         rest = ((value[0] - product) - error) + (value[1] - first_part * pivot[1])
         return first_part, rest * inverse
 
@@ -223,40 +240,50 @@
         return [total, low - (total - high)]
 
     for k in range(NB):
-        line_real = [rows_of(part, k) for part in real]
-        line_imag = [rows_of(part, k) for part in imag]
+        at = k % 8
+        line_real = [jnp.broadcast_to(part[at:at + 1], shape) for part in real[k // 8]]
+        line_imag = [jnp.broadcast_to(part[at:at + 1], shape) for part in imag[k // 8]]
         pivot_real = [spread(part, k) for part in line_real]
         pivot_imag = [jnp.where(two_real, spread(part, k), own) for part, own in zip(line_imag, pivot_real)]
-        below = row > k
+        real_halves, imag_halves = halves(pivot_real[0]), halves(pivot_imag[0])
+        real_inverse = 1.0 / pivot_real[0]
+        imag_inverse = jnp.where(two_real, 1.0 / pivot_imag[0], real_inverse)
         here = column == k
-        step_real = [jnp.where(below, spread(part, k), 0.0) for part in real]
-        step_imag = [jnp.where(below, spread(part, k), 0.0) for part in imag]
-        step_real = quotient(step_real, pivot_real, halves(pivot_real[0]), 1.0 / pivot_real[0])
-        step_imag = quotient(step_imag, pivot_imag, halves(pivot_imag[0]), 1.0 / pivot_imag[0])
-        cross = tuple(jnp.where(two_real, 0.0, part) for part in step_imag)
-        own = tuple(jnp.where(two_real, b, a) for a, b in zip(step_real, step_imag))
-        one = jnp.where(here, 1.0, 0.0)
         line_real = (jnp.where(here, 1.0, line_real[0]), jnp.where(here, 0.0, line_real[1]))
         line_imag = (
             jnp.where(here, jnp.where(two_real, 1.0, 0.0), line_imag[0]),
             jnp.where(here, 0.0, line_imag[1]),
         )
-        clear = jnp.logical_and(below, here)
-        real = [jnp.where(clear, 0.0, part) for part in real]
-        imag = [jnp.where(clear, 0.0, part) for part in imag]
         line_real_halves, line_imag_halves = halves(line_real[0]), halves(line_imag[0])
-        step_halves, cross_halves, own_halves = halves(step_real[0]), halves(cross[0]), halves(own[0])
-        p = pair_product(step_real, step_halves, line_real, line_real_halves)
-        q = pair_product(cross, cross_halves, line_imag, line_imag_halves)
-        real = minus(real, [p, (-q[0], -q[1])])
-        p = pair_product(own, own_halves, line_imag, line_imag_halves)
-        q = pair_product(cross, cross_halves, line_real, line_real_halves)
-        imag = minus(imag, [p, q])
-    pivot_real = spread(real[0], row)
-    pivot_imag = jnp.where(two_real, spread(imag[0], row), pivot_real)
-    good = row < NB
-    out_ref[0] = jnp.where(good, real[0] / jnp.sqrt(pivot_real), 0.0)
-    out_ref[1] = jnp.where(good, imag[0] / jnp.sqrt(pivot_imag), 0.0)
+        for i in range((k + 1) // 8, 4):
+            some = 8 * i <= k
+            below = row > k - 8 * i
+            step_real = [spread(part, k) for part in real[i]]
+            step_imag = [spread(part, k) for part in imag[i]]
+            if some:
+                step_real = [jnp.where(below, part, 0.0) for part in step_real]
+                step_imag = [jnp.where(below, part, 0.0) for part in step_imag]
+            step_real = quotient(step_real, pivot_real, real_halves, real_inverse)
+            step_imag = quotient(step_imag, pivot_imag, imag_halves, imag_inverse)
+            cross = tuple(jnp.where(two_real, 0.0, part) for part in step_imag)
+            own = tuple(jnp.where(two_real, b, a) for a, b in zip(step_real, step_imag))
+            clear = jnp.logical_and(below, here) if some else here
+            block_real = [jnp.where(clear, 0.0, part) for part in real[i]]
+            block_imag = [jnp.where(clear, 0.0, part) for part in imag[i]]
+            step_halves, cross_halves, own_halves = halves(step_real[0]), halves(cross[0]), halves(own[0])
+            p = pair_product(step_real, step_halves, line_real, line_real_halves)
+            q = pair_product(cross, cross_halves, line_imag, line_imag_halves)
+            real[i] = minus(block_real, [p, (-q[0], -q[1])])
+            p = pair_product(own, own_halves, line_imag, line_imag_halves)
+            q = pair_product(cross, cross_halves, line_real, line_real_halves)
+            imag[i] = minus(block_imag, [p, q])
+    for i in range(4):
+        at = slice(8 * i, 8 * i + 8)
+        pivot_real = spread(real[i][0], row + 8 * i)
+        pivot_imag = jnp.where(two_real, spread(imag[i][0], row + 8 * i), pivot_real)
+        good = row + 8 * i < NB
+        out_ref[0, at] = jnp.where(good, real[i][0] / jnp.sqrt(pivot_real), 0.0)
+        out_ref[1, at] = jnp.where(good, imag[i][0] / jnp.sqrt(pivot_imag), 0.0)
 
 
 def apply_kernel(me_ref, *refs):
@@ -361,7 +388,8 @@
     part = f32(2, 32, 128)
     got = lax.ppermute(send, "tm", xor_pairs(tm, 1))
     parts = call(core_sum_kernel, (part,) * SIDE, [], [place, keep, got])
-    parts = [parts[0]] + [lax.ppermute(parts[d], "pts", xor_pairs(pts, d)) for d in range(1, SIDE)]
+    parts = [lax.ppermute(parts[d], "pts", xor_pairs(pts, d)) for d in reversed(range(1, SIDE))] + [parts[0]]
+    parts = parts[::-1]
     total = call(lambda _, *refs: pair_sum_kernel(*refs), part, [], [place] + parts)
     if pts > SIDE:
         parts = [total] + [lax.ppermute(total, "pts", xor_pairs(pts, d)) for d in range(SIDE, pts, SIDE)]
@@ -377,19 +405,38 @@
     me = lax.axis_index("tm")
     points = weights.shape[0]
     scale = 1.0 / (points * tm * pts)
-    pieces = []
-    for d in range(tm):
-        piece = lax.dynamic_slice_in_dim(snapshots, (me ^ d) * points, points, 1)
-        pieces.append(piece if d == 0 else lax.ppermute(piece, "tm", xor_pairs(tm, d)))
+
+    def piece_of(array, d, start, size):
+        return lax.dynamic_slice_in_dim(array, (me ^ d) * points + start, size, 1)
+
+    def exchanged(piece, d):
+        return lax.ppermute(piece, "tm", xor_pairs(tm, d))
+
+    last = max(128, points // 4 // 128 * 128)
+    body = points - last
+    parted = {tm // 2: tm - 1, 3 * tm // 4: tm - 1}
+    pieces = {}
+    farthest = tm - 1
+    sent = piece_of(snapshots, farthest, 0, points)
+    rest, sent = lax.optimization_barrier((snapshots, sent))
+    pieces[farthest, 0] = exchanged(sent, farthest)
+    for d in reversed(range(farthest)):
+        piece = piece_of(rest, d, 0, body if d in parted else points)
+        pieces[d, 0] = exchanged(piece, d) if d else piece
+    for d, after in parted.items():
+        sent = piece_of(rest, d, body, last)
+        if after is not None:
+            sent, _ = lax.optimization_barrier((sent, pieces[after, 0]))
+        pieces[d, body] = exchanged(sent, d)
     root = jnp.sqrt(weights)[None, :]
     table_t = jnp.asarray(fourier_table().T)
     place = jnp.stack([me, lax.axis_index("pts")]).astype(jnp.int32)
     half = f32(SIDE, 2, 32, 128)
     spec, keep, send = call(
-        functools.partial(spectrum_kernel, tm=tm),
+        functools.partial(spectrum_kernel, places=tuple(pieces)),
         (f32(SEG, 32, points), half, half),
         [pltpu.VMEM((NT, points), jnp.float32)],
-        [place, table_t, root] + pieces,
+        [place, table_t, root, *pieces.values()],
     )
     factors = factor_over_devices(place, keep, send, scale)
     tiles = points // 128

time: 95.5 us -> 93.9 us (0.983)
  local copies, waits for them, and re-layouts: 3.4 us -> 5.9 us
  waiting for transfers between devices: 45.1 us -> 42.9 us
  Pallas kernels: 18.3 us -> 17.1 us
    ppermute x3, starting transfers between devices: 7.67 us -> 4.45 us  [factor_over_devices(): lax.ppermute(total, 'tm', xor_pairs(tm, d))]
    dynamic_slice x1 -> x4, local copies, waits for them, and re-layouts: 1.81 us -> 4.31 us  [piece_of(): return lax.dynamic_slice_in_dim(array, (me ^ d) * points + start, size, 1)]
    ppermute x7 -> x9, starting transfers between devices: 12.4 us -> 14.7 us  [exchanged(): return lax.ppermute(piece, 'tm', xor_pairs(tm, d))]
    ppermute x7 -> x9, waiting for transfers between devices: 32.5 us -> 31 us  [exchanged(): return lax.ppermute(piece, 'tm', xor_pairs(tm, d))]
    pallas_call x5, Pallas kernels: 18.3 us -> 17.1 us  [call(): pl.pallas_call(body, out_shape=out_shape, in_specs=[smem] + [vmem] * (len...]
  transfers between devices with their start and end apart: 21 -> 23, of which waited for: 14 -> 16; matrix products, arithmetic and copies ran while one was open for 0% -> 4% of each run, Pallas kernels for 0% -> 0%
where the time goes in v2:
time: 93.9 us; the launch traced here: 93.6 us
  waiting for transfers between devices  42.9 us (46%)
  starting transfers between devices  26.9 us (29%)
  Pallas kernels  17.1 us (18%)
  local copies, waits for them, and re-layouts  5.9 us (6%)
    ppermute x9, waiting for transfers between devices, exchanged(): return lax.ppermute(piece, 'tm', xor_pairs(tm, d))  31 us
    pallas_call x5, Pallas kernels, call(): pl.pallas_call(body, out_shape=out_shape, in_specs=[smem] + [vmem] * (len...  17.1 us
    ppermute x9, starting transfers between devices, exchanged(): return lax.ppermute(piece, 'tm', xor_pairs(tm, d))  14.7 us
    ppermute x3, starting transfers between devices, factor_over_devices(): lax.ppermute(total, 'tm', xor_pairs(tm, d))  4.45 us
    ppermute x3, waiting for transfers between devices, factor_over_devices(): lax.ppermute(parts[d], 'pts', xor_pairs(pts, d))  4.34 us
    dynamic_slice x4, local copies, waits for them, and re-layouts, piece_of(): return lax.dynamic_slice_in_dim(array, (me ^ d) * points + start, size, 1)  4.31 us
    ppermute x3, starting transfers between devices, factor_over_devices(): lax.ppermute(own, 'pts', xor_pairs(pts, d))  3.55 us
    ppermute x3, starting transfers between devices, factor_over_devices(): lax.ppermute(parts[d], 'pts', xor_pairs(pts, d))  3.55 us
  transfers between devices with their start and end apart: 23, of which 16 were waited for; matrix products, arithmetic and copies ran while one was open for 4% of the time, Pallas kernels for 0%

profile of v2, /device:TPU:0, one launch (start us, length us, event | category | flops | bytes accessed | tf_op | source)
XLA Modules:
  0.0 93.6 jit_solution(7805545025195494350)
XLA Ops:
  0.6 0.0 copy-start.1
  0.6 0.0 copy-start
  0.7 1.0 %constant_dynamic-slice_fusion.9 = f32[128,512]{1,0:T(8,128)S(1)} fusion(f32[128,4096]{1,0:T(8,128)} %param.3, s32[]{:T(128)S(6)} %select_n.30), kind=kLoop, calls=%fused_computation.9 | loop fusion | bytes 524292 | tf_op jit(solution)/shard_map/dynamic_slice | solution.py:410
  1.6 4.6 %collective-permute-start = (f32[128,512]{1,0:T(8,128)S(1)}, f32[128,512]{1,0:T(8,128)S(1)}, u32[]{:S(2)}, u32[]{:S(2)}) collective-permute-start(f32[128,512]{1,0:T(8,128)S(1)} %constant_dynamic-slice_fusion.9), channel_id=1, source_target_pairs={{0,28},{4,24},{8,20},{12,16},{16,12},{20,8},{24,4},{28,0},{1,29},{... | collective-permute-start | bytes 786440 | tf_op jit(solution)/shard_map/ppermute | solution.py:413
  6.2 1.0 %constant_dynamic-slice_fusion.6 = (f32[128,384]{1,0:T(8,128)S(1)}, f32[128,384]{1,0:T(8,128)S(1)}) fusion(f32[128,4096]{1,0:T(8,128)} %param.3, s32[]{:T(128)S(6)} %select_n.33, s32[]{:T(128)S(6)} %select_n.31), kind=kLoop, calls=%fused_computation.6 | loop fusion | bytes 786440 | tf_op jit(solution)/shard_map/dynamic_slice | solution.py:410
  7.2 0.1 collective-permute-start.3
  7.4 1.4 %constant_dynamic-slice_fusion.2 = (f32[128,512]{1,0:T(8,128)S(1)}, f32[128,512]{1,0:T(8,128)S(1)}, f32[128,512]{1,0:T(8,128)S(1)}, f32[128,512]{1,0:T(8,128)S(1)}, f32[128,512]{1,0:T(8,128)S(1)}) fusion(f32[128,4096]{1,0:T(8,128)} %param.3, s32[]{:T(128)S(6)} %select_n.37, s32[]{:T(128)S(6)} %select_n.36, s32[]{:T(128)S(6)} %select_n.35, s32[]{:T(128)S(6)} %select_n.34, ...), kind=kLoop, calls=%fused_computation.2 | loop fusion | bytes 2621460 | tf_op jit(solution)/shard_map/dynamic_slice | solution.py:410
  8.8 0.7 collective-permute-start.6
  9.5 1.6 %collective-permute-start.1 = (f32[128,384]{1,0:T(8,128)S(1)}, f32[128,384]{1,0:T(8,128)S(1)}, u32[]{:S(2)}, u32[]{:S(2)}) collective-permute-start(f32[128,384]{1,0:T(8,128)S(1)} %get-tuple-element.38), channel_id=1, source_target_pairs={{0,24},{4,28},{8,16},{12,20},{16,8},{20,12},{24,0},{28,4},{1,25},{... | collective-permute-start | bytes 589832 | tf_op jit(solution)/shard_map/ppermute | solution.py:413
  11.1 1.6 %collective-permute-start.5 = (f32[128,512]{1,0:T(8,128)S(1)}, f32[128,512]{1,0:T(8,128)S(1)}, u32[]{:S(2)}, u32[]{:S(2)}) collective-permute-start(f32[128,512]{1,0:T(8,128)S(1)} %get-tuple-element.34), channel_id=1, source_target_pairs={{0,8},{4,12},{8,0},{12,4},{16,24},{20,28},{24,16},{28,20},{1,9},{5... | collective-permute-start | bytes 786440 | tf_op jit(solution)/shard_map/ppermute | solution.py:413
  12.7 18.5 %collective-permute-done.3.refs_3_ = f32[128,384]{1,0:T(8,128)S(1)} collective-permute-done((f32[128,384]{1,0:T(8,128)S(1)}, f32[128,384]{1,0:T(8,128)S(1)}, u32[]{:S(2)}, u32[]{:S(2)}) %collective-permute-start.3) | collective-permute-done | bytes 196640 | tf_op jit(solution)/shard_map/ppermute | solution.py:413
  31.2 0.0 collective-permute-start.4
  31.2 0.0 collective-permute-done.refs_0_
  31.2 2.7 %collective-permute-start.2 = (f32[128,512]{1,0:T(8,128)S(1)}, f32[128,512]{1,0:T(8,128)S(1)}, u32[]{:S(2)}, u32[]{:S(2)}) collective-permute-start(f32[128,512]{1,0:T(8,128)S(1)} %get-tuple-element.36), channel_id=1, source_target_pairs={{0,20},{4,16},{8,28},{12,24},{16,4},{20,0},{24,12},{28,8},{1,21},{... | collective-permute-start | bytes 786440 | tf_op jit(solution)/shard_map/ppermute | solution.py:413
  33.8 0.0 copy-done.1
  33.8 0.9 constant_dynamic-slice_fusion
  34.7 0.0 collective-permute-done.1.refs_1_
  34.7 2.1 %collective-permute-start.7 = (f32[128,128]{1,0:T(8,128)S(1)}, f32[128,128]{1,0:T(8,128)S(1)}, u32[]{:S(2)}, u32[]{:S(2)}) collective-permute-start(f32[128,128]{1,0:T(8,128)S(1)} %get-tuple-element.17), channel_id=1, source_target_pairs={{0,16},{4,20},{8,24},{12,28},{16,0},{20,4},{24,8},{28,12},{1,17},{... | collective-permute-start | bytes 196616 | tf_op jit(solution)/shard_map/ppermute | solution.py:413
  36.8 0.0 collective-permute-done.6.refs_6_
  36.8 1.5 %collective-permute-start.8 = (f32[128,128]{1,0:T(8,128)S(1)}, f32[128,128]{1,0:T(8,128)S(1)}, u32[]{:S(2)}, u32[]{:S(2)}) collective-permute-start(f32[128,128]{1,0:T(8,128)S(1)} %get-tuple-element.18), channel_id=1, source_target_pairs={{0,24},{4,28},{8,16},{12,20},{16,8},{20,12},{24,0},{28,4},{1,25},{... | collective-permute-start | bytes 196616 | tf_op jit(solution)/shard_map/ppermute | solution.py:413
  38.3 0.1 pad_add_fusion.me_ref._
  38.4 0.0 collective-permute-done.5.refs_5_
  38.4 6.2 %collective-permute-done.4.refs_4_ = f32[128,512]{1,0:T(8,128)S(1)} collective-permute-done((f32[128,512]{1,0:T(8,128)S(1)}, f32[128,512]{1,0:T(8,128)S(1)}, u32[]{:S(2)}, u32[]{:S(2)}) %collective-permute-start.4) | collective-permute-done | bytes 262176 | tf_op jit(solution)/shard_map/ppermute | solution.py:413
  44.6 4.6 %collective-permute-done.2.refs_2_ = f32[128,512]{1,0:T(8,128)S(1)} collective-permute-done((f32[128,512]{1,0:T(8,128)S(1)}, f32[128,512]{1,0:T(8,128)S(1)}, u32[]{:S(2)}, u32[]{:S(2)}) %collective-permute-start.2) | collective-permute-done | bytes 262176 | tf_op jit(solution)/shard_map/ppermute | solution.py:413
  49.2 1.7 %collective-permute-done.7.refs_8_ = f32[128,128]{1,0:T(8,128)S(1)} collective-permute-done((f32[128,128]{1,0:T(8,128)S(1)}, f32[128,128]{1,0:T(8,128)S(1)}, u32[]{:S(2)}, u32[]{:S(2)}) %collective-permute-start.7) | collective-permute-done | bytes 65568 | tf_op jit(solution)/shard_map/ppermute | solution.py:413
  50.9 0.0 collective-permute-done.8.refs_9_
  50.9 0.0 copy-done
  50.9 6.9 %shard_map.50 = (f32[64,32,512]{2,1,0:T(8,128)S(1)}, f32[4,2,32,128]{3,2,1,0:T(8,128)S(1)}, f32[4,2,32,128]{3,2,1,0:T(8,128)S(1)}) custom-call(s32[2]{0:T(128)S(1)} %pad_add_fusion.me_ref._, f32[64,64]{1,0:T(8,128)S(1)} %copy-done, f32[1,512]{1,0:T(1,128)S(1)} %bitcast.8, f32[128,512]{1,0:T(8,128)S(1)} %collective-permute-done.refs_0_, ...), custom_call_target="tpu_custom_call" | custom-call | tf_op jit(solution)/shard_map/pallas_call | solution.py:368
  57.8 0.1 collective-permute-start.9
  57.9 1.3 %collective-permute-done.9.got_ref = f32[4,2,32,128]{3,2,1,0:T(8,128)S(1)} collective-permute-done((f32[4,2,32,128]{3,2,1,0:T(8,128)S(1)}, f32[4,2,32,128]{3,2,1,0:T(8,128)S(1)}, u32[]{:S(2)}, u32[]{:S(2)}) %collective-permute-start.9) | collective-permute-done | bytes 131104 | tf_op jit(solution)/shard_map/ppermute | solution.py:389
  59.2 0.6 shard_map.51
  59.8 1.6 %collective-permute-start.10 = (f32[2,32,128]{2,1,0:T(8,128)S(1)}, f32[2,32,128]{2,1,0:T(8,128)S(1)}, u32[]{:S(2)}, u32[]{:S(2)}) collective-permute-start(f32[2,32,128]{2,1,0:T(8,128)S(1)} %get-tuple-element.22), channel_id=1, source_target_pairs={{0,1},{1,0},{2,3},{3,2},{4,5},{5,4},{6,7},{7,6},{8,9},{9,8},{10,11... | collective-permute-start | bytes 98312 | tf_op jit(solution)/shard_map/ppermute | solution.py:391
  61.4 1.5 %collective-permute-start.11 = (f32[2,32,128]{2,1,0:T(8,128)S(1)}, f32[2,32,128]{2,1,0:T(8,128)S(1)}, u32[]{:S(2)}, u32[]{:S(2)}) collective-permute-start(f32[2,32,128]{2,1,0:T(8,128)S(1)} %get-tuple-element.23), channel_id=1, source_target_pairs={{0,2},{1,3},{2,0},{3,1},{4,6},{5,7},{6,4},{7,5},{8,10},{9,11},{10,... | collective-permute-start | bytes 98312 | tf_op jit(solution)/shard_map/ppermute | solution.py:391
  62.9 0.5 collective-permute-start.12
  63.4 0.4 collective-permute-done.10.refs_1_
  63.8 1.5 %collective-permute-done.11.refs_2_ = f32[2,32,128]{2,1,0:T(8,128)S(1)} collective-permute-done((f32[2,32,128]{2,1,0:T(8,128)S(1)}, f32[2,32,128]{2,1,0:T(8,128)S(1)}, u32[]{:S(2)}, u32[]{:S(2)}) %collective-permute-start.11) | collective-permute-done | bytes 32800 | tf_op jit(solution)/shard_map/ppermute | solution.py:391
  65.3 2.4 %collective-permute-done.12.refs_3_ = f32[2,32,128]{2,1,0:T(8,128)S(1)} collective-permute-done((f32[2,32,128]{2,1,0:T(8,128)S(1)}, f32[2,32,128]{2,1,0:T(8,128)S(1)}, u32[]{:S(2)}, u32[]{:S(2)}) %collective-permute-start.12) | collective-permute-done | bytes 32800 | tf_op jit(solution)/shard_map/ppermute | solution.py:391
  67.7 0.6 shard_map.52.refs_0_
  68.3 2.4 %collective-permute-start.15 = (f32[2,32,128]{2,1,0:T(8,128)S(1)}, f32[2,32,128]{2,1,0:T(8,128)S(1)}, u32[]{:S(2)}, u32[]{:S(2)}) collective-permute-start(f32[2,32,128]{2,1,0:T(8,128)S(1)} %shard_map.52.refs_0_), channel_id=1, source_target_pairs={{0,24},{4,28},{8,16},{12,20},{16,8},{20,12},{24,0},{28,4},{1,25},{... | collective-permute-start | bytes 98312 | tf_op jit(solution)/shard_map/ppermute | solution.py:397
  70.7 0.9 %collective-permute-start.14 = (f32[2,32,128]{2,1,0:T(8,128)S(1)}, f32[2,32,128]{2,1,0:T(8,128)S(1)}, u32[]{:S(2)}, u32[]{:S(2)}) collective-permute-start(f32[2,32,128]{2,1,0:T(8,128)S(1)} %shard_map.52.refs_0_), channel_id=1, source_target_pairs={{0,16},{4,20},{8,24},{12,28},{16,0},{20,4},{24,8},{28,12},{1,17},{... | collective-permute-start | bytes 98312 | tf_op jit(solution)/shard_map/ppermute | solution.py:397
  71.6 1.1 %collective-permute-start.13 = (f32[2,32,128]{2,1,0:T(8,128)S(1)}, f32[2,32,128]{2,1,0:T(8,128)S(1)}, u32[]{:S(2)}, u32[]{:S(2)}) collective-permute-start(f32[2,32,128]{2,1,0:T(8,128)S(1)} %shard_map.52.refs_0_), channel_id=1, source_target_pairs={{0,8},{4,12},{8,0},{12,4},{16,24},{20,28},{24,16},{28,20},{1,9},{5... | collective-permute-start | bytes 98312 | tf_op jit(solution)/shard_map/ppermute | solution.py:397
  72.7 1.5 %collective-permute-done.15.refs_3_ = f32[2,32,128]{2,1,0:T(8,128)S(1)} collective-permute-done((f32[2,32,128]{2,1,0:T(8,128)S(1)}, f32[2,32,128]{2,1,0:T(8,128)S(1)}, u32[]{:S(2)}, u32[]{:S(2)}) %collective-permute-start.15) | collective-permute-done | bytes 32800 | tf_op jit(solution)/shard_map/ppermute | solution.py:397
  74.2 1.3 %collective-permute-done.14.refs_2_ = f32[2,32,128]{2,1,0:T(8,128)S(1)} collective-permute-done((f32[2,32,128]{2,1,0:T(8,128)S(1)}, f32[2,32,128]{2,1,0:T(8,128)S(1)}, u32[]{:S(2)}, u32[]{:S(2)}) %collective-permute-start.14) | collective-permute-done | bytes 32800 | tf_op jit(solution)/shard_map/ppermute | solution.py:397
  75.5 0.3 collective-permute-done.13.refs_1_
  75.9 4.4 %shard_map.53.refs_0_ = f32[2,32,128]{2,1,0:T(8,128)S(1)} custom-call(s32[2]{0:T(128)S(1)} %pad_add_fusion.me_ref._, f32[2,32,128]{2,1,0:T(8,128)S(1)} %shard_map.52.refs_0_, f32[2,32,128]{2,1,0:T(8,128)S(1)} %collective-permute-done.13.refs_1_, f32[2,32,128]{2,1,0:T(8,128)S(1)} %collective-permute-done.14.refs_2_, ...), custom_call_target="tpu_custom_call" | custom-call | tf_op jit(solution)/shard_map/pallas_call | solution.py:368
  80.3 0.5 collective-permute-start.18
  80.9 1.5 %collective-permute-start.17 = (f32[2,32,128]{2,1,0:T(8,128)S(1)}, f32[2,32,128]{2,1,0:T(8,128)S(1)}, u32[]{:S(2)}, u32[]{:S(2)}) collective-permute-start(f32[2,32,128]{2,1,0:T(8,128)S(1)} %shard_map.53.refs_0_), channel_id=1, source_target_pairs={{0,2},{1,3},{2,0},{3,1},{4,6},{5,7},{6,4},{7,5},{8,10},{9,11},{10,... | collective-permute-start | bytes 98312 | tf_op jit(solution)/shard_map/ppermute | solution.py:399
  82.4 1.5 %collective-permute-start.16 = (f32[2,32,128]{2,1,0:T(8,128)S(1)}, f32[2,32,128]{2,1,0:T(8,128)S(1)}, u32[]{:S(2)}, u32[]{:S(2)}) collective-permute-start(f32[2,32,128]{2,1,0:T(8,128)S(1)} %shard_map.53.refs_0_), channel_id=1, source_target_pairs={{0,1},{1,0},{2,3},{3,2},{4,5},{5,4},{6,7},{7,6},{8,9},{9,8},{10,11... | collective-permute-start | bytes 98312 | tf_op jit(solution)/shard_map/ppermute | solution.py:399
  83.9 0.0 collective-permute-start.19
  83.9 1.3 %collective-permute-done.18.refs_3_ = f32[2,32,128]{2,1,0:T(8,128)S(1)} collective-permute-done((f32[2,32,128]{2,1,0:T(8,128)S(1)}, f32[2,32,128]{2,1,0:T(8,128)S(1)}, u32[]{:S(2)}, u32[]{:S(2)}) %collective-permute-start.18) | collective-permute-done | bytes 32800 | tf_op jit(solution)/shard_map/ppermute | solution.py:399
  85.2 0.0 collective-permute-start.22
  85.2 0.0 collective-permute-done.17.refs_2_
  85.2 0.5 collective-permute-start.21
  85.7 0.6 collective-permute-done.16.refs_1_
  86.3 0.0 collective-permute-start.20
  86.3 0.0 collective-permute-done.19.refs_4_
  86.3 0.1 collective-permute-done.22.refs_7_
  86.4 0.2 collective-permute-done.21.refs_6_
  86.6 0.9 %collective-permute-done.20.refs_5_ = f32[2,32,128]{2,1,0:T(8,128)S(1)} collective-permute-done((f32[2,32,128]{2,1,0:T(8,128)S(1)}, f32[2,32,128]{2,1,0:T(8,128)S(1)}, u32[]{:S(2)}, u32[]{:S(2)}) %collective-permute-start.20) | collective-permute-done | bytes 32800 | tf_op jit(solution)/shard_map/ppermute | solution.py:400
  87.5 4.6 %shard_map.54 = (f32[33,31,8,128]{3,2,1,0:T(8,128)}, f32[2,33,31,31]{3,2,1,0:T(8,128)S(1)}) custom-call(s32[2]{0:T(128)S(1)} %pad_add_fusion.me_ref._, f32[2,32,128]{2,1,0:T(8,128)S(1)} %shard_map.53.refs_0_, f32[2,32,128]{2,1,0:T(8,128)S(1)} %collective-permute-done.16.refs_1_, f32[2,32,128]{2,1,0:T(8,128)S(1)} %collective-permute-done.17.refs_2_, ...), custom_call_target="tpu_custom_call" | custom-call | tf_op jit(solution)/shard_map/pallas_call | solution.py:368
  92.1 1.6 %copy.6 = f32[2,33,31,31]{1,0,3,2:T(2,128)} copy(f32[2,33,31,31]{3,2,1,0:T(8,128)S(1)} %get-tuple-element.29) | data formatting | bytes 507408
  (1 shorter events, 0.0 us)
Async XLA Ops:
  0.6 33.2 %copy-start.1 = (f32[512]{0:T(512)S(1)}, f32[512]{0:T(512)}, u32[]{:S(2)}) copy-start(f32[512]{0:T(512)} %param.4) | copy-start | bytes 6148
  0.6 50.2 %copy-start = (f32[64,64]{1,0:T(8,128)S(1)}, f32[64,64]{1,0:T(8,128)}, u32[]{:S(2)}) copy-start(f32[64,64]{1,0:T(8,128)} %constant.36.clone.table_ref) | copy-start | bytes 49156
  1.6 29.5 %collective-permute-start = (f32[128,512]{1,0:T(8,128)S(1)}, f32[128,512]{1,0:T(8,128)S(1)}, u32[]{:S(2)}, u32[]{:S(2)}) collective-permute-start(f32[128,512]{1,0:T(8,128)S(1)} %constant_dynamic-slice_fusion.9), channel_id=1, source_target_pairs={{0,28},{4,24},{8,20},{12,16},{16,12},{20,8},{24,4},{28,0},{1,29},{... | collective-permute-start | bytes 786440 | tf_op jit(solution)/shard_map/ppermute | solution.py:413
  7.2 23.9 %collective-permute-start.3 = (f32[128,384]{1,0:T(8,128)S(1)}, f32[128,384]{1,0:T(8,128)S(1)}, u32[]{:S(2)}, u32[]{:S(2)}) collective-permute-start(f32[128,384]{1,0:T(8,128)S(1)} %get-tuple-element.37), channel_id=1, source_target_pairs={{0,16},{4,20},{8,24},{12,28},{16,0},{20,4},{24,8},{28,12},{1,17},{... | collective-permute-start | bytes 589832 | tf_op jit(solution)/shard_map/ppermute | solution.py:413
  8.8 28.1 %collective-permute-start.6 = (f32[128,512]{1,0:T(8,128)S(1)}, f32[128,512]{1,0:T(8,128)S(1)}, u32[]{:S(2)}, u32[]{:S(2)}) collective-permute-start(f32[128,512]{1,0:T(8,128)S(1)} %get-tuple-element.33), channel_id=1, source_target_pairs={{0,4},{4,0},{8,12},{12,8},{16,20},{20,16},{24,28},{28,24},{1,5},{5... | collective-permute-start | bytes 786440 | tf_op jit(solution)/shard_map/ppermute | solution.py:413
  9.5 25.2 %collective-permute-start.1 = (f32[128,384]{1,0:T(8,128)S(1)}, f32[128,384]{1,0:T(8,128)S(1)}, u32[]{:S(2)}, u32[]{:S(2)}) collective-permute-start(f32[128,384]{1,0:T(8,128)S(1)} %get-tuple-element.38), channel_id=1, source_target_pairs={{0,24},{4,28},{8,16},{12,20},{16,8},{20,12},{24,0},{28,4},{1,25},{... | collective-permute-start | bytes 589832 | tf_op jit(solution)/shard_map/ppermute | solution.py:413
  11.1 27.3 %collective-permute-start.5 = (f32[128,512]{1,0:T(8,128)S(1)}, f32[128,512]{1,0:T(8,128)S(1)}, u32[]{:S(2)}, u32[]{:S(2)}) collective-permute-start(f32[128,512]{1,0:T(8,128)S(1)} %get-tuple-element.34), channel_id=1, source_target_pairs={{0,8},{4,12},{8,0},{12,4},{16,24},{20,28},{24,16},{28,20},{1,9},{5... | collective-permute-start | bytes 786440 | tf_op jit(solution)/shard_map/ppermute | solution.py:413
  31.2 13.5 %collective-permute-start.4 = (f32[128,512]{1,0:T(8,128)S(1)}, f32[128,512]{1,0:T(8,128)S(1)}, u32[]{:S(2)}, u32[]{:S(2)}) collective-permute-start(f32[128,512]{1,0:T(8,128)S(1)} %get-tuple-element.35), channel_id=1, source_target_pairs={{0,12},{4,8},{8,4},{12,0},{16,28},{20,24},{24,20},{28,16},{1,13},{... | collective-permute-start | bytes 786440 | tf_op jit(solution)/shard_map/ppermute | solution.py:413
  31.2 18.0 %collective-permute-start.2 = (f32[128,512]{1,0:T(8,128)S(1)}, f32[128,512]{1,0:T(8,128)S(1)}, u32[]{:S(2)}, u32[]{:S(2)}) collective-permute-start(f32[128,512]{1,0:T(8,128)S(1)} %get-tuple-element.36), channel_id=1, source_target_pairs={{0,20},{4,16},{8,28},{12,24},{16,4},{20,0},{24,12},{28,8},{1,21},{... | collective-permute-start | bytes 786440 | tf_op jit(solution)/shard_map/ppermute | solution.py:413
  34.7 16.1 %collective-permute-start.7 = (f32[128,128]{1,0:T(8,128)S(1)}, f32[128,128]{1,0:T(8,128)S(1)}, u32[]{:S(2)}, u32[]{:S(2)}) collective-permute-start(f32[128,128]{1,0:T(8,128)S(1)} %get-tuple-element.17), channel_id=1, source_target_pairs={{0,16},{4,20},{8,24},{12,28},{16,0},{20,4},{24,8},{28,12},{1,17},{... | collective-permute-start | bytes 196616 | tf_op jit(solution)/shard_map/ppermute | solution.py:413
  36.8 14.0 %collective-permute-start.8 = (f32[128,128]{1,0:T(8,128)S(1)}, f32[128,128]{1,0:T(8,128)S(1)}, u32[]{:S(2)}, u32[]{:S(2)}) collective-permute-start(f32[128,128]{1,0:T(8,128)S(1)} %get-tuple-element.18), channel_id=1, source_target_pairs={{0,24},{4,28},{8,16},{12,20},{16,8},{20,12},{24,0},{28,4},{1,25},{... | collective-permute-start | bytes 196616 | tf_op jit(solution)/shard_map/ppermute | solution.py:413
  57.8 1.4 %collective-permute-start.9 = (f32[4,2,32,128]{3,2,1,0:T(8,128)S(1)}, f32[4,2,32,128]{3,2,1,0:T(8,128)S(1)}, u32[]{:S(2)}, u32[]{:S(2)}) collective-permute-start(f32[4,2,32,128]{3,2,1,0:T(8,128)S(1)} %get-tuple-element.20), channel_id=1, source_target_pairs={{0,4},{4,0},{8,12},{12,8},{16,20},{20,16},{24,28},{28,24},{1,5},{5... | collective-permute-start | bytes 393224 | tf_op jit(solution)/shard_map/ppermute | solution.py:389
  59.8 4.0 %collective-permute-start.10 = (f32[2,32,128]{2,1,0:T(8,128)S(1)}, f32[2,32,128]{2,1,0:T(8,128)S(1)}, u32[]{:S(2)}, u32[]{:S(2)}) collective-permute-start(f32[2,32,128]{2,1,0:T(8,128)S(1)} %get-tuple-element.22), channel_id=1, source_target_pairs={{0,1},{1,0},{2,3},{3,2},{4,5},{5,4},{6,7},{7,6},{8,9},{9,8},{10,11... | collective-permute-start | bytes 98312 | tf_op jit(solution)/shard_map/ppermute | solution.py:391
  61.4 3.9 %collective-permute-start.11 = (f32[2,32,128]{2,1,0:T(8,128)S(1)}, f32[2,32,128]{2,1,0:T(8,128)S(1)}, u32[]{:S(2)}, u32[]{:S(2)}) collective-permute-start(f32[2,32,128]{2,1,0:T(8,128)S(1)} %get-tuple-element.23), channel_id=1, source_target_pairs={{0,2},{1,3},{2,0},{3,1},{4,6},{5,7},{6,4},{7,5},{8,10},{9,11},{10,... | collective-permute-start | bytes 98312 | tf_op jit(solution)/shard_map/ppermute | solution.py:391
  62.9 4.8 %collective-permute-start.12 = (f32[2,32,128]{2,1,0:T(8,128)S(1)}, f32[2,32,128]{2,1,0:T(8,128)S(1)}, u32[]{:S(2)}, u32[]{:S(2)}) collective-permute-start(f32[2,32,128]{2,1,0:T(8,128)S(1)} %get-tuple-element.24), channel_id=1, source_target_pairs={{0,3},{1,2},{2,1},{3,0},{4,7},{5,6},{6,5},{7,4},{8,11},{9,10},{10,... | collective-permute-start | bytes 98312 | tf_op jit(solution)/shard_map/ppermute | solution.py:391
  68.3 6.0 %collective-permute-start.15 = (f32[2,32,128]{2,1,0:T(8,128)S(1)}, f32[2,32,128]{2,1,0:T(8,128)S(1)}, u32[]{:S(2)}, u32[]{:S(2)}) collective-permute-start(f32[2,32,128]{2,1,0:T(8,128)S(1)} %shard_map.52.refs_0_), channel_id=1, source_target_pairs={{0,24},{4,28},{8,16},{12,20},{16,8},{20,12},{24,0},{28,4},{1,25},{... | collective-permute-start | bytes 98312 | tf_op jit(solution)/shard_map/ppermute | solution.py:397
  70.7 4.8 %collective-permute-start.14 = (f32[2,32,128]{2,1,0:T(8,128)S(1)}, f32[2,32,128]{2,1,0:T(8,128)S(1)}, u32[]{:S(2)}, u32[]{:S(2)}) collective-permute-start(f32[2,32,128]{2,1,0:T(8,128)S(1)} %shard_map.52.refs_0_), channel_id=1, source_target_pairs={{0,16},{4,20},{8,24},{12,28},{16,0},{20,4},{24,8},{28,12},{1,17},{... | collective-permute-start | bytes 98312 | tf_op jit(solution)/shard_map/ppermute | solution.py:397
  71.6 4.2 %collective-permute-start.13 = (f32[2,32,128]{2,1,0:T(8,128)S(1)}, f32[2,32,128]{2,1,0:T(8,128)S(1)}, u32[]{:S(2)}, u32[]{:S(2)}) collective-permute-start(f32[2,32,128]{2,1,0:T(8,128)S(1)} %shard_map.52.refs_0_), channel_id=1, source_target_pairs={{0,8},{4,12},{8,0},{12,4},{16,24},{20,28},{24,16},{28,20},{1,9},{5... | collective-permute-start | bytes 98312 | tf_op jit(solution)/shard_map/ppermute | solution.py:397
  80.3 4.9 %collective-permute-start.18 = (f32[2,32,128]{2,1,0:T(8,128)S(1)}, f32[2,32,128]{2,1,0:T(8,128)S(1)}, u32[]{:S(2)}, u32[]{:S(2)}) collective-permute-start(f32[2,32,128]{2,1,0:T(8,128)S(1)} %shard_map.53.refs_0_), channel_id=1, source_target_pairs={{0,3},{1,2},{2,1},{3,0},{4,7},{5,6},{6,5},{7,4},{8,11},{9,10},{10,... | collective-permute-start | bytes 98312 | tf_op jit(solution)/shard_map/ppermute | solution.py:399
  80.9 4.3 %collective-permute-start.17 = (f32[2,32,128]{2,1,0:T(8,128)S(1)}, f32[2,32,128]{2,1,0:T(8,128)S(1)}, u32[]{:S(2)}, u32[]{:S(2)}) collective-permute-start(f32[2,32,128]{2,1,0:T(8,128)S(1)} %shard_map.53.refs_0_), channel_id=1, source_target_pairs={{0,2},{1,3},{2,0},{3,1},{4,6},{5,7},{6,4},{7,5},{8,10},{9,11},{10,... | collective-permute-start | bytes 98312 | tf_op jit(solution)/shard_map/ppermute | solution.py:399
  82.4 3.9 %collective-permute-start.16 = (f32[2,32,128]{2,1,0:T(8,128)S(1)}, f32[2,32,128]{2,1,0:T(8,128)S(1)}, u32[]{:S(2)}, u32[]{:S(2)}) collective-permute-start(f32[2,32,128]{2,1,0:T(8,128)S(1)} %shard_map.53.refs_0_), channel_id=1, source_target_pairs={{0,1},{1,0},{2,3},{3,2},{4,5},{5,4},{6,7},{7,6},{8,9},{9,8},{10,11... | collective-permute-start | bytes 98312 | tf_op jit(solution)/shard_map/ppermute | solution.py:399
  83.9 2.4 %collective-permute-start.19 = (f32[2,32,128]{2,1,0:T(8,128)S(1)}, f32[2,32,128]{2,1,0:T(8,128)S(1)}, u32[]{:S(2)}, u32[]{:S(2)}) collective-permute-start(f32[2,32,128]{2,1,0:T(8,128)S(1)} %shard_map.53.refs_0_), channel_id=1, source_target_pairs={{0,4},{4,0},{8,12},{12,8},{16,20},{20,16},{24,28},{28,24},{1,5},{5... | collective-permute-start | bytes 98312 | tf_op jit(solution)/shard_map/ppermute | solution.py:400
  85.2 1.2 %collective-permute-start.22 = (f32[2,32,128]{2,1,0:T(8,128)S(1)}, f32[2,32,128]{2,1,0:T(8,128)S(1)}, u32[]{:S(2)}, u32[]{:S(2)}) collective-permute-start(f32[2,32,128]{2,1,0:T(8,128)S(1)} %collective-permute-done.18.refs_3_), channel_id=1, source_target_pairs={{0,4},{4,0},{8,12},{12,8},{16,20},{20,16},{24,28},{28,24},{1,5},{5... | collective-permute-start | bytes 98312 | tf_op jit(solution)/shard_map/ppermute | solution.py:400
  85.2 1.4 %collective-permute-start.21 = (f32[2,32,128]{2,1,0:T(8,128)S(1)}, f32[2,32,128]{2,1,0:T(8,128)S(1)}, u32[]{:S(2)}, u32[]{:S(2)}) collective-permute-start(f32[2,32,128]{2,1,0:T(8,128)S(1)} %collective-permute-done.17.refs_2_), channel_id=1, source_target_pairs={{0,4},{4,0},{8,12},{12,8},{16,20},{20,16},{24,28},{28,24},{1,5},{5... | collective-permute-start | bytes 98312 | tf_op jit(solution)/shard_map/ppermute | solution.py:400
  86.3 1.2 %collective-permute-start.20 = (f32[2,32,128]{2,1,0:T(8,128)S(1)}, f32[2,32,128]{2,1,0:T(8,128)S(1)}, u32[]{:S(2)}, u32[]{:S(2)}) collective-permute-start(f32[2,32,128]{2,1,0:T(8,128)S(1)} %collective-permute-done.16.refs_1_), channel_id=1, source_target_pairs={{0,4},{4,0},{8,12},{12,8},{16,20},{20,16},{24,28},{28,24},{1,5},{5... | collective-permute-start | bytes 98312 | tf_op jit(solution)/shard_map/ppermute | solution.py:400

commit v3 on v2

--- a/solution.py
+++ b/solution.py
@@ -136,47 +136,52 @@
     return total, low - (total - high)
 
 
-def spectrum_kernel(me_ref, table_ref, root_ref, *refs, places):
-    pieces, (spec_ref, keep_ref, send_ref, records_ref) = refs[:len(places)], refs[len(places):]
-    for (d, first), piece in zip(places, pieces):
-        rows, size = piece.shape
-        start = pl.multiple_of((me_ref[0] ^ d) * rows, rows)
-        at = slice(first, first + size)
-        records_ref[pl.ds(start, rows), at] = piece[...] * root_ref[:, at]
-    spectrum_body(table_ref[...], records_ref[...], spec_ref)
-    core = me_ref[0] & 1
+def gram_half(spec_ref, out_ref, side):
     row = lax.broadcasted_iota(jnp.int32, (32, 32), 0)
     column = lax.broadcasted_iota(jnp.int32, (32, 32), 1)
-    order = [(j, q, s) for j in (1, 0) for q in range(SIDE) for s in range(4)]
 
     def products_of(step):
-        j, q, s = order[step]
-        slot = ((core ^ j) * SIDE + q) * 4 + s
+        slot = side * SIDE * 4 + step
         return gram_products(spec_ref[slot], spec_ref[SLOTS + slot])
 
     ahead = products_of(0)
-    for step, (j, q, s) in enumerate(order):
+    for step in range(4 * SIDE):
         products = ahead
-        if step + 1 < len(order):
+        if step + 1 < 4 * SIDE:
             ahead = products_of(step + 1)
-        special = q == 0 and s == 0
+        q, s = divmod(step, 4)
         if s == 0:
             packed = [[], []]
-        sums = gram_pairs(products, (core ^ j) == 0 if special else None)
+        sums = gram_pairs(products, side == 0 if step == 0 else None)
         for part in range(2):
             real, imag = sums[part][:, :32], sums[part][:, 32:]
             square = jnp.where(column >= row, real, imag)
-            if special:
+            if step == 0:
                 diagonal = jnp.sum(jnp.where(column == row, imag, 0.0), axis=0, keepdims=True)
                 square = jnp.where(row == NB, diagonal, square)
             packed[part].append(square)
             if s == 3:
-                (keep_ref, send_ref)[j][q, part] = jnp.concatenate(packed[part], axis=1)
-
-
-def core_sum_kernel(me_ref, keep_ref, got_ref, *out_refs):
+                out_ref[q, part] = jnp.concatenate(packed[part], axis=1)
+
+
+def spectrum_kernel(table_ref, root_ref, *refs, places):
+    pieces, (spec_ref, send_ref, records_ref) = refs[:len(places)], refs[len(places):]
+    for (d, first), piece in zip(places, pieces):
+        rows, size = piece.shape
+        start = pl.multiple_of((lax.axis_index("tm") ^ d) * rows, rows)
+        at = slice(first, first + size)
+        records_ref[pl.ds(start, rows), at] = piece[...] * root_ref[:, at]
+    spectrum_body(table_ref[...], records_ref[...], spec_ref)
+    gram_half(spec_ref, send_ref, (lax.axis_index("tm") & 1) ^ 1)
+
+
+def keep_kernel(spec_ref, keep_ref):
+    gram_half(spec_ref, keep_ref, lax.axis_index("tm") & 1)
+
+
+def core_sum_kernel(keep_ref, got_ref, *out_refs):
     for d in range(SIDE):
-        q = (me_ref[1] & (SIDE - 1)) ^ d
+        q = (lax.axis_index("pts") & (SIDE - 1)) ^ d
         high, low = pair_add((keep_ref[q, 0], keep_ref[q, 1]), (got_ref[q, 0], got_ref[q, 1]))
         out_refs[d][0] = high
         out_refs[d][1] = low
@@ -193,14 +198,14 @@
     return jnp.concatenate([turned[32 * s:32 * s + 32] for s in range(4)], axis=1)
 
 
-def factor_kernel(me_ref, *refs, scale):
+def factor_kernel(*refs, scale):
     out_ref = refs[-1]
     high, low = pair_tree([(ref[0], ref[1]) for ref in refs[:-1]])
     shape = (32, 128)
     row = lax.broadcasted_iota(jnp.int32, shape, 0)
     lane = lax.broadcasted_iota(jnp.int32, shape, 1)
     column = lane % 32
-    first = jnp.logical_and((me_ref[0] & 1) == 0, (me_ref[1] & (SIDE - 1)) == 0)
+    first = jnp.logical_and((lax.axis_index("tm") & 1) == 0, (lax.axis_index("pts") & (SIDE - 1)) == 0)
     two_real = jnp.logical_and(lane < 32, first)
     sign = jnp.where(two_real, 1.0, -1.0)
     real, imag = [], []
@@ -286,7 +291,7 @@
         out_ref[1, at] = jnp.where(good, imag[i][0] / jnp.sqrt(pivot_imag), 0.0)
 
 
-def apply_kernel(me_ref, *refs):
+def apply_kernel(*refs):
     pieces, (spec_ref, modes_ref, triangle_ref, tiles_ref, sent) = refs[:GROUPS], refs[GROUPS:]
     points = spec_ref.shape[-1]
     shape = (32, 128)
@@ -315,7 +320,7 @@
     for c in range(2):
         for d in range(SIDE):
             piece = pieces[SIDE * c + d]
-            group = ((me_ref[0] & 1) ^ c) * SIDE + ((me_ref[1] & (SIDE - 1)) ^ d)
+            group = ((lax.axis_index("tm") & 1) ^ c) * SIDE + ((lax.axis_index("pts") & (SIDE - 1)) ^ d)
             is_first = group == 0
             both_real, both_imag = piece[0], piece[1]
             upper_real = jnp.where(column >= row, both_real, 0.0)
@@ -363,12 +368,11 @@
 
 
 def call(body, out_shape, scratch, operands, out_spaces=None):
-    smem = pl.BlockSpec(memory_space=pltpu.SMEM)
     vmem = pl.BlockSpec(memory_space=pltpu.VMEM)
     return pl.pallas_call(
         body,
         out_shape=out_shape,
-        in_specs=[smem] + [vmem] * (len(operands) - 1),
+        in_specs=[vmem] * len(operands),
         out_specs=[pl.BlockSpec(memory_space=space) for space in out_spaces] if out_spaces else jax.tree.map(lambda _: vmem, out_shape),
         scratch_shapes=scratch,
         compiler_params=pltpu.CompilerParams(vmem_limit_bytes=VMEM_BYTES),
@@ -383,19 +387,18 @@
     return [(i, i ^ difference) for i in range(size)]
 
 
-def factor_over_devices(place, keep, send, scale):
+def factor_over_devices(keep, got, scale):
     tm, pts = lax.axis_size("tm"), lax.axis_size("pts")
     part = f32(2, 32, 128)
-    got = lax.ppermute(send, "tm", xor_pairs(tm, 1))
-    parts = call(core_sum_kernel, (part,) * SIDE, [], [place, keep, got])
+    parts = call(core_sum_kernel, (part,) * SIDE, [], [keep, got])
     parts = [lax.ppermute(parts[d], "pts", xor_pairs(pts, d)) for d in reversed(range(1, SIDE))] + [parts[0]]
     parts = parts[::-1]
-    total = call(lambda _, *refs: pair_sum_kernel(*refs), part, [], [place] + parts)
+    total = call(pair_sum_kernel, part, [], parts)
     if pts > SIDE:
         parts = [total] + [lax.ppermute(total, "pts", xor_pairs(pts, d)) for d in range(SIDE, pts, SIDE)]
-        total = call(lambda _, *refs: pair_sum_kernel(*refs), part, [], [place] + parts)
+        total = call(pair_sum_kernel, part, [], parts)
     parts = [total] + [lax.ppermute(total, "tm", xor_pairs(tm, d)) for d in range(2, tm, 2)]
-    own = call(functools.partial(factor_kernel, scale=scale), part, [], [place] + parts)
+    own = call(functools.partial(factor_kernel, scale=scale), part, [], parts)
     own = [own] + [lax.ppermute(own, "pts", xor_pairs(pts, d)) for d in range(1, SIDE)]
     return own + [lax.ppermute(piece, "tm", xor_pairs(tm, 1)) for piece in own]
 
@@ -430,21 +433,22 @@
         pieces[d, body] = exchanged(sent, d)
     root = jnp.sqrt(weights)[None, :]
     table_t = jnp.asarray(fourier_table().T)
-    place = jnp.stack([me, lax.axis_index("pts")]).astype(jnp.int32)
     half = f32(SIDE, 2, 32, 128)
-    spec, keep, send = call(
+    spec, send = call(
         functools.partial(spectrum_kernel, places=tuple(pieces)),
-        (f32(SEG, 32, points), half, half),
+        (f32(SEG, 32, points), half),
         [pltpu.VMEM((NT, points), jnp.float32)],
-        [place, table_t, root, *pieces.values()],
+        [table_t, root, *pieces.values()],
     )
-    factors = factor_over_devices(place, keep, send, scale)
+    got = lax.ppermute(send, "tm", xor_pairs(tm, 1))
+    keep = call(keep_kernel, half, [], [spec])
+    factors = factor_over_devices(keep, got, scale)
     tiles = points // 128
     modes, triangle = call(
         apply_kernel,
         (f32(NF, NB, tiles * 2, 128), f32(2, NF, NB, NB)),
         [pltpu.VMEM((NF, NB, tiles * 2, 128), jnp.float32), pltpu.SemaphoreType.DMA((NF,))],
-        [place] + factors + [spec],
+        factors + [spec],
         [pl.ANY, pltpu.VMEM],
     )
     modes = modes.reshape(NF, NB, tiles, 2, 128).transpose(3, 0, 1, 2, 4).reshape(2, NF, NB, points)

time: 93.9 us -> 90.2 us (0.961)
  Pallas kernels: 17.1 us -> 14.6 us
  waiting for transfers between devices: 42.9 us -> 41.7 us
    pallas_call x5 -> x6, Pallas kernels: 17.1 us -> 14.6 us  [call(): pl.pallas_call(body, out_shape=out_shape, in_specs=[vmem] * len(operands)...]
    ppermute x1, waiting for transfers between devices: 1.33 us -> 0.01 us  [shards(): got = lax.ppermute(send, 'tm', xor_pairs(tm, 1))]
  transfers between devices with their start and end apart: 23 -> 23, of which waited for: 16 -> 15; matrix products, arithmetic and copies ran while one was open for 4% -> 4% of each run, Pallas kernels for 0% -> 3%
where the time goes in v3:
time: 90.2 us; the launch traced here: 89.9 us
  waiting for transfers between devices  41.7 us (46%)
  starting transfers between devices  26.9 us (30%)
  Pallas kernels  14.6 us (16%)
  local copies, waits for them, and re-layouts  5.88 us (7%)
    ppermute x9, waiting for transfers between devices, exchanged(): return lax.ppermute(piece, 'tm', xor_pairs(tm, d))  31.1 us
    ppermute x9, starting transfers between devices, exchanged(): return lax.ppermute(piece, 'tm', xor_pairs(tm, d))  14.8 us
    pallas_call x6, Pallas kernels, call(): pl.pallas_call(body, out_shape=out_shape, in_specs=[vmem] * len(operands)...  14.6 us
    ppermute x3, starting transfers between devices, factor_over_devices(): lax.ppermute(total, 'tm', xor_pairs(tm, d))  4.45 us
    ppermute x3, waiting for transfers between devices, factor_over_devices(): lax.ppermute(parts[d], 'pts', xor_pairs(pts, d))  4.34 us
    dynamic_slice x4, local copies, waits for them, and re-layouts, piece_of(): return lax.dynamic_slice_in_dim(array, (me ^ d) * points + start, size, 1)  4.29 us
    ppermute x3, starting transfers between devices, factor_over_devices(): lax.ppermute(own, 'pts', xor_pairs(pts, d))  3.55 us
    ppermute x3, starting transfers between devices, factor_over_devices(): lax.ppermute(parts[d], 'pts', xor_pairs(pts, d))  3.55 us
  transfers between devices with their start and end apart: 23, of which 15 were waited for; matrix products, arithmetic and copies ran while one was open for 4% of the time, Pallas kernels for 3%

profile of v3, /device:TPU:0, one launch (start us, length us, event | category | flops | bytes accessed | tf_op | source)
XLA Modules:
  0.0 89.9 jit_solution(16134182576149881610)
XLA Ops:
  0.6 0.0 copy-start.1
  0.6 0.0 copy-start
  0.7 1.0 %constant_dynamic-slice_fusion.9 = f32[128,512]{1,0:T(8,128)S(1)} fusion(f32[128,4096]{1,0:T(8,128)} %param.3, s32[]{:T(128)S(6)} %select_n.30), kind=kLoop, calls=%fused_computation.9 | loop fusion | bytes 524292 | tf_op jit(solution)/shard_map/dynamic_slice | solution.py:413
  1.6 4.6 %collective-permute-start = (f32[128,512]{1,0:T(8,128)S(1)}, f32[128,512]{1,0:T(8,128)S(1)}, u32[]{:S(2)}, u32[]{:S(2)}) collective-permute-start(f32[128,512]{1,0:T(8,128)S(1)} %constant_dynamic-slice_fusion.9), channel_id=1, source_target_pairs={{0,28},{4,24},{8,20},{12,16},{16,12},{20,8},{24,4},{28,0},{1,29},{... | collective-permute-start | bytes 786440 | tf_op jit(solution)/shard_map/ppermute | solution.py:416
  6.2 1.0 %constant_dynamic-slice_fusion.6 = (f32[128,384]{1,0:T(8,128)S(1)}, f32[128,384]{1,0:T(8,128)S(1)}) fusion(f32[128,4096]{1,0:T(8,128)} %param.3, s32[]{:T(128)S(6)} %select_n.33, s32[]{:T(128)S(6)} %select_n.31), kind=kLoop, calls=%fused_computation.6 | loop fusion | bytes 786440 | tf_op jit(solution)/shard_map/dynamic_slice | solution.py:413
  7.2 0.1 collective-permute-start.3
  7.4 1.4 %constant_dynamic-slice_fusion.2 = (f32[128,512]{1,0:T(8,128)S(1)}, f32[128,512]{1,0:T(8,128)S(1)}, f32[128,512]{1,0:T(8,128)S(1)}, f32[128,512]{1,0:T(8,128)S(1)}, f32[128,512]{1,0:T(8,128)S(1)}) fusion(f32[128,4096]{1,0:T(8,128)} %param.3, s32[]{:T(128)S(6)} %select_n.37, s32[]{:T(128)S(6)} %select_n.36, s32[]{:T(128)S(6)} %select_n.35, s32[]{:T(128)S(6)} %select_n.34, ...), kind=kLoop, calls=%fused_computation.2 | loop fusion | bytes 2621460 | tf_op jit(solution)/shard_map/dynamic_slice | solution.py:413
  8.7 0.7 collective-permute-start.6
  9.5 1.6 %collective-permute-start.1 = (f32[128,384]{1,0:T(8,128)S(1)}, f32[128,384]{1,0:T(8,128)S(1)}, u32[]{:S(2)}, u32[]{:S(2)}) collective-permute-start(f32[128,384]{1,0:T(8,128)S(1)} %get-tuple-element.36), channel_id=1, source_target_pairs={{0,24},{4,28},{8,16},{12,20},{16,8},{20,12},{24,0},{28,4},{1,25},{... | collective-permute-start | bytes 589832 | tf_op jit(solution)/shard_map/ppermute | solution.py:416
  11.1 1.6 %collective-permute-start.5 = (f32[128,512]{1,0:T(8,128)S(1)}, f32[128,512]{1,0:T(8,128)S(1)}, u32[]{:S(2)}, u32[]{:S(2)}) collective-permute-start(f32[128,512]{1,0:T(8,128)S(1)} %get-tuple-element.32), channel_id=1, source_target_pairs={{0,8},{4,12},{8,0},{12,4},{16,24},{20,28},{24,16},{28,20},{1,9},{5... | collective-permute-start | bytes 786440 | tf_op jit(solution)/shard_map/ppermute | solution.py:416
  12.6 18.5 %collective-permute-done.3.refs_3_ = f32[128,384]{1,0:T(8,128)S(1)} collective-permute-done((f32[128,384]{1,0:T(8,128)S(1)}, f32[128,384]{1,0:T(8,128)S(1)}, u32[]{:S(2)}, u32[]{:S(2)}) %collective-permute-start.3) | collective-permute-done | bytes 196640 | tf_op jit(solution)/shard_map/ppermute | solution.py:416
  31.2 0.0 collective-permute-start.4
  31.2 0.0 collective-permute-done.refs_0_
  31.2 2.7 %collective-permute-start.2 = (f32[128,512]{1,0:T(8,128)S(1)}, f32[128,512]{1,0:T(8,128)S(1)}, u32[]{:S(2)}, u32[]{:S(2)}) collective-permute-start(f32[128,512]{1,0:T(8,128)S(1)} %get-tuple-element.34), channel_id=1, source_target_pairs={{0,20},{4,16},{8,28},{12,24},{16,4},{20,0},{24,12},{28,8},{1,21},{... | collective-permute-start | bytes 786440 | tf_op jit(solution)/shard_map/ppermute | solution.py:416
  33.8 0.9 constant_dynamic-slice_fusion
  34.7 0.0 collective-permute-done.1.refs_1_
  34.7 2.1 %collective-permute-start.7 = (f32[128,128]{1,0:T(8,128)S(1)}, f32[128,128]{1,0:T(8,128)S(1)}, u32[]{:S(2)}, u32[]{:S(2)}) collective-permute-start(f32[128,128]{1,0:T(8,128)S(1)} %get-tuple-element.16), channel_id=1, source_target_pairs={{0,16},{4,20},{8,24},{12,28},{16,0},{20,4},{24,8},{28,12},{1,17},{... | collective-permute-start | bytes 196616 | tf_op jit(solution)/shard_map/ppermute | solution.py:416
  36.8 0.0 collective-permute-done.6.refs_6_
  36.8 1.5 %collective-permute-start.8 = (f32[128,128]{1,0:T(8,128)S(1)}, f32[128,128]{1,0:T(8,128)S(1)}, u32[]{:S(2)}, u32[]{:S(2)}) collective-permute-start(f32[128,128]{1,0:T(8,128)S(1)} %get-tuple-element.17), channel_id=1, source_target_pairs={{0,24},{4,28},{8,16},{12,20},{16,8},{20,12},{24,0},{28,4},{1,25},{... | collective-permute-start | bytes 196616 | tf_op jit(solution)/shard_map/ppermute | solution.py:416
  38.3 0.0 copy-done.1
  38.3 0.0 collective-permute-done.5.refs_5_
  38.3 6.3 %collective-permute-done.4.refs_4_ = f32[128,512]{1,0:T(8,128)S(1)} collective-permute-done((f32[128,512]{1,0:T(8,128)S(1)}, f32[128,512]{1,0:T(8,128)S(1)}, u32[]{:S(2)}, u32[]{:S(2)}) %collective-permute-start.4) | collective-permute-done | bytes 262176 | tf_op jit(solution)/shard_map/ppermute | solution.py:416
  44.6 4.6 %collective-permute-done.2.refs_2_ = f32[128,512]{1,0:T(8,128)S(1)} collective-permute-done((f32[128,512]{1,0:T(8,128)S(1)}, f32[128,512]{1,0:T(8,128)S(1)}, u32[]{:S(2)}, u32[]{:S(2)}) %collective-permute-start.2) | collective-permute-done | bytes 262176 | tf_op jit(solution)/shard_map/ppermute | solution.py:416
  49.2 1.7 %collective-permute-done.7.refs_8_ = f32[128,128]{1,0:T(8,128)S(1)} collective-permute-done((f32[128,128]{1,0:T(8,128)S(1)}, f32[128,128]{1,0:T(8,128)S(1)}, u32[]{:S(2)}, u32[]{:S(2)}) %collective-permute-start.7) | collective-permute-done | bytes 65568 | tf_op jit(solution)/shard_map/ppermute | solution.py:416
  50.9 0.0 collective-permute-done.8.refs_9_
  50.9 0.0 copy-done
  50.9 4.4 %shard_map.50 = (f32[64,32,512]{2,1,0:T(8,128)S(1)}, f32[4,2,32,128]{3,2,1,0:T(8,128)S(1)}) custom-call(f32[64,64]{1,0:T(8,128)S(1)} %copy-done, f32[1,512]{1,0:T(1,128)S(1)} %bitcast.6, f32[128,512]{1,0:T(8,128)S(1)} %collective-permute-done.refs_0_, f32[128,384]{1,0:T(8,128)S(1)} %collective-permute-done.1.refs_1_, ...), custom_call_target="tpu_custom_call" | custom-call | tf_op jit(solution)/shard_map/pallas_call | solution.py:372
  55.2 0.1 collective-permute-start.9
  55.3 2.4 %shard_map.51.keep_ref = f32[4,2,32,128]{3,2,1,0:T(8,128)S(1)} custom-call(f32[64,32,512]{2,1,0:T(8,128)S(1)} %get-tuple-element.18.spec_ref.refs_8_), custom_call_target="tpu_custom_call" | custom-call | tf_op jit(solution)/shard_map/pallas_call | solution.py:372
  57.7 0.0 collective-permute-done.9.got_ref
  57.7 1.6 %collective-permute-start.10 = (f32[2,32,128]{2,1,0:T(8,128)S(1)}, f32[2,32,128]{2,1,0:T(8,128)S(1)}, u32[]{:S(2)}, u32[]{:S(2)}) collective-permute-start(f32[2,32,128]{2,1,0:T(8,128)S(1)} %get-tuple-element.21), channel_id=1, source_target_pairs={{0,1},{1,0},{2,3},{3,2},{4,5},{5,4},{6,7},{7,6},{8,9},{9,8},{10,11... | collective-permute-start | bytes 98312 | tf_op jit(solution)/shard_map/ppermute | solution.py:394
  59.3 1.5 %collective-permute-start.11 = (f32[2,32,128]{2,1,0:T(8,128)S(1)}, f32[2,32,128]{2,1,0:T(8,128)S(1)}, u32[]{:S(2)}, u32[]{:S(2)}) collective-permute-start(f32[2,32,128]{2,1,0:T(8,128)S(1)} %get-tuple-element.22), channel_id=1, source_target_pairs={{0,2},{1,3},{2,0},{3,1},{4,6},{5,7},{6,4},{7,5},{8,10},{9,11},{10,... | collective-permute-start | bytes 98312 | tf_op jit(solution)/shard_map/ppermute | solution.py:394
  60.8 0.5 collective-permute-start.12
  61.3 0.4 collective-permute-done.10.refs_1_
  61.7 1.5 %collective-permute-done.11.refs_2_ = f32[2,32,128]{2,1,0:T(8,128)S(1)} collective-permute-done((f32[2,32,128]{2,1,0:T(8,128)S(1)}, f32[2,32,128]{2,1,0:T(8,128)S(1)}, u32[]{:S(2)}, u32[]{:S(2)}) %collective-permute-start.11) | collective-permute-done | bytes 32800 | tf_op jit(solution)/shard_map/ppermute | solution.py:394
  63.2 2.4 %collective-permute-done.12.refs_3_ = f32[2,32,128]{2,1,0:T(8,128)S(1)} collective-permute-done((f32[2,32,128]{2,1,0:T(8,128)S(1)}, f32[2,32,128]{2,1,0:T(8,128)S(1)}, u32[]{:S(2)}, u32[]{:S(2)}) %collective-permute-start.12) | collective-permute-done | bytes 32800 | tf_op jit(solution)/shard_map/ppermute | solution.py:394
  65.7 2.5 %collective-permute-start.15 = (f32[2,32,128]{2,1,0:T(8,128)S(1)}, f32[2,32,128]{2,1,0:T(8,128)S(1)}, u32[]{:S(2)}, u32[]{:S(2)}) collective-permute-start(f32[2,32,128]{2,1,0:T(8,128)S(1)} %shard_map.53.refs_0_), channel_id=1, source_target_pairs={{0,24},{4,28},{8,16},{12,20},{16,8},{20,12},{24,0},{28,4},{1,25},{... | collective-permute-start | bytes 98312 | tf_op jit(solution)/shard_map/ppermute | solution.py:400
  68.2 0.9 collective-permute-start.14
  69.0 1.1 %collective-permute-start.13 = (f32[2,32,128]{2,1,0:T(8,128)S(1)}, f32[2,32,128]{2,1,0:T(8,128)S(1)}, u32[]{:S(2)}, u32[]{:S(2)}) collective-permute-start(f32[2,32,128]{2,1,0:T(8,128)S(1)} %shard_map.53.refs_0_), channel_id=1, source_target_pairs={{0,8},{4,12},{8,0},{12,4},{16,24},{20,28},{24,16},{28,20},{1,9},{5... | collective-permute-start | bytes 98312 | tf_op jit(solution)/shard_map/ppermute | solution.py:400
  70.1 1.5 %collective-permute-done.15.refs_3_ = f32[2,32,128]{2,1,0:T(8,128)S(1)} collective-permute-done((f32[2,32,128]{2,1,0:T(8,128)S(1)}, f32[2,32,128]{2,1,0:T(8,128)S(1)}, u32[]{:S(2)}, u32[]{:S(2)}) %collective-permute-start.15) | collective-permute-done | bytes 32800 | tf_op jit(solution)/shard_map/ppermute | solution.py:400
  71.6 1.5 %collective-permute-done.14.refs_2_ = f32[2,32,128]{2,1,0:T(8,128)S(1)} collective-permute-done((f32[2,32,128]{2,1,0:T(8,128)S(1)}, f32[2,32,128]{2,1,0:T(8,128)S(1)}, u32[]{:S(2)}, u32[]{:S(2)}) %collective-permute-start.14) | collective-permute-done | bytes 32800 | tf_op jit(solution)/shard_map/ppermute | solution.py:400
  73.1 0.2 collective-permute-done.13.refs_1_
  73.3 3.9 %shard_map.54.refs_0_ = f32[2,32,128]{2,1,0:T(8,128)S(1)} custom-call(f32[2,32,128]{2,1,0:T(8,128)S(1)} %shard_map.53.refs_0_, f32[2,32,128]{2,1,0:T(8,128)S(1)} %collective-permute-done.13.refs_1_, f32[2,32,128]{2,1,0:T(8,128)S(1)} %collective-permute-done.14.refs_2_, f32[2,32,128]{2,1,0:T(8,128)S(1)} %collective-permute-done.15.refs_3_), custom_call_target="tpu_custom_call" | custom-call | tf_op jit(solution)/shard_map/pallas_call | solution.py:372
  77.2 0.5 collective-permute-start.18
  77.8 1.5 %collective-permute-start.17 = (f32[2,32,128]{2,1,0:T(8,128)S(1)}, f32[2,32,128]{2,1,0:T(8,128)S(1)}, u32[]{:S(2)}, u32[]{:S(2)}) collective-permute-start(f32[2,32,128]{2,1,0:T(8,128)S(1)} %shard_map.54.refs_0_), channel_id=1, source_target_pairs={{0,2},{1,3},{2,0},{3,1},{4,6},{5,7},{6,4},{7,5},{8,10},{9,11},{10,... | collective-permute-start | bytes 98312 | tf_op jit(solution)/shard_map/ppermute | solution.py:402
  79.3 1.5 %collective-permute-start.16 = (f32[2,32,128]{2,1,0:T(8,128)S(1)}, f32[2,32,128]{2,1,0:T(8,128)S(1)}, u32[]{:S(2)}, u32[]{:S(2)}) collective-permute-start(f32[2,32,128]{2,1,0:T(8,128)S(1)} %shard_map.54.refs_0_), channel_id=1, source_target_pairs={{0,1},{1,0},{2,3},{3,2},{4,5},{5,4},{6,7},{7,6},{8,9},{9,8},{10,11... | collective-permute-start | bytes 98312 | tf_op jit(solution)/shard_map/ppermute | solution.py:402
  80.8 0.0 collective-permute-start.19
  80.8 1.3 %collective-permute-done.18.refs_3_ = f32[2,32,128]{2,1,0:T(8,128)S(1)} collective-permute-done((f32[2,32,128]{2,1,0:T(8,128)S(1)}, f32[2,32,128]{2,1,0:T(8,128)S(1)}, u32[]{:S(2)}, u32[]{:S(2)}) %collective-permute-start.18) | collective-permute-done | bytes 32800 | tf_op jit(solution)/shard_map/ppermute | solution.py:402
  82.1 0.0 collective-permute-start.22
  82.1 0.0 collective-permute-done.17.refs_2_
  82.1 0.5 collective-permute-start.21
  82.6 0.6 collective-permute-done.16.refs_1_
  83.2 0.0 collective-permute-start.20
  83.2 0.0 collective-permute-done.19.refs_4_
  83.2 0.1 collective-permute-done.22.refs_7_
  83.3 0.2 collective-permute-done.21.refs_6_
  83.5 0.9 %collective-permute-done.20.refs_5_ = f32[2,32,128]{2,1,0:T(8,128)S(1)} collective-permute-done((f32[2,32,128]{2,1,0:T(8,128)S(1)}, f32[2,32,128]{2,1,0:T(8,128)S(1)}, u32[]{:S(2)}, u32[]{:S(2)}) %collective-permute-start.20) | collective-permute-done | bytes 32800 | tf_op jit(solution)/shard_map/ppermute | solution.py:403
  84.4 4.0 %shard_map.55 = (f32[33,31,8,128]{3,2,1,0:T(8,128)}, f32[2,33,31,31]{3,2,1,0:T(8,128)S(1)}) custom-call(f32[2,32,128]{2,1,0:T(8,128)S(1)} %shard_map.54.refs_0_, f32[2,32,128]{2,1,0:T(8,128)S(1)} %collective-permute-done.16.refs_1_, f32[2,32,128]{2,1,0:T(8,128)S(1)} %collective-permute-done.17.refs_2_, f32[2,32,128]{2,1,0:T(8,128)S(1)} %collective-permute-done.18.refs_3_, ...), custom_call_target="tpu_custom_call" | custom-call | tf_op jit(solution)/shard_map/pallas_call | solution.py:372
  88.4 1.6 %copy.6 = f32[2,33,31,31]{1,0,3,2:T(2,128)} copy(f32[2,33,31,31]{3,2,1,0:T(8,128)S(1)} %get-tuple-element.27) | data formatting | bytes 507408
  (3 shorter events, 0.1 us)
Async XLA Ops:
  0.6 37.7 %copy-start.1 = (f32[512]{0:T(512)S(1)}, f32[512]{0:T(512)}, u32[]{:S(2)}) copy-start(f32[512]{0:T(512)} %param.4) | copy-start | bytes 6148
  0.6 50.2 %copy-start = (f32[64,64]{1,0:T(8,128)S(1)}, f32[64,64]{1,0:T(8,128)}, u32[]{:S(2)}) copy-start(f32[64,64]{1,0:T(8,128)} %constant.33.clone.table_ref) | copy-start | bytes 49156
  1.6 29.5 %collective-permute-start = (f32[128,512]{1,0:T(8,128)S(1)}, f32[128,512]{1,0:T(8,128)S(1)}, u32[]{:S(2)}, u32[]{:S(2)}) collective-permute-start(f32[128,512]{1,0:T(8,128)S(1)} %constant_dynamic-slice_fusion.9), channel_id=1, source_target_pairs={{0,28},{4,24},{8,20},{12,16},{16,12},{20,8},{24,4},{28,0},{1,29},{... | collective-permute-start | bytes 786440 | tf_op jit(solution)/shard_map/ppermute | solution.py:416
  7.2 23.9 %collective-permute-start.3 = (f32[128,384]{1,0:T(8,128)S(1)}, f32[128,384]{1,0:T(8,128)S(1)}, u32[]{:S(2)}, u32[]{:S(2)}) collective-permute-start(f32[128,384]{1,0:T(8,128)S(1)} %get-tuple-element.35), channel_id=1, source_target_pairs={{0,16},{4,20},{8,24},{12,28},{16,0},{20,4},{24,8},{28,12},{1,17},{... | collective-permute-start | bytes 589832 | tf_op jit(solution)/shard_map/ppermute | solution.py:416
  8.7 28.1 %collective-permute-start.6 = (f32[128,512]{1,0:T(8,128)S(1)}, f32[128,512]{1,0:T(8,128)S(1)}, u32[]{:S(2)}, u32[]{:S(2)}) collective-permute-start(f32[128,512]{1,0:T(8,128)S(1)} %get-tuple-element.31), channel_id=1, source_target_pairs={{0,4},{4,0},{8,12},{12,8},{16,20},{20,16},{24,28},{28,24},{1,5},{5... | collective-permute-start | bytes 786440 | tf_op jit(solution)/shard_map/ppermute | solution.py:416
  9.5 25.2 %collective-permute-start.1 = (f32[128,384]{1,0:T(8,128)S(1)}, f32[128,384]{1,0:T(8,128)S(1)}, u32[]{:S(2)}, u32[]{:S(2)}) collective-permute-start(f32[128,384]{1,0:T(8,128)S(1)} %get-tuple-element.36), channel_id=1, source_target_pairs={{0,24},{4,28},{8,16},{12,20},{16,8},{20,12},{24,0},{28,4},{1,25},{... | collective-permute-start | bytes 589832 | tf_op jit(solution)/shard_map/ppermute | solution.py:416
  11.1 27.3 %collective-permute-start.5 = (f32[128,512]{1,0:T(8,128)S(1)}, f32[128,512]{1,0:T(8,128)S(1)}, u32[]{:S(2)}, u32[]{:S(2)}) collective-permute-start(f32[128,512]{1,0:T(8,128)S(1)} %get-tuple-element.32), channel_id=1, source_target_pairs={{0,8},{4,12},{8,0},{12,4},{16,24},{20,28},{24,16},{28,20},{1,9},{5... | collective-permute-start | bytes 786440 | tf_op jit(solution)/shard_map/ppermute | solution.py:416
  31.2 13.5 %collective-permute-start.4 = (f32[128,512]{1,0:T(8,128)S(1)}, f32[128,512]{1,0:T(8,128)S(1)}, u32[]{:S(2)}, u32[]{:S(2)}) collective-permute-start(f32[128,512]{1,0:T(8,128)S(1)} %get-tuple-element.33), channel_id=1, source_target_pairs={{0,12},{4,8},{8,4},{12,0},{16,28},{20,24},{24,20},{28,16},{1,13},{... | collective-permute-start | bytes 786440 | tf_op jit(solution)/shard_map/ppermute | solution.py:416
  31.2 18.0 %collective-permute-start.2 = (f32[128,512]{1,0:T(8,128)S(1)}, f32[128,512]{1,0:T(8,128)S(1)}, u32[]{:S(2)}, u32[]{:S(2)}) collective-permute-start(f32[128,512]{1,0:T(8,128)S(1)} %get-tuple-element.34), channel_id=1, source_target_pairs={{0,20},{4,16},{8,28},{12,24},{16,4},{20,0},{24,12},{28,8},{1,21},{... | collective-permute-start | bytes 786440 | tf_op jit(solution)/shard_map/ppermute | solution.py:416
  34.7 16.2 %collective-permute-start.7 = (f32[128,128]{1,0:T(8,128)S(1)}, f32[128,128]{1,0:T(8,128)S(1)}, u32[]{:S(2)}, u32[]{:S(2)}) collective-permute-start(f32[128,128]{1,0:T(8,128)S(1)} %get-tuple-element.16), channel_id=1, source_target_pairs={{0,16},{4,20},{8,24},{12,28},{16,0},{20,4},{24,8},{28,12},{1,17},{... | collective-permute-start | bytes 196616 | tf_op jit(solution)/shard_map/ppermute | solution.py:416
  36.8 14.0 %collective-permute-start.8 = (f32[128,128]{1,0:T(8,128)S(1)}, f32[128,128]{1,0:T(8,128)S(1)}, u32[]{:S(2)}, u32[]{:S(2)}) collective-permute-start(f32[128,128]{1,0:T(8,128)S(1)} %get-tuple-element.17), channel_id=1, source_target_pairs={{0,24},{4,28},{8,16},{12,20},{16,8},{20,12},{24,0},{28,4},{1,25},{... | collective-permute-start | bytes 196616 | tf_op jit(solution)/shard_map/ppermute | solution.py:416
  55.2 2.5 %collective-permute-start.9 = (f32[4,2,32,128]{3,2,1,0:T(8,128)S(1)}, f32[4,2,32,128]{3,2,1,0:T(8,128)S(1)}, u32[]{:S(2)}, u32[]{:S(2)}) collective-permute-start(f32[4,2,32,128]{3,2,1,0:T(8,128)S(1)} %get-tuple-element.19), channel_id=1, source_target_pairs={{0,4},{4,0},{8,12},{12,8},{16,20},{20,16},{24,28},{28,24},{1,5},{5... | collective-permute-start | bytes 393224 | tf_op jit(solution)/shard_map/ppermute | solution.py:443
  57.7 4.0 %collective-permute-start.10 = (f32[2,32,128]{2,1,0:T(8,128)S(1)}, f32[2,32,128]{2,1,0:T(8,128)S(1)}, u32[]{:S(2)}, u32[]{:S(2)}) collective-permute-start(f32[2,32,128]{2,1,0:T(8,128)S(1)} %get-tuple-element.21), channel_id=1, source_target_pairs={{0,1},{1,0},{2,3},{3,2},{4,5},{5,4},{6,7},{7,6},{8,9},{9,8},{10,11... | collective-permute-start | bytes 98312 | tf_op jit(solution)/shard_map/ppermute | solution.py:394
  59.3 3.9 %collective-permute-start.11 = (f32[2,32,128]{2,1,0:T(8,128)S(1)}, f32[2,32,128]{2,1,0:T(8,128)S(1)}, u32[]{:S(2)}, u32[]{:S(2)}) collective-permute-start(f32[2,32,128]{2,1,0:T(8,128)S(1)} %get-tuple-element.22), channel_id=1, source_target_pairs={{0,2},{1,3},{2,0},{3,1},{4,6},{5,7},{6,4},{7,5},{8,10},{9,11},{10,... | collective-permute-start | bytes 98312 | tf_op jit(solution)/shard_map/ppermute | solution.py:394
  60.8 4.8 %collective-permute-start.12 = (f32[2,32,128]{2,1,0:T(8,128)S(1)}, f32[2,32,128]{2,1,0:T(8,128)S(1)}, u32[]{:S(2)}, u32[]{:S(2)}) collective-permute-start(f32[2,32,128]{2,1,0:T(8,128)S(1)} %get-tuple-element.23), channel_id=1, source_target_pairs={{0,3},{1,2},{2,1},{3,0},{4,7},{5,6},{6,5},{7,4},{8,11},{9,10},{10,... | collective-permute-start | bytes 98312 | tf_op jit(solution)/shard_map/ppermute | solution.py:394
  65.7 5.9 %collective-permute-start.15 = (f32[2,32,128]{2,1,0:T(8,128)S(1)}, f32[2,32,128]{2,1,0:T(8,128)S(1)}, u32[]{:S(2)}, u32[]{:S(2)}) collective-permute-start(f32[2,32,128]{2,1,0:T(8,128)S(1)} %shard_map.53.refs_0_), channel_id=1, source_target_pairs={{0,24},{4,28},{8,16},{12,20},{16,8},{20,12},{24,0},{28,4},{1,25},{... | collective-permute-start | bytes 98312 | tf_op jit(solution)/shard_map/ppermute | solution.py:400
  68.2 4.9 %collective-permute-start.14 = (f32[2,32,128]{2,1,0:T(8,128)S(1)}, f32[2,32,128]{2,1,0:T(8,128)S(1)}, u32[]{:S(2)}, u32[]{:S(2)}) collective-permute-start(f32[2,32,128]{2,1,0:T(8,128)S(1)} %shard_map.53.refs_0_), channel_id=1, source_target_pairs={{0,16},{4,20},{8,24},{12,28},{16,0},{20,4},{24,8},{28,12},{1,17},{... | collective-permute-start | bytes 98312 | tf_op jit(solution)/shard_map/ppermute | solution.py:400
  69.0 4.3 %collective-permute-start.13 = (f32[2,32,128]{2,1,0:T(8,128)S(1)}, f32[2,32,128]{2,1,0:T(8,128)S(1)}, u32[]{:S(2)}, u32[]{:S(2)}) collective-permute-start(f32[2,32,128]{2,1,0:T(8,128)S(1)} %shard_map.53.refs_0_), channel_id=1, source_target_pairs={{0,8},{4,12},{8,0},{12,4},{16,24},{20,28},{24,16},{28,20},{1,9},{5... | collective-permute-start | bytes 98312 | tf_op jit(solution)/shard_map/ppermute | solution.py:400
  77.2 4.9 %collective-permute-start.18 = (f32[2,32,128]{2,1,0:T(8,128)S(1)}, f32[2,32,128]{2,1,0:T(8,128)S(1)}, u32[]{:S(2)}, u32[]{:S(2)}) collective-permute-start(f32[2,32,128]{2,1,0:T(8,128)S(1)} %shard_map.54.refs_0_), channel_id=1, source_target_pairs={{0,3},{1,2},{2,1},{3,0},{4,7},{5,6},{6,5},{7,4},{8,11},{9,10},{10,... | collective-permute-start | bytes 98312 | tf_op jit(solution)/shard_map/ppermute | solution.py:402
  77.8 4.3 %collective-permute-start.17 = (f32[2,32,128]{2,1,0:T(8,128)S(1)}, f32[2,32,128]{2,1,0:T(8,128)S(1)}, u32[]{:S(2)}, u32[]{:S(2)}) collective-permute-start(f32[2,32,128]{2,1,0:T(8,128)S(1)} %shard_map.54.refs_0_), channel_id=1, source_target_pairs={{0,2},{1,3},{2,0},{3,1},{4,6},{5,7},{6,4},{7,5},{8,10},{9,11},{10,... | collective-permute-start | bytes 98312 | tf_op jit(solution)/shard_map/ppermute | solution.py:402
  79.3 3.9 %collective-permute-start.16 = (f32[2,32,128]{2,1,0:T(8,128)S(1)}, f32[2,32,128]{2,1,0:T(8,128)S(1)}, u32[]{:S(2)}, u32[]{:S(2)}) collective-permute-start(f32[2,32,128]{2,1,0:T(8,128)S(1)} %shard_map.54.refs_0_), channel_id=1, source_target_pairs={{0,1},{1,0},{2,3},{3,2},{4,5},{5,4},{6,7},{7,6},{8,9},{9,8},{10,11... | collective-permute-start | bytes 98312 | tf_op jit(solution)/shard_map/ppermute | solution.py:402
  80.8 2.4 %collective-permute-start.19 = (f32[2,32,128]{2,1,0:T(8,128)S(1)}, f32[2,32,128]{2,1,0:T(8,128)S(1)}, u32[]{:S(2)}, u32[]{:S(2)}) collective-permute-start(f32[2,32,128]{2,1,0:T(8,128)S(1)} %shard_map.54.refs_0_), channel_id=1, source_target_pairs={{0,4},{4,0},{8,12},{12,8},{16,20},{20,16},{24,28},{28,24},{1,5},{5... | collective-permute-start | bytes 98312 | tf_op jit(solution)/shard_map/ppermute | solution.py:403
  82.1 1.2 %collective-permute-start.22 = (f32[2,32,128]{2,1,0:T(8,128)S(1)}, f32[2,32,128]{2,1,0:T(8,128)S(1)}, u32[]{:S(2)}, u32[]{:S(2)}) collective-permute-start(f32[2,32,128]{2,1,0:T(8,128)S(1)} %collective-permute-done.18.refs_3_), channel_id=1, source_target_pairs={{0,4},{4,0},{8,12},{12,8},{16,20},{20,16},{24,28},{28,24},{1,5},{5... | collective-permute-start | bytes 98312 | tf_op jit(solution)/shard_map/ppermute | solution.py:403
  82.1 1.4 %collective-permute-start.21 = (f32[2,32,128]{2,1,0:T(8,128)S(1)}, f32[2,32,128]{2,1,0:T(8,128)S(1)}, u32[]{:S(2)}, u32[]{:S(2)}) collective-permute-start(f32[2,32,128]{2,1,0:T(8,128)S(1)} %collective-permute-done.17.refs_2_), channel_id=1, source_target_pairs={{0,4},{4,0},{8,12},{12,8},{16,20},{20,16},{24,28},{28,24},{1,5},{5... | collective-permute-start | bytes 98312 | tf_op jit(solution)/shard_map/ppermute | solution.py:403
  83.2 1.2 %collective-permute-start.20 = (f32[2,32,128]{2,1,0:T(8,128)S(1)}, f32[2,32,128]{2,1,0:T(8,128)S(1)}, u32[]{:S(2)}, u32[]{:S(2)}) collective-permute-start(f32[2,32,128]{2,1,0:T(8,128)S(1)} %collective-permute-done.16.refs_1_), channel_id=1, source_target_pairs={{0,4},{4,0},{8,12},{12,8},{16,20},{20,16},{24,28},{28,24},{1,5},{5... | collective-permute-start | bytes 98312 | tf_op jit(solution)/shard_map/ppermute | solution.py:403

commit v4 on v3

--- a/solution.py
+++ b/solution.py
@@ -136,32 +136,38 @@
     return total, low - (total - high)
 
 
-def gram_half(spec_ref, out_ref, side):
+def group_at(other_core, d):
+    return ((lax.axis_index("tm") & 1) ^ other_core) * SIDE + ((lax.axis_index("pts") & (SIDE - 1)) ^ d)
+
+
+def gram_groups(spec_ref, groups):
     row = lax.broadcasted_iota(jnp.int32, (32, 32), 0)
     column = lax.broadcasted_iota(jnp.int32, (32, 32), 1)
 
     def products_of(step):
-        slot = side * SIDE * 4 + step
+        slot = groups[step // 4] * 4 + step % 4
         return gram_products(spec_ref[slot], spec_ref[SLOTS + slot])
 
+    results = []
     ahead = products_of(0)
-    for step in range(4 * SIDE):
+    for step in range(4 * len(groups)):
         products = ahead
-        if step + 1 < 4 * SIDE:
+        if step + 1 < 4 * len(groups):
             ahead = products_of(step + 1)
-        q, s = divmod(step, 4)
+        s = step % 4
         if s == 0:
             packed = [[], []]
-        sums = gram_pairs(products, side == 0 if step == 0 else None)
+        sums = gram_pairs(products, None if s else groups[step // 4] == 0)
         for part in range(2):
             real, imag = sums[part][:, :32], sums[part][:, 32:]
             square = jnp.where(column >= row, real, imag)
-            if step == 0:
+            if s == 0:
                 diagonal = jnp.sum(jnp.where(column == row, imag, 0.0), axis=0, keepdims=True)
                 square = jnp.where(row == NB, diagonal, square)
             packed[part].append(square)
-            if s == 3:
-                out_ref[q, part] = jnp.concatenate(packed[part], axis=1)
+        if s == 3:
+            results.append([jnp.concatenate(part, axis=1) for part in packed])
+    return results
 
 
 def spectrum_kernel(table_ref, root_ref, *refs, places):
@@ -172,19 +178,24 @@
         at = slice(first, first + size)
         records_ref[pl.ds(start, rows), at] = piece[...] * root_ref[:, at]
     spectrum_body(table_ref[...], records_ref[...], spec_ref)
-    gram_half(spec_ref, send_ref, (lax.axis_index("tm") & 1) ^ 1)
+    for d, pair in enumerate(gram_groups(spec_ref, [group_at(1, d) for d in range(SIDE)])):
+        send_ref[d, 0], send_ref[d, 1] = pair
 
 
 def keep_kernel(spec_ref, keep_ref):
-    gram_half(spec_ref, keep_ref, lax.axis_index("tm") & 1)
+    for number, pair in enumerate(gram_groups(spec_ref, [group_at(0, d) for d in range(1, SIDE)])):
+        keep_ref[number, 0], keep_ref[number, 1] = pair
 
 
 def core_sum_kernel(keep_ref, got_ref, *out_refs):
-    for d in range(SIDE):
-        q = (lax.axis_index("pts") & (SIDE - 1)) ^ d
-        high, low = pair_add((keep_ref[q, 0], keep_ref[q, 1]), (got_ref[q, 0], got_ref[q, 1]))
-        out_refs[d][0] = high
-        out_refs[d][1] = low
+    for number, out_ref in enumerate(out_refs):
+        d = number + 1
+        out_ref[0], out_ref[1] = pair_add((keep_ref[number, 0], keep_ref[number, 1]), (got_ref[d, 0], got_ref[d, 1]))
+
+
+def own_kernel(spec_ref, got_ref, out_ref):
+    own = gram_groups(spec_ref, [group_at(0, 0)])[0]
+    out_ref[0], out_ref[1] = pair_add(own, (got_ref[0, 0], got_ref[0, 1]))
 
 
 def pair_sum_kernel(*refs):
@@ -244,15 +255,34 @@
         total = high + low
         return [total, low - (total - high)]
 
+    def pivots(real_part, imag_part):
+        return real_part, [jnp.where(two_real, b, a) for a, b in zip(real_part, imag_part)]
+
+    def row_of(blocks, at):
+        return [jnp.broadcast_to(part[at % 8:at % 8 + 1], shape) for part in blocks[at // 8]]
+
+    def next_pivots(k):
+        next_real, next_imag = row_of(real, k + 1), row_of(imag, k + 1)
+        left_real, left_imag = ([spread(part, k) for part in parts] for parts in (next_real, next_imag))
+        step_real = quotient(left_real, pivot_real, real_halves, real_inverse)
+        step_imag = quotient(left_imag, pivot_imag, imag_halves, imag_inverse)
+        p = pair_product(step_real, halves(step_real[0]), left_real, halves(left_real[0]))
+        q = pair_product(step_imag, halves(step_imag[0]), left_imag, halves(left_imag[0]))
+        cross = [jnp.where(two_real, 0.0, part) for part in q]
+        new_real = minus([spread(part, k + 1) for part in next_real], [p, cross])
+        new_imag = minus([spread(part, k + 1) for part in next_imag], [q])
+        return pivots(new_real, new_imag)
+
+    pivot_real, pivot_imag = pivots([spread(part, 0) for part in row_of(real, 0)], [spread(part, 0) for part in row_of(imag, 0)])
     for k in range(NB):
         at = k % 8
         line_real = [jnp.broadcast_to(part[at:at + 1], shape) for part in real[k // 8]]
         line_imag = [jnp.broadcast_to(part[at:at + 1], shape) for part in imag[k // 8]]
-        pivot_real = [spread(part, k) for part in line_real]
-        pivot_imag = [jnp.where(two_real, spread(part, k), own) for part, own in zip(line_imag, pivot_real)]
         real_halves, imag_halves = halves(pivot_real[0]), halves(pivot_imag[0])
         real_inverse = 1.0 / pivot_real[0]
         imag_inverse = jnp.where(two_real, 1.0 / pivot_imag[0], real_inverse)
+        if k + 1 < NB:
+            coming = next_pivots(k)
         here = column == k
         line_real = (jnp.where(here, 1.0, line_real[0]), jnp.where(here, 0.0, line_real[1]))
         line_imag = (
@@ -282,6 +312,7 @@
             p = pair_product(own, own_halves, line_imag, line_imag_halves)
             q = pair_product(cross, cross_halves, line_real, line_real_halves)
             imag[i] = minus(block_imag, [p, q])
+        pivot_real, pivot_imag = coming
     for i in range(4):
         at = slice(8 * i, 8 * i + 8)
         pivot_real = spread(real[i][0], row + 8 * i)
@@ -291,8 +322,12 @@
         out_ref[1, at] = jnp.where(good, imag[i][0] / jnp.sqrt(pivot_imag), 0.0)
 
 
-def apply_kernel(*refs):
-    pieces, (spec_ref, modes_ref, triangle_ref, tiles_ref, sent) = refs[:GROUPS], refs[GROUPS:]
+def apply_kernel(*refs, side):
+    pieces, spec_ref = refs[:SIDE], refs[SIDE]
+    if side == 0:
+        modes_ref, last_ref, tiles_ref, sent = refs[SIDE + 1:]
+    else:
+        others, before_ref, _, modes_ref, triangle_ref, tiles_ref, sent = refs[SIDE + 1:2 * SIDE + 1], *refs[2 * SIDE + 1:]
     points = spec_ref.shape[-1]
     shape = (32, 128)
     row = lax.broadcasted_iota(jnp.int32, shape, 0)
@@ -315,64 +350,78 @@
         copy.start()
         copies.append(copy)
 
-    last_real = jnp.zeros((32, points), jnp.float32)
-    last_triangle = jnp.zeros((NB, NB), jnp.float32)
-    for c in range(2):
-        for d in range(SIDE):
-            piece = pieces[SIDE * c + d]
-            group = ((lax.axis_index("tm") & 1) ^ c) * SIDE + ((lax.axis_index("pts") & (SIDE - 1)) ^ d)
-            is_first = group == 0
-            both_real, both_imag = piece[0], piece[1]
-            upper_real = jnp.where(column >= row, both_real, 0.0)
-            upper_imag = jnp.where(column >= row, both_imag, 0.0)
-            two_real = jnp.logical_and(lane < 32, is_first)
-            low_real = jnp.where(column < row, both_real, jnp.where(here, 1.0 / both_real, 0.0))
-            low_imag = jnp.where(
-                column < row, both_imag, jnp.where(jnp.logical_and(here, two_real), 1.0 / both_imag, 0.0)
-            )
-            good = row < NB
-            low_real = jnp.where(good, low_real, 0.0)
-            low_imag = jnp.where(good, low_imag, 0.0)
-            cross = jnp.where(two_real, 0.0, low_imag)
-            own = jnp.where(two_real, low_imag, low_real)
-            for s in range(4):
-                slot = 4 * group + s
-
-                def spread(value):
-                    return jnp.take_along_axis(value, 32 * s + column, axis=1, mode="promise_in_bounds")
-
-                wide_cross = spread(cross)
-                top = jnp.where(even, spread(low_real), wide_cross)
-                bottom = jnp.where(even, -wide_cross, spread(own))
-                l0, l1, l2 = (part.astype(jnp.float32) for part in slices_of(jnp.concatenate([top, bottom], axis=0), 3))
-                left = [l0, jnp.where(wide, l1, l0), jnp.where(wide, l1, l2)]
-                left = jnp.concatenate([part.astype(jnp.bfloat16) for part in left], axis=1)
-                r0, r1, r2 = slices_of(jnp.concatenate([spec_ref[slot], spec_ref[SLOTS + slot]], axis=0), 3)
-                right = jnp.concatenate([r0, r1, r0, r2, r1, r0], axis=0)
-                out = jnp.dot(left, right, preferred_element_type=jnp.float32)
-                real, imag = out[:32], out[32:]
-                square = upper_imag[:NB, 32 * s:32 * s + NB]
-                if s == 0:
-                    last_real = jnp.where(is_first, imag, last_real)
-                    last_triangle = jnp.where(is_first, square, last_triangle)
-                    imag = jnp.where(is_first, 0.0, imag)
-                    square = jnp.where(is_first, 0.0, square)
-                put(slot, real, imag)
-                triangle_ref[0, slot] = upper_real[:NB, 32 * s:32 * s + NB]
-                triangle_ref[1, slot] = square
-    put(SLOTS, last_real, None)
-    triangle_ref[0, SLOTS] = last_triangle
-    triangle_ref[1, SLOTS] = jnp.zeros((NB, NB), jnp.float32)
+    def group_of(c, d):
+        return ((lax.axis_index("tm") & 1) ^ c) * SIDE + ((lax.axis_index("pts") & (SIDE - 1)) ^ d)
+
+    last_real = jnp.zeros((32, points), jnp.float32) if side == 0 else before_ref[...]
+    for d in range(SIDE):
+        piece = pieces[d]
+        group = group_of(side, d)
+        is_first = group == 0
+        both_real, both_imag = piece[0], piece[1]
+        two_real = jnp.logical_and(lane < 32, is_first)
+        low_real = jnp.where(column < row, both_real, jnp.where(here, 1.0 / both_real, 0.0))
+        low_imag = jnp.where(
+            column < row, both_imag, jnp.where(jnp.logical_and(here, two_real), 1.0 / both_imag, 0.0)
+        )
+        good = row < NB
+        low_real = jnp.where(good, low_real, 0.0)
+        low_imag = jnp.where(good, low_imag, 0.0)
+        cross = jnp.where(two_real, 0.0, low_imag)
+        own = jnp.where(two_real, low_imag, low_real)
+        for s in range(4):
+            slot = 4 * group + s
+
+            def spread(value):
+                return jnp.take_along_axis(value, 32 * s + column, axis=1, mode="promise_in_bounds")
+
+            wide_cross = spread(cross)
+            top = jnp.where(even, spread(low_real), wide_cross)
+            bottom = jnp.where(even, -wide_cross, spread(own))
+            l0, l1, l2 = (part.astype(jnp.float32) for part in slices_of(jnp.concatenate([top, bottom], axis=0), 3))
+            left = [l0, jnp.where(wide, l1, l0), jnp.where(wide, l1, l2)]
+            left = jnp.concatenate([part.astype(jnp.bfloat16) for part in left], axis=1)
+            r0, r1, r2 = slices_of(jnp.concatenate([spec_ref[slot], spec_ref[SLOTS + slot]], axis=0), 3)
+            right = jnp.concatenate([r0, r1, r0, r2, r1, r0], axis=0)
+            out = jnp.dot(left, right, preferred_element_type=jnp.float32)
+            real, imag = out[:32], out[32:]
+            if s == 0:
+                last_real = jnp.where(is_first, imag, last_real)
+                imag = jnp.where(is_first, 0.0, imag)
+            put(slot, real, imag)
+    if side == 0:
+        last_ref[...] = last_real
+    else:
+        put(SLOTS, last_real, None)
+        last_triangle = jnp.zeros((NB, NB), jnp.float32)
+        for c, parts in ((0, others), (1, pieces)):
+            for d, piece in enumerate(parts):
+                group = group_of(c, d)
+                upper_real = jnp.where(column >= row, piece[0], 0.0)
+                upper_imag = jnp.where(column >= row, piece[1], 0.0)
+                for s in range(4):
+                    square = upper_imag[:NB, 32 * s:32 * s + NB]
+                    if s == 0:
+                        last_triangle = jnp.where(group == 0, square, last_triangle)
+                        square = jnp.where(group == 0, 0.0, square)
+                    triangle_ref[0, 4 * group + s] = upper_real[:NB, 32 * s:32 * s + NB]
+                    triangle_ref[1, 4 * group + s] = square
+        triangle_ref[0, SLOTS] = last_triangle
+        triangle_ref[1, SLOTS] = jnp.zeros((NB, NB), jnp.float32)
     for copy in copies:
         copy.wait()
 
 
-def call(body, out_shape, scratch, operands, out_spaces=None):
+def call(body, out_shape, scratch, operands, out_spaces=None, aliases=None):
     vmem = pl.BlockSpec(memory_space=pltpu.VMEM)
     return pl.pallas_call(
         body,
         out_shape=out_shape,
-        in_specs=[vmem] * len(operands),
+        in_specs=[
+            pl.BlockSpec(memory_space=pl.ANY) if number in (aliases or {}) else vmem
+            for number in range(len(operands))
+        ],
+        input_output_aliases=aliases or {},
         out_specs=[pl.BlockSpec(memory_space=space) for space in out_spaces] if out_spaces else jax.tree.map(lambda _: vmem, out_shape),
         scratch_shapes=scratch,
         compiler_params=pltpu.CompilerParams(vmem_limit_bytes=VMEM_BYTES),
@@ -387,12 +436,13 @@
     return [(i, i ^ difference) for i in range(size)]
 
 
-def factor_over_devices(keep, got, scale):
+def factor_over_devices(spec, got, scale):
     tm, pts = lax.axis_size("tm"), lax.axis_size("pts")
     part = f32(2, 32, 128)
-    parts = call(core_sum_kernel, (part,) * SIDE, [], [keep, got])
-    parts = [lax.ppermute(parts[d], "pts", xor_pairs(pts, d)) for d in reversed(range(1, SIDE))] + [parts[0]]
-    parts = parts[::-1]
+    keep = call(keep_kernel, f32(SIDE - 1, 2, 32, 128), [], [spec])
+    parts = call(core_sum_kernel, (part,) * (SIDE - 1), [], [keep, got])
+    parts = [lax.ppermute(parts[d - 1], "pts", xor_pairs(pts, d)) for d in range(SIDE - 1, 0, -1)]
+    parts = [call(own_kernel, part, [], [spec, got])] + parts
     total = call(pair_sum_kernel, part, [], parts)
     if pts > SIDE:
         parts = [total] + [lax.ppermute(total, "pts", xor_pairs(pts, d)) for d in range(SIDE, pts, SIDE)]
@@ -441,15 +491,25 @@
         [table_t, root, *pieces.values()],
     )
     got = lax.ppermute(send, "tm", xor_pairs(tm, 1))
-    keep = call(keep_kernel, half, [], [spec])
-    factors = factor_over_devices(keep, got, scale)
+    factors = factor_over_devices(spec, got, scale)
     tiles = points // 128
+    shape = f32(NF, NB, tiles * 2, 128)
+    scratch = [pltpu.VMEM((4 * SIDE + 1, NB, tiles * 2, 128), jnp.float32), pltpu.SemaphoreType.DMA((4 * SIDE + 1,))]
+    own, others = factors[:SIDE], factors[SIDE:]
+    modes, last_real = call(
+        functools.partial(apply_kernel, side=0),
+        (shape, f32(32, points)),
+        scratch,
+        [*own, spec],
+        [pl.ANY, pltpu.VMEM],
+    )
     modes, triangle = call(
-        apply_kernel,
-        (f32(NF, NB, tiles * 2, 128), f32(2, NF, NB, NB)),
-        [pltpu.VMEM((NF, NB, tiles * 2, 128), jnp.float32), pltpu.SemaphoreType.DMA((NF,))],
-        factors + [spec],
+        functools.partial(apply_kernel, side=1),
+        (shape, f32(2, NF, NB, NB)),
+        scratch,
+        [*others, spec, *own, last_real, modes],
         [pl.ANY, pltpu.VMEM],
+        {2 * SIDE + 2: 0},
     )
     modes = modes.reshape(NF, NB, tiles, 2, 128).transpose(3, 0, 1, 2, 4).reshape(2, NF, NB, points)
     return (modes, triangle)

time: 90.2 us -> 88.3 us (0.979)
  waiting for transfers between devices: 41.7 us -> 39.1 us
  Pallas kernels: 14.6 us -> 15.8 us
    ppermute x3, waiting for transfers between devices: 4.34 us -> 2.39 us  [factor_over_devices(): lax.ppermute(parts[d - 1], 'pts', xor_pairs(pts, d))]
    ppermute x4, waiting for transfers between devices: 1.2 us -> 0.01 us  [factor_over_devices(): return own + [lax.ppermute(piece, 'tm', xor_pairs(tm, 1)) for piece in own]]
    pallas_call x6 -> x8, Pallas kernels: 14.6 us -> 15.8 us  [call(): pl.pallas_call(body, out_shape=out_shape, in_specs=[pl.BlockSpec(memory_s...]
  transfers between devices with their start and end apart: 23 -> 23, of which waited for: 15 -> 13; matrix products, arithmetic and copies ran while one was open for 4% -> 4% of each run, Pallas kernels for 3% -> 6%
where the time goes in v4:
time: 88.3 us; the launch traced here: 88 us
  waiting for transfers between devices  39.1 us (44%)
  starting transfers between devices  26.4 us (30%)
  Pallas kernels  15.8 us (18%)
  local copies, waits for them, and re-layouts  5.88 us (7%)
    ppermute x9, waiting for transfers between devices, exchanged(): return lax.ppermute(piece, 'tm', xor_pairs(tm, d))  31.1 us
    pallas_call x8, Pallas kernels, call(): pl.pallas_call(body, out_shape=out_shape, in_specs=[pl.BlockSpec(memory_s...  15.8 us
    ppermute x9, starting transfers between devices, exchanged(): return lax.ppermute(piece, 'tm', xor_pairs(tm, d))  14.8 us
    ppermute x3, starting transfers between devices, factor_over_devices(): lax.ppermute(total, 'tm', xor_pairs(tm, d))  4.45 us
    dynamic_slice x4, local copies, waits for them, and re-layouts, piece_of(): return lax.dynamic_slice_in_dim(array, (me ^ d) * points + start, size, 1)  4.29 us
    ppermute x3, starting transfers between devices, factor_over_devices(): lax.ppermute(parts[d - 1], 'pts', xor_pairs(pts, d))  3.55 us
    ppermute x3, starting transfers between devices, factor_over_devices(): lax.ppermute(own, 'pts', xor_pairs(pts, d))  3.55 us
    ppermute x3, waiting for transfers between devices, factor_over_devices(): lax.ppermute(total, 'tm', xor_pairs(tm, d))  3.17 us
  transfers between devices with their start and end apart: 23, of which 13 were waited for; matrix products, arithmetic and copies ran while one was open for 4% of the time, Pallas kernels for 6%

profile of v4, /device:TPU:0, one launch (start us, length us, event | category | flops | bytes accessed | tf_op | source)
XLA Modules:
  0.0 88.0 jit_solution(14232974996190403205)
XLA Ops:
  0.6 0.0 copy-start.1
  0.6 0.0 copy-start
  0.7 1.0 %constant_dynamic-slice_fusion.9 = f32[128,512]{1,0:T(8,128)S(1)} fusion(f32[128,4096]{1,0:T(8,128)} %param.3, s32[]{:T(128)S(6)} %select_n.30), kind=kLoop, calls=%fused_computation.9 | loop fusion | bytes 524292 | tf_op jit(solution)/shard_map/dynamic_slice | solution.py:463
  1.6 4.6 %collective-permute-start = (f32[128,512]{1,0:T(8,128)S(1)}, f32[128,512]{1,0:T(8,128)S(1)}, u32[]{:S(2)}, u32[]{:S(2)}) collective-permute-start(f32[128,512]{1,0:T(8,128)S(1)} %constant_dynamic-slice_fusion.9), channel_id=1, source_target_pairs={{0,28},{4,24},{8,20},{12,16},{16,12},{20,8},{24,4},{28,0},{1,29},{... | collective-permute-start | bytes 786440 | tf_op jit(solution)/shard_map/ppermute | solution.py:466
  6.2 1.0 %constant_dynamic-slice_fusion.6 = (f32[128,384]{1,0:T(8,128)S(1)}, f32[128,384]{1,0:T(8,128)S(1)}) fusion(f32[128,4096]{1,0:T(8,128)} %param.3, s32[]{:T(128)S(6)} %select_n.33, s32[]{:T(128)S(6)} %select_n.31), kind=kLoop, calls=%fused_computation.6 | loop fusion | bytes 786440 | tf_op jit(solution)/shard_map/dynamic_slice | solution.py:463
  7.2 0.1 collective-permute-start.3
  7.4 1.4 %constant_dynamic-slice_fusion.2 = (f32[128,512]{1,0:T(8,128)S(1)}, f32[128,512]{1,0:T(8,128)S(1)}, f32[128,512]{1,0:T(8,128)S(1)}, f32[128,512]{1,0:T(8,128)S(1)}, f32[128,512]{1,0:T(8,128)S(1)}) fusion(f32[128,4096]{1,0:T(8,128)} %param.3, s32[]{:T(128)S(6)} %select_n.37, s32[]{:T(128)S(6)} %select_n.36, s32[]{:T(128)S(6)} %select_n.35, s32[]{:T(128)S(6)} %select_n.34, ...), kind=kLoop, calls=%fused_computation.2 | loop fusion | bytes 2621460 | tf_op jit(solution)/shard_map/dynamic_slice | solution.py:463
  8.7 0.7 collective-permute-start.6
  9.5 1.6 %collective-permute-start.1 = (f32[128,384]{1,0:T(8,128)S(1)}, f32[128,384]{1,0:T(8,128)S(1)}, u32[]{:S(2)}, u32[]{:S(2)}) collective-permute-start(f32[128,384]{1,0:T(8,128)S(1)} %get-tuple-element.38), channel_id=1, source_target_pairs={{0,24},{4,28},{8,16},{12,20},{16,8},{20,12},{24,0},{28,4},{1,25},{... | collective-permute-start | bytes 589832 | tf_op jit(solution)/shard_map/ppermute | solution.py:466
  11.1 1.6 %collective-permute-start.5 = (f32[128,512]{1,0:T(8,128)S(1)}, f32[128,512]{1,0:T(8,128)S(1)}, u32[]{:S(2)}, u32[]{:S(2)}) collective-permute-start(f32[128,512]{1,0:T(8,128)S(1)} %get-tuple-element.34), channel_id=1, source_target_pairs={{0,8},{4,12},{8,0},{12,4},{16,24},{20,28},{24,16},{28,20},{1,9},{5... | collective-permute-start | bytes 786440 | tf_op jit(solution)/shard_map/ppermute | solution.py:466
  12.6 18.5 %collective-permute-done.3.refs_3_ = f32[128,384]{1,0:T(8,128)S(1)} collective-permute-done((f32[128,384]{1,0:T(8,128)S(1)}, f32[128,384]{1,0:T(8,128)S(1)}, u32[]{:S(2)}, u32[]{:S(2)}) %collective-permute-start.3) | collective-permute-done | bytes 196640 | tf_op jit(solution)/shard_map/ppermute | solution.py:466
  31.2 0.0 collective-permute-start.4
  31.2 0.0 collective-permute-done.refs_0_
  31.2 2.7 %collective-permute-start.2 = (f32[128,512]{1,0:T(8,128)S(1)}, f32[128,512]{1,0:T(8,128)S(1)}, u32[]{:S(2)}, u32[]{:S(2)}) collective-permute-start(f32[128,512]{1,0:T(8,128)S(1)} %get-tuple-element.36), channel_id=1, source_target_pairs={{0,20},{4,16},{8,28},{12,24},{16,4},{20,0},{24,12},{28,8},{1,21},{... | collective-permute-start | bytes 786440 | tf_op jit(solution)/shard_map/ppermute | solution.py:466
  33.8 0.9 %constant_dynamic-slice_fusion = (f32[128,128]{1,0:T(8,128)S(1)}, f32[128,128]{1,0:T(8,128)S(1)}) fusion(f32[128,4096]{1,0:T(8,128)} %param.3, s32[]{:T(128)S(6)} %select_n.39, s32[]{:T(128)S(6)} %select_n.38), kind=kLoop, calls=%fused_computation | loop fusion | bytes 262152 | tf_op jit(solution)/shard_map/dynamic_slice | solution.py:463
  34.7 0.0 collective-permute-done.1.refs_1_
  34.7 2.1 %collective-permute-start.7 = (f32[128,128]{1,0:T(8,128)S(1)}, f32[128,128]{1,0:T(8,128)S(1)}, u32[]{:S(2)}, u32[]{:S(2)}) collective-permute-start(f32[128,128]{1,0:T(8,128)S(1)} %get-tuple-element.17), channel_id=1, source_target_pairs={{0,16},{4,20},{8,24},{12,28},{16,0},{20,4},{24,8},{28,12},{1,17},{... | collective-permute-start | bytes 196616 | tf_op jit(solution)/shard_map/ppermute | solution.py:466
  36.8 0.0 collective-permute-done.6.refs_6_
  36.8 1.5 %collective-permute-start.8 = (f32[128,128]{1,0:T(8,128)S(1)}, f32[128,128]{1,0:T(8,128)S(1)}, u32[]{:S(2)}, u32[]{:S(2)}) collective-permute-start(f32[128,128]{1,0:T(8,128)S(1)} %get-tuple-element.18), channel_id=1, source_target_pairs={{0,24},{4,28},{8,16},{12,20},{16,8},{20,12},{24,0},{28,4},{1,25},{... | collective-permute-start | bytes 196616 | tf_op jit(solution)/shard_map/ppermute | solution.py:466
  38.3 0.0 copy-done.1
  38.3 0.0 collective-permute-done.5.refs_5_
  38.3 6.3 %collective-permute-done.4.refs_4_ = f32[128,512]{1,0:T(8,128)S(1)} collective-permute-done((f32[128,512]{1,0:T(8,128)S(1)}, f32[128,512]{1,0:T(8,128)S(1)}, u32[]{:S(2)}, u32[]{:S(2)}) %collective-permute-start.4) | collective-permute-done | bytes 262176 | tf_op jit(solution)/shard_map/ppermute | solution.py:466
  44.6 4.6 %collective-permute-done.2.refs_2_ = f32[128,512]{1,0:T(8,128)S(1)} collective-permute-done((f32[128,512]{1,0:T(8,128)S(1)}, f32[128,512]{1,0:T(8,128)S(1)}, u32[]{:S(2)}, u32[]{:S(2)}) %collective-permute-start.2) | collective-permute-done | bytes 262176 | tf_op jit(solution)/shard_map/ppermute | solution.py:466
  49.2 1.7 %collective-permute-done.7.refs_8_ = f32[128,128]{1,0:T(8,128)S(1)} collective-permute-done((f32[128,128]{1,0:T(8,128)S(1)}, f32[128,128]{1,0:T(8,128)S(1)}, u32[]{:S(2)}, u32[]{:S(2)}) %collective-permute-start.7) | collective-permute-done | bytes 65568 | tf_op jit(solution)/shard_map/ppermute | solution.py:466
  50.9 0.0 collective-permute-done.8.refs_9_
  50.9 0.0 copy-done
  50.9 4.4 %shard_map.50 = (f32[64,32,512]{2,1,0:T(8,128)S(1)}, f32[4,2,32,128]{3,2,1,0:T(8,128)S(1)}) custom-call(f32[64,64]{1,0:T(8,128)S(1)} %copy-done, f32[1,512]{1,0:T(1,128)S(1)} %bitcast.6, f32[128,512]{1,0:T(8,128)S(1)} %collective-permute-done.refs_0_, f32[128,384]{1,0:T(8,128)S(1)} %collective-permute-done.1.refs_1_, ...), custom_call_target="tpu_custom_call" | custom-call | tf_op jit(solution)/shard_map/pallas_call | solution.py:417
  55.3 0.1 collective-permute-start.9
  55.3 1.9 %shard_map.52.keep_ref = f32[3,2,32,128]{3,2,1,0:T(8,128)S(1)} custom-call(f32[64,32,512]{2,1,0:T(8,128)S(1)} %get-tuple-element.19.spec_ref.refs_4_), custom_call_target="tpu_custom_call" | custom-call | tf_op jit(solution)/shard_map/pallas_call | solution.py:417
  57.3 0.0 collective-permute-done.9.got_ref
  57.3 2.5 %collective-permute-start.10 = (f32[2,32,128]{2,1,0:T(8,128)S(1)}, f32[2,32,128]{2,1,0:T(8,128)S(1)}, u32[]{:S(2)}, u32[]{:S(2)}) collective-permute-start(f32[2,32,128]{2,1,0:T(8,128)S(1)} %get-tuple-element.21), channel_id=1, source_target_pairs={{0,3},{1,2},{2,1},{3,0},{4,7},{5,6},{6,5},{7,4},{8,11},{9,10},{10,... | collective-permute-start | bytes 98312 | tf_op jit(solution)/shard_map/ppermute | solution.py:444
  59.8 0.5 collective-permute-start.11
  60.3 0.5 collective-permute-start.12
  60.9 1.0 %shard_map.51.refs_0_ = f32[2,32,128]{2,1,0:T(8,128)S(1)} custom-call(f32[64,32,512]{2,1,0:T(8,128)S(1)} %get-tuple-element.19.spec_ref.refs_4_, f32[4,2,32,128]{3,2,1,0:T(8,128)S(1)} %collective-permute-done.9.got_ref), custom_call_target="tpu_custom_call" | custom-call | tf_op jit(solution)/shard_map/pallas_call | solution.py:417
  61.9 0.3 collective-permute-done.10.refs_1_
  62.2 1.6 %collective-permute-done.11.refs_2_ = f32[2,32,128]{2,1,0:T(8,128)S(1)} collective-permute-done((f32[2,32,128]{2,1,0:T(8,128)S(1)}, f32[2,32,128]{2,1,0:T(8,128)S(1)}, u32[]{:S(2)}, u32[]{:S(2)}) %collective-permute-start.11) | collective-permute-done | bytes 32800 | tf_op jit(solution)/shard_map/ppermute | solution.py:444
  63.7 0.5 collective-permute-done.12.refs_3_
  64.3 2.5 %collective-permute-start.15 = (f32[2,32,128]{2,1,0:T(8,128)S(1)}, f32[2,32,128]{2,1,0:T(8,128)S(1)}, u32[]{:S(2)}, u32[]{:S(2)}) collective-permute-start(f32[2,32,128]{2,1,0:T(8,128)S(1)} %shard_map.54.refs_0_), channel_id=1, source_target_pairs={{0,24},{4,28},{8,16},{12,20},{16,8},{20,12},{24,0},{28,4},{1,25},{... | collective-permute-start | bytes 98312 | tf_op jit(solution)/shard_map/ppermute | solution.py:450
  66.8 0.9 collective-permute-start.14
  67.6 1.1 %collective-permute-start.13 = (f32[2,32,128]{2,1,0:T(8,128)S(1)}, f32[2,32,128]{2,1,0:T(8,128)S(1)}, u32[]{:S(2)}, u32[]{:S(2)}) collective-permute-start(f32[2,32,128]{2,1,0:T(8,128)S(1)} %shard_map.54.refs_0_), channel_id=1, source_target_pairs={{0,8},{4,12},{8,0},{12,4},{16,24},{20,28},{24,16},{28,20},{1,9},{5... | collective-permute-start | bytes 98312 | tf_op jit(solution)/shard_map/ppermute | solution.py:450
  68.7 1.5 %collective-permute-done.15.refs_3_ = f32[2,32,128]{2,1,0:T(8,128)S(1)} collective-permute-done((f32[2,32,128]{2,1,0:T(8,128)S(1)}, f32[2,32,128]{2,1,0:T(8,128)S(1)}, u32[]{:S(2)}, u32[]{:S(2)}) %collective-permute-start.15) | collective-permute-done | bytes 32800 | tf_op jit(solution)/shard_map/ppermute | solution.py:450
  70.2 1.5 %collective-permute-done.14.refs_2_ = f32[2,32,128]{2,1,0:T(8,128)S(1)} collective-permute-done((f32[2,32,128]{2,1,0:T(8,128)S(1)}, f32[2,32,128]{2,1,0:T(8,128)S(1)}, u32[]{:S(2)}, u32[]{:S(2)}) %collective-permute-start.14) | collective-permute-done | bytes 32800 | tf_op jit(solution)/shard_map/ppermute | solution.py:450
  71.7 0.2 collective-permute-done.13.refs_1_
  71.9 3.8 %shard_map.55.refs_0_.refs_5_ = f32[2,32,128]{2,1,0:T(8,128)S(1)} custom-call(f32[2,32,128]{2,1,0:T(8,128)S(1)} %shard_map.54.refs_0_, f32[2,32,128]{2,1,0:T(8,128)S(1)} %collective-permute-done.13.refs_1_, f32[2,32,128]{2,1,0:T(8,128)S(1)} %collective-permute-done.14.refs_2_, f32[2,32,128]{2,1,0:T(8,128)S(1)} %collective-permute-done.15.refs_3_), custom_call_target="tpu_custom_call" | custom-call | tf_op jit(solution)/shard_map/pallas_call | solution.py:417
  75.7 1.6 %collective-permute-start.21 = (f32[2,32,128]{2,1,0:T(8,128)S(1)}, f32[2,32,128]{2,1,0:T(8,128)S(1)}, u32[]{:S(2)}, u32[]{:S(2)}) collective-permute-start(f32[2,32,128]{2,1,0:T(8,128)S(1)} %shard_map.55.refs_0_.refs_5_), channel_id=1, source_target_pairs={{0,3},{1,2},{2,1},{3,0},{4,7},{5,6},{6,5},{7,4},{8,11},{9,10},{10,... | collective-permute-start | bytes 98312 | tf_op jit(solution)/shard_map/ppermute | solution.py:452
  77.3 0.5 collective-permute-start.19
  77.8 1.5 %collective-permute-start.17 = (f32[2,32,128]{2,1,0:T(8,128)S(1)}, f32[2,32,128]{2,1,0:T(8,128)S(1)}, u32[]{:S(2)}, u32[]{:S(2)}) collective-permute-start(f32[2,32,128]{2,1,0:T(8,128)S(1)} %shard_map.55.refs_0_.refs_5_), channel_id=1, source_target_pairs={{0,1},{1,0},{2,3},{3,2},{4,5},{5,4},{6,7},{7,6},{8,9},{9,8},{10,11... | collective-permute-start | bytes 98312 | tf_op jit(solution)/shard_map/ppermute | solution.py:452
  79.2 0.0 collective-permute-start.16
  79.3 1.3 %collective-permute-done.21.refs_3_.refs_8_ = f32[2,32,128]{2,1,0:T(8,128)S(1)} collective-permute-done((f32[2,32,128]{2,1,0:T(8,128)S(1)}, f32[2,32,128]{2,1,0:T(8,128)S(1)}, u32[]{:S(2)}, u32[]{:S(2)}) %collective-permute-start.21) | collective-permute-done | bytes 32800 | tf_op jit(solution)/shard_map/ppermute | solution.py:452
  80.6 0.0 collective-permute-start.22
  80.6 0.6 collective-permute-done.19.refs_2_.refs_7_
  81.2 0.0 collective-permute-start.20
  81.2 0.5 collective-permute-done.17.refs_1_.refs_6_
  81.7 0.0 collective-permute-start.18
  81.7 2.3 %shard_map.56 = (f32[33,31,8,128]{3,2,1,0:T(8,128)}, f32[32,512]{1,0:T(8,128)S(1)}) custom-call(f32[2,32,128]{2,1,0:T(8,128)S(1)} %shard_map.55.refs_0_.refs_5_, f32[2,32,128]{2,1,0:T(8,128)S(1)} %collective-permute-done.17.refs_1_.refs_6_, f32[2,32,128]{2,1,0:T(8,128)S(1)} %collective-permute-done.19.refs_2_.refs_7_, ...), custom_call_target="tpu_custom_call" | custom-call | tf_op jit(solution)/shard_map/pallas_call | solution.py:417
  84.0 0.0 collective-permute-done.16.refs_0_
  84.0 0.0 collective-permute-done.22.refs_3_
  84.0 0.0 collective-permute-done.20.refs_2_
  84.0 0.0 collective-permute-done.18.refs_1_
  84.0 2.4 %shard_map.57 = (f32[33,31,8,128]{3,2,1,0:T(8,128)}, f32[2,33,31,31]{3,2,1,0:T(8,128)S(1)}) custom-call(f32[2,32,128]{2,1,0:T(8,128)S(1)} %collective-permute-done.16.refs_0_, f32[2,32,128]{2,1,0:T(8,128)S(1)} %collective-permute-done.18.refs_1_, f32[2,32,128]{2,1,0:T(8,128)S(1)} %collective-permute-done.20.refs_2_, ...), custom_call_target="tpu_custom_call", output_to_operand_aliasing={{0}: (10, {})} | custom-call | tf_op jit(solution)/shard_map/pallas_call | solution.py:417
  86.4 1.6 %copy.7 = f32[2,33,31,31]{1,0,3,2:T(2,128)} copy(f32[2,33,31,31]{3,2,1,0:T(8,128)S(1)} %get-tuple-element.29) | data formatting | bytes 507408
  (3 shorter events, 0.1 us)
Async XLA Ops:
  0.6 37.7 %copy-start.1 = (f32[512]{0:T(512)S(1)}, f32[512]{0:T(512)}, u32[]{:S(2)}) copy-start(f32[512]{0:T(512)} %param.4) | copy-start | bytes 6148
  0.6 50.2 %copy-start = (f32[64,64]{1,0:T(8,128)S(1)}, f32[64,64]{1,0:T(8,128)}, u32[]{:S(2)}) copy-start(f32[64,64]{1,0:T(8,128)} %constant.33.clone.table_ref) | copy-start | bytes 49156
  1.6 29.5 %collective-permute-start = (f32[128,512]{1,0:T(8,128)S(1)}, f32[128,512]{1,0:T(8,128)S(1)}, u32[]{:S(2)}, u32[]{:S(2)}) collective-permute-start(f32[128,512]{1,0:T(8,128)S(1)} %constant_dynamic-slice_fusion.9), channel_id=1, source_target_pairs={{0,28},{4,24},{8,20},{12,16},{16,12},{20,8},{24,4},{28,0},{1,29},{... | collective-permute-start | bytes 786440 | tf_op jit(solution)/shard_map/ppermute | solution.py:466
  7.2 23.9 %collective-permute-start.3 = (f32[128,384]{1,0:T(8,128)S(1)}, f32[128,384]{1,0:T(8,128)S(1)}, u32[]{:S(2)}, u32[]{:S(2)}) collective-permute-start(f32[128,384]{1,0:T(8,128)S(1)} %get-tuple-element.37), channel_id=1, source_target_pairs={{0,16},{4,20},{8,24},{12,28},{16,0},{20,4},{24,8},{28,12},{1,17},{... | collective-permute-start | bytes 589832 | tf_op jit(solution)/shard_map/ppermute | solution.py:466
  8.7 28.1 %collective-permute-start.6 = (f32[128,512]{1,0:T(8,128)S(1)}, f32[128,512]{1,0:T(8,128)S(1)}, u32[]{:S(2)}, u32[]{:S(2)}) collective-permute-start(f32[128,512]{1,0:T(8,128)S(1)} %get-tuple-element.33), channel_id=1, source_target_pairs={{0,4},{4,0},{8,12},{12,8},{16,20},{20,16},{24,28},{28,24},{1,5},{5... | collective-permute-start | bytes 786440 | tf_op jit(solution)/shard_map/ppermute | solution.py:466
  9.5 25.2 %collective-permute-start.1 = (f32[128,384]{1,0:T(8,128)S(1)}, f32[128,384]{1,0:T(8,128)S(1)}, u32[]{:S(2)}, u32[]{:S(2)}) collective-permute-start(f32[128,384]{1,0:T(8,128)S(1)} %get-tuple-element.38), channel_id=1, source_target_pairs={{0,24},{4,28},{8,16},{12,20},{16,8},{20,12},{24,0},{28,4},{1,25},{... | collective-permute-start | bytes 589832 | tf_op jit(solution)/shard_map/ppermute | solution.py:466
  11.1 27.3 %collective-permute-start.5 = (f32[128,512]{1,0:T(8,128)S(1)}, f32[128,512]{1,0:T(8,128)S(1)}, u32[]{:S(2)}, u32[]{:S(2)}) collective-permute-start(f32[128,512]{1,0:T(8,128)S(1)} %get-tuple-element.34), channel_id=1, source_target_pairs={{0,8},{4,12},{8,0},{12,4},{16,24},{20,28},{24,16},{28,20},{1,9},{5... | collective-permute-start | bytes 786440 | tf_op jit(solution)/shard_map/ppermute | solution.py:466
  31.2 13.5 %collective-permute-start.4 = (f32[128,512]{1,0:T(8,128)S(1)}, f32[128,512]{1,0:T(8,128)S(1)}, u32[]{:S(2)}, u32[]{:S(2)}) collective-permute-start(f32[128,512]{1,0:T(8,128)S(1)} %get-tuple-element.35), channel_id=1, source_target_pairs={{0,12},{4,8},{8,4},{12,0},{16,28},{20,24},{24,20},{28,16},{1,13},{... | collective-permute-start | bytes 786440 | tf_op jit(solution)/shard_map/ppermute | solution.py:466
  31.2 18.0 %collective-permute-start.2 = (f32[128,512]{1,0:T(8,128)S(1)}, f32[128,512]{1,0:T(8,128)S(1)}, u32[]{:S(2)}, u32[]{:S(2)}) collective-permute-start(f32[128,512]{1,0:T(8,128)S(1)} %get-tuple-element.36), channel_id=1, source_target_pairs={{0,20},{4,16},{8,28},{12,24},{16,4},{20,0},{24,12},{28,8},{1,21},{... | collective-permute-start | bytes 786440 | tf_op jit(solution)/shard_map/ppermute | solution.py:466
  34.7 16.2 %collective-permute-start.7 = (f32[128,128]{1,0:T(8,128)S(1)}, f32[128,128]{1,0:T(8,128)S(1)}, u32[]{:S(2)}, u32[]{:S(2)}) collective-permute-start(f32[128,128]{1,0:T(8,128)S(1)} %get-tuple-element.17), channel_id=1, source_target_pairs={{0,16},{4,20},{8,24},{12,28},{16,0},{20,4},{24,8},{28,12},{1,17},{... | collective-permute-start | bytes 196616 | tf_op jit(solution)/shard_map/ppermute | solution.py:466
  36.8 14.0 %collective-permute-start.8 = (f32[128,128]{1,0:T(8,128)S(1)}, f32[128,128]{1,0:T(8,128)S(1)}, u32[]{:S(2)}, u32[]{:S(2)}) collective-permute-start(f32[128,128]{1,0:T(8,128)S(1)} %get-tuple-element.18), channel_id=1, source_target_pairs={{0,24},{4,28},{8,16},{12,20},{16,8},{20,12},{24,0},{28,4},{1,25},{... | collective-permute-start | bytes 196616 | tf_op jit(solution)/shard_map/ppermute | solution.py:466
  55.3 2.0 %collective-permute-start.9 = (f32[4,2,32,128]{3,2,1,0:T(8,128)S(1)}, f32[4,2,32,128]{3,2,1,0:T(8,128)S(1)}, u32[]{:S(2)}, u32[]{:S(2)}) collective-permute-start(f32[4,2,32,128]{3,2,1,0:T(8,128)S(1)} %get-tuple-element.20), channel_id=1, source_target_pairs={{0,4},{4,0},{8,12},{12,8},{16,20},{20,16},{24,28},{28,24},{1,5},{5... | collective-permute-start | bytes 393224 | tf_op jit(solution)/shard_map/ppermute | solution.py:493
  57.3 4.9 %collective-permute-start.10 = (f32[2,32,128]{2,1,0:T(8,128)S(1)}, f32[2,32,128]{2,1,0:T(8,128)S(1)}, u32[]{:S(2)}, u32[]{:S(2)}) collective-permute-start(f32[2,32,128]{2,1,0:T(8,128)S(1)} %get-tuple-element.21), channel_id=1, source_target_pairs={{0,3},{1,2},{2,1},{3,0},{4,7},{5,6},{6,5},{7,4},{8,11},{9,10},{10,... | collective-permute-start | bytes 98312 | tf_op jit(solution)/shard_map/ppermute | solution.py:444
  59.8 3.9 %collective-permute-start.11 = (f32[2,32,128]{2,1,0:T(8,128)S(1)}, f32[2,32,128]{2,1,0:T(8,128)S(1)}, u32[]{:S(2)}, u32[]{:S(2)}) collective-permute-start(f32[2,32,128]{2,1,0:T(8,128)S(1)} %get-tuple-element.22), channel_id=1, source_target_pairs={{0,2},{1,3},{2,0},{3,1},{4,6},{5,7},{6,4},{7,5},{8,10},{9,11},{10,... | collective-permute-start | bytes 98312 | tf_op jit(solution)/shard_map/ppermute | solution.py:444
  60.3 3.9 %collective-permute-start.12 = (f32[2,32,128]{2,1,0:T(8,128)S(1)}, f32[2,32,128]{2,1,0:T(8,128)S(1)}, u32[]{:S(2)}, u32[]{:S(2)}) collective-permute-start(f32[2,32,128]{2,1,0:T(8,128)S(1)} %get-tuple-element.23), channel_id=1, source_target_pairs={{0,1},{1,0},{2,3},{3,2},{4,5},{5,4},{6,7},{7,6},{8,9},{9,8},{10,11... | collective-permute-start | bytes 98312 | tf_op jit(solution)/shard_map/ppermute | solution.py:444
  64.3 5.9 %collective-permute-start.15 = (f32[2,32,128]{2,1,0:T(8,128)S(1)}, f32[2,32,128]{2,1,0:T(8,128)S(1)}, u32[]{:S(2)}, u32[]{:S(2)}) collective-permute-start(f32[2,32,128]{2,1,0:T(8,128)S(1)} %shard_map.54.refs_0_), channel_id=1, source_target_pairs={{0,24},{4,28},{8,16},{12,20},{16,8},{20,12},{24,0},{28,4},{1,25},{... | collective-permute-start | bytes 98312 | tf_op jit(solution)/shard_map/ppermute | solution.py:450
  66.8 4.9 %collective-permute-start.14 = (f32[2,32,128]{2,1,0:T(8,128)S(1)}, f32[2,32,128]{2,1,0:T(8,128)S(1)}, u32[]{:S(2)}, u32[]{:S(2)}) collective-permute-start(f32[2,32,128]{2,1,0:T(8,128)S(1)} %shard_map.54.refs_0_), channel_id=1, source_target_pairs={{0,16},{4,20},{8,24},{12,28},{16,0},{20,4},{24,8},{28,12},{1,17},{... | collective-permute-start | bytes 98312 | tf_op jit(solution)/shard_map/ppermute | solution.py:450
  67.6 4.3 %collective-permute-start.13 = (f32[2,32,128]{2,1,0:T(8,128)S(1)}, f32[2,32,128]{2,1,0:T(8,128)S(1)}, u32[]{:S(2)}, u32[]{:S(2)}) collective-permute-start(f32[2,32,128]{2,1,0:T(8,128)S(1)} %shard_map.54.refs_0_), channel_id=1, source_target_pairs={{0,8},{4,12},{8,0},{12,4},{16,24},{20,28},{24,16},{28,20},{1,9},{5... | collective-permute-start | bytes 98312 | tf_op jit(solution)/shard_map/ppermute | solution.py:450
  75.7 4.9 %collective-permute-start.21 = (f32[2,32,128]{2,1,0:T(8,128)S(1)}, f32[2,32,128]{2,1,0:T(8,128)S(1)}, u32[]{:S(2)}, u32[]{:S(2)}) collective-permute-start(f32[2,32,128]{2,1,0:T(8,128)S(1)} %shard_map.55.refs_0_.refs_5_), channel_id=1, source_target_pairs={{0,3},{1,2},{2,1},{3,0},{4,7},{5,6},{6,5},{7,4},{8,11},{9,10},{10,... | collective-permute-start | bytes 98312 | tf_op jit(solution)/shard_map/ppermute | solution.py:452
  77.3 3.9 %collective-permute-start.19 = (f32[2,32,128]{2,1,0:T(8,128)S(1)}, f32[2,32,128]{2,1,0:T(8,128)S(1)}, u32[]{:S(2)}, u32[]{:S(2)}) collective-permute-start(f32[2,32,128]{2,1,0:T(8,128)S(1)} %shard_map.55.refs_0_.refs_5_), channel_id=1, source_target_pairs={{0,2},{1,3},{2,0},{3,1},{4,6},{5,7},{6,4},{7,5},{8,10},{9,11},{10,... | collective-permute-start | bytes 98312 | tf_op jit(solution)/shard_map/ppermute | solution.py:452
  77.8 3.9 %collective-permute-start.17 = (f32[2,32,128]{2,1,0:T(8,128)S(1)}, f32[2,32,128]{2,1,0:T(8,128)S(1)}, u32[]{:S(2)}, u32[]{:S(2)}) collective-permute-start(f32[2,32,128]{2,1,0:T(8,128)S(1)} %shard_map.55.refs_0_.refs_5_), channel_id=1, source_target_pairs={{0,1},{1,0},{2,3},{3,2},{4,5},{5,4},{6,7},{7,6},{8,9},{9,8},{10,11... | collective-permute-start | bytes 98312 | tf_op jit(solution)/shard_map/ppermute | solution.py:452
  79.2 4.7 %collective-permute-start.16 = (f32[2,32,128]{2,1,0:T(8,128)S(1)}, f32[2,32,128]{2,1,0:T(8,128)S(1)}, u32[]{:S(2)}, u32[]{:S(2)}) collective-permute-start(f32[2,32,128]{2,1,0:T(8,128)S(1)} %shard_map.55.refs_0_.refs_5_), channel_id=1, source_target_pairs={{0,4},{4,0},{8,12},{12,8},{16,20},{20,16},{24,28},{28,24},{1,5},{5... | collective-permute-start | bytes 98312 | tf_op jit(solution)/shard_map/ppermute | solution.py:453
  80.6 3.4 %collective-permute-start.22 = (f32[2,32,128]{2,1,0:T(8,128)S(1)}, f32[2,32,128]{2,1,0:T(8,128)S(1)}, u32[]{:S(2)}, u32[]{:S(2)}) collective-permute-start(f32[2,32,128]{2,1,0:T(8,128)S(1)} %collective-permute-done.21.refs_3_.refs_8_), channel_id=1, source_target_pairs={{0,4},{4,0},{8,12},{12,8},{16,20},{20,16},{24,28},{28,24},{1,5},{5... | collective-permute-start | bytes 98312 | tf_op jit(solution)/shard_map/ppermute | solution.py:453
  81.2 2.9 %collective-permute-start.20 = (f32[2,32,128]{2,1,0:T(8,128)S(1)}, f32[2,32,128]{2,1,0:T(8,128)S(1)}, u32[]{:S(2)}, u32[]{:S(2)}) collective-permute-start(f32[2,32,128]{2,1,0:T(8,128)S(1)} %collective-permute-done.19.refs_2_.refs_7_), channel_id=1, source_target_pairs={{0,4},{4,0},{8,12},{12,8},{16,20},{20,16},{24,28},{28,24},{1,5},{5... | collective-permute-start | bytes 98312 | tf_op jit(solution)/shard_map/ppermute | solution.py:453
  81.7 2.4 %collective-permute-start.18 = (f32[2,32,128]{2,1,0:T(8,128)S(1)}, f32[2,32,128]{2,1,0:T(8,128)S(1)}, u32[]{:S(2)}, u32[]{:S(2)}) collective-permute-start(f32[2,32,128]{2,1,0:T(8,128)S(1)} %collective-permute-done.17.refs_1_.refs_6_), channel_id=1, source_target_pairs={{0,4},{4,0},{8,12},{12,8},{16,20},{20,16},{24,28},{28,24},{1,5},{5... | collective-permute-start | bytes 98312 | tf_op jit(solution)/shard_map/ppermute | solution.py:453

commit v5 on v4

--- a/solution.py
+++ b/solution.py
@@ -467,7 +467,7 @@
 
     last = max(128, points // 4 // 128 * 128)
     body = points - last
-    parted = {tm // 2: tm - 1, 3 * tm // 4: tm - 1}
+    parted = {tm // 2 + 1: tm - 1, 3 * tm // 4: tm - 1}
     pieces = {}
     farthest = tm - 1
     sent = piece_of(snapshots, farthest, 0, points)

time: 88.3 us -> 88.3 us (level)
  no operation moved by 1% of the time
where the time goes in v5:
time: 88.3 us; the launch traced here: 88 us
  waiting for transfers between devices  39.3 us (45%)
  starting transfers between devices  26.2 us (30%)
  Pallas kernels  15.8 us (18%)
  local copies, waits for them, and re-layouts  5.88 us (7%)
    ppermute x9, waiting for transfers between devices, exchanged(): return lax.ppermute(piece, 'tm', xor_pairs(tm, d))  31.2 us
    pallas_call x8, Pallas kernels, call(): pl.pallas_call(body, out_shape=out_shape, in_specs=[pl.BlockSpec(memory_s...  15.8 us
    ppermute x9, starting transfers between devices, exchanged(): return lax.ppermute(piece, 'tm', xor_pairs(tm, d))  14.4 us
    ppermute x3, starting transfers between devices, factor_over_devices(): lax.ppermute(total, 'tm', xor_pairs(tm, d))  4.45 us
    dynamic_slice x4, local copies, waits for them, and re-layouts, piece_of(): return lax.dynamic_slice_in_dim(array, (me ^ d) * points + start, size, 1)  4.29 us
    ppermute x3, starting transfers between devices, factor_over_devices(): lax.ppermute(parts[d - 1], 'pts', xor_pairs(pts, d))  3.55 us
    ppermute x3, starting transfers between devices, factor_over_devices(): lax.ppermute(own, 'pts', xor_pairs(pts, d))  3.55 us
    ppermute x3, waiting for transfers between devices, factor_over_devices(): lax.ppermute(total, 'tm', xor_pairs(tm, d))  3.31 us
  transfers between devices with their start and end apart: 23, of which 13 were waited for; matrix products, arithmetic and copies ran while one was open for 4% of the time, Pallas kernels for 6%

profile of v5, /device:TPU:0, one launch (start us, length us, event | category | flops | bytes accessed | tf_op | source)
XLA Modules:
  0.0 88.0 jit_solution(5172191416547555289)
XLA Ops:
  0.6 0.0 copy-start.1
  0.6 0.0 copy-start
  0.7 1.0 %constant_dynamic-slice_fusion.9 = f32[128,512]{1,0:T(8,128)S(1)} fusion(f32[128,4096]{1,0:T(8,128)} %param.3, s32[]{:T(128)S(6)} %select_n.30), kind=kLoop, calls=%fused_computation.9 | loop fusion | bytes 524292 | tf_op jit(solution)/shard_map/dynamic_slice | solution.py:463
  1.6 4.6 %collective-permute-start = (f32[128,512]{1,0:T(8,128)S(1)}, f32[128,512]{1,0:T(8,128)S(1)}, u32[]{:S(2)}, u32[]{:S(2)}) collective-permute-start(f32[128,512]{1,0:T(8,128)S(1)} %constant_dynamic-slice_fusion.9), channel_id=1, source_target_pairs={{0,28},{4,24},{8,20},{12,16},{16,12},{20,8},{24,4},{28,0},{1,29},{... | collective-permute-start | bytes 786440 | tf_op jit(solution)/shard_map/ppermute | solution.py:466
  6.2 1.0 %constant_dynamic-slice_fusion.7 = (f32[128,384]{1,0:T(8,128)S(1)}, f32[128,384]{1,0:T(8,128)S(1)}) fusion(f32[128,4096]{1,0:T(8,128)} %param.3, s32[]{:T(128)S(6)} %select_n.32, s32[]{:T(128)S(6)} %select_n.31), kind=kLoop, calls=%fused_computation.7 | loop fusion | bytes 786440 | tf_op jit(solution)/shard_map/dynamic_slice | solution.py:463
  7.2 0.1 collective-permute-start.2
  7.4 1.4 %constant_dynamic-slice_fusion.2 = (f32[128,512]{1,0:T(8,128)S(1)}, f32[128,512]{1,0:T(8,128)S(1)}, f32[128,512]{1,0:T(8,128)S(1)}, f32[128,512]{1,0:T(8,128)S(1)}, f32[128,512]{1,0:T(8,128)S(1)}) fusion(f32[128,4096]{1,0:T(8,128)} %param.3, s32[]{:T(128)S(6)} %select_n.37, s32[]{:T(128)S(6)} %select_n.36, s32[]{:T(128)S(6)} %select_n.35, s32[]{:T(128)S(6)} %select_n.34, ...), kind=kLoop, calls=%fused_computation.2 | loop fusion | bytes 2621460 | tf_op jit(solution)/shard_map/dynamic_slice | solution.py:463
  8.7 0.7 collective-permute-start.6
  9.5 1.5 %collective-permute-start.1 = (f32[128,384]{1,0:T(8,128)S(1)}, f32[128,384]{1,0:T(8,128)S(1)}, u32[]{:S(2)}, u32[]{:S(2)}) collective-permute-start(f32[128,384]{1,0:T(8,128)S(1)} %get-tuple-element.38), channel_id=1, source_target_pairs={{0,24},{4,28},{8,16},{12,20},{16,8},{20,12},{24,0},{28,4},{1,25},{... | collective-permute-start | bytes 589832 | tf_op jit(solution)/shard_map/ppermute | solution.py:466
  11.0 1.6 %collective-permute-start.5 = (f32[128,512]{1,0:T(8,128)S(1)}, f32[128,512]{1,0:T(8,128)S(1)}, u32[]{:S(2)}, u32[]{:S(2)}) collective-permute-start(f32[128,512]{1,0:T(8,128)S(1)} %get-tuple-element.34), channel_id=1, source_target_pairs={{0,8},{4,12},{8,0},{12,4},{16,24},{20,28},{24,16},{28,20},{1,9},{5... | collective-permute-start | bytes 786440 | tf_op jit(solution)/shard_map/ppermute | solution.py:466
  12.6 18.3 %collective-permute-done.2.refs_2_ = f32[128,384]{1,0:T(8,128)S(1)} collective-permute-done((f32[128,384]{1,0:T(8,128)S(1)}, f32[128,384]{1,0:T(8,128)S(1)}, u32[]{:S(2)}, u32[]{:S(2)}) %collective-permute-start.2) | collective-permute-done | bytes 196640 | tf_op jit(solution)/shard_map/ppermute | solution.py:466
  30.9 0.0 collective-permute-start.4
  30.9 0.0 collective-permute-done.refs_0_
  30.9 2.9 %collective-permute-start.3 = (f32[128,512]{1,0:T(8,128)S(1)}, f32[128,512]{1,0:T(8,128)S(1)}, u32[]{:S(2)}, u32[]{:S(2)}) collective-permute-start(f32[128,512]{1,0:T(8,128)S(1)} %get-tuple-element.36), channel_id=1, source_target_pairs={{0,16},{4,20},{8,24},{12,28},{16,0},{20,4},{24,8},{28,12},{1,17},{... | collective-permute-start | bytes 786440 | tf_op jit(solution)/shard_map/ppermute | solution.py:466
  33.8 0.9 %constant_dynamic-slice_fusion = (f32[128,128]{1,0:T(8,128)S(1)}, f32[128,128]{1,0:T(8,128)S(1)}) fusion(f32[128,4096]{1,0:T(8,128)} %param.3, s32[]{:T(128)S(6)} %select_n.39, s32[]{:T(128)S(6)} %select_n.38), kind=kLoop, calls=%fused_computation | loop fusion | bytes 262152 | tf_op jit(solution)/shard_map/dynamic_slice | solution.py:463
  34.7 0.0 collective-permute-done.1.refs_1_
  34.7 1.9 %collective-permute-start.7 = (f32[128,128]{1,0:T(8,128)S(1)}, f32[128,128]{1,0:T(8,128)S(1)}, u32[]{:S(2)}, u32[]{:S(2)}) collective-permute-start(f32[128,128]{1,0:T(8,128)S(1)} %get-tuple-element.17), channel_id=1, source_target_pairs={{0,20},{4,16},{8,28},{12,24},{16,4},{20,0},{24,12},{28,8},{1,21},{... | collective-permute-start | bytes 196616 | tf_op jit(solution)/shard_map/ppermute | solution.py:466
  36.5 0.0 collective-permute-done.6.refs_6_
  36.5 1.2 %collective-permute-start.8 = (f32[128,128]{1,0:T(8,128)S(1)}, f32[128,128]{1,0:T(8,128)S(1)}, u32[]{:S(2)}, u32[]{:S(2)}) collective-permute-start(f32[128,128]{1,0:T(8,128)S(1)} %get-tuple-element.18), channel_id=1, source_target_pairs={{0,24},{4,28},{8,16},{12,20},{16,8},{20,12},{24,0},{28,4},{1,25},{... | collective-permute-start | bytes 196616 | tf_op jit(solution)/shard_map/ppermute | solution.py:466
  37.8 0.0 copy-done.1
  37.8 0.0 collective-permute-done.5.refs_5_
  37.8 6.3 %collective-permute-done.4.refs_4_ = f32[128,512]{1,0:T(8,128)S(1)} collective-permute-done((f32[128,512]{1,0:T(8,128)S(1)}, f32[128,512]{1,0:T(8,128)S(1)}, u32[]{:S(2)}, u32[]{:S(2)}) %collective-permute-start.4) | collective-permute-done | bytes 262176 | tf_op jit(solution)/shard_map/ppermute | solution.py:466
  44.1 5.4 %collective-permute-done.3.refs_3_ = f32[128,512]{1,0:T(8,128)S(1)} collective-permute-done((f32[128,512]{1,0:T(8,128)S(1)}, f32[128,512]{1,0:T(8,128)S(1)}, u32[]{:S(2)}, u32[]{:S(2)}) %collective-permute-start.3) | collective-permute-done | bytes 262176 | tf_op jit(solution)/shard_map/ppermute | solution.py:466
  49.5 1.1 %collective-permute-done.7.refs_8_ = f32[128,128]{1,0:T(8,128)S(1)} collective-permute-done((f32[128,128]{1,0:T(8,128)S(1)}, f32[128,128]{1,0:T(8,128)S(1)}, u32[]{:S(2)}, u32[]{:S(2)}) %collective-permute-start.7) | collective-permute-done | bytes 65568 | tf_op jit(solution)/shard_map/ppermute | solution.py:466
  50.6 0.0 collective-permute-done.8.refs_9_
  50.6 0.0 copy-done
  50.6 4.4 %shard_map.50 = (f32[64,32,512]{2,1,0:T(8,128)S(1)}, f32[4,2,32,128]{3,2,1,0:T(8,128)S(1)}) custom-call(f32[64,64]{1,0:T(8,128)S(1)} %copy-done, f32[1,512]{1,0:T(1,128)S(1)} %bitcast.6, f32[128,512]{1,0:T(8,128)S(1)} %collective-permute-done.refs_0_, f32[128,384]{1,0:T(8,128)S(1)} %collective-permute-done.1.refs_1_, ...), custom_call_target="tpu_custom_call" | custom-call | tf_op jit(solution)/shard_map/pallas_call | solution.py:417
  55.0 0.2 collective-permute-start.9
  55.2 1.9 %shard_map.52.keep_ref = f32[3,2,32,128]{3,2,1,0:T(8,128)S(1)} custom-call(f32[64,32,512]{2,1,0:T(8,128)S(1)} %get-tuple-element.19.spec_ref.refs_4_), custom_call_target="tpu_custom_call" | custom-call | tf_op jit(solution)/shard_map/pallas_call | solution.py:417
  57.1 0.0 collective-permute-done.9.got_ref
  57.1 2.5 %collective-permute-start.10 = (f32[2,32,128]{2,1,0:T(8,128)S(1)}, f32[2,32,128]{2,1,0:T(8,128)S(1)}, u32[]{:S(2)}, u32[]{:S(2)}) collective-permute-start(f32[2,32,128]{2,1,0:T(8,128)S(1)} %get-tuple-element.21), channel_id=1, source_target_pairs={{0,3},{1,2},{2,1},{3,0},{4,7},{5,6},{6,5},{7,4},{8,11},{9,10},{10,... | collective-permute-start | bytes 98312 | tf_op jit(solution)/shard_map/ppermute | solution.py:444
  59.6 0.5 collective-permute-start.11
  60.2 0.5 collective-permute-start.12
  60.7 1.0 %shard_map.51.refs_0_ = f32[2,32,128]{2,1,0:T(8,128)S(1)} custom-call(f32[64,32,512]{2,1,0:T(8,128)S(1)} %get-tuple-element.19.spec_ref.refs_4_, f32[4,2,32,128]{3,2,1,0:T(8,128)S(1)} %collective-permute-done.9.got_ref), custom_call_target="tpu_custom_call" | custom-call | tf_op jit(solution)/shard_map/pallas_call | solution.py:417
  61.7 0.3 collective-permute-done.10.refs_1_
  62.0 1.5 %collective-permute-done.11.refs_2_ = f32[2,32,128]{2,1,0:T(8,128)S(1)} collective-permute-done((f32[2,32,128]{2,1,0:T(8,128)S(1)}, f32[2,32,128]{2,1,0:T(8,128)S(1)}, u32[]{:S(2)}, u32[]{:S(2)}) %collective-permute-start.11) | collective-permute-done | bytes 32800 | tf_op jit(solution)/shard_map/ppermute | solution.py:444
  63.6 0.5 collective-permute-done.12.refs_3_
  64.1 2.6 %collective-permute-start.15 = (f32[2,32,128]{2,1,0:T(8,128)S(1)}, f32[2,32,128]{2,1,0:T(8,128)S(1)}, u32[]{:S(2)}, u32[]{:S(2)}) collective-permute-start(f32[2,32,128]{2,1,0:T(8,128)S(1)} %shard_map.54.refs_0_), channel_id=1, source_target_pairs={{0,24},{4,28},{8,16},{12,20},{16,8},{20,12},{24,0},{28,4},{1,25},{... | collective-permute-start | bytes 98312 | tf_op jit(solution)/shard_map/ppermute | solution.py:450
  66.8 0.9 collective-permute-start.14
  67.6 1.0 %collective-permute-start.13 = (f32[2,32,128]{2,1,0:T(8,128)S(1)}, f32[2,32,128]{2,1,0:T(8,128)S(1)}, u32[]{:S(2)}, u32[]{:S(2)}) collective-permute-start(f32[2,32,128]{2,1,0:T(8,128)S(1)} %shard_map.54.refs_0_), channel_id=1, source_target_pairs={{0,8},{4,12},{8,0},{12,4},{16,24},{20,28},{24,16},{28,20},{1,9},{5... | collective-permute-start | bytes 98312 | tf_op jit(solution)/shard_map/ppermute | solution.py:450
  68.6 1.7 %collective-permute-done.15.refs_3_ = f32[2,32,128]{2,1,0:T(8,128)S(1)} collective-permute-done((f32[2,32,128]{2,1,0:T(8,128)S(1)}, f32[2,32,128]{2,1,0:T(8,128)S(1)}, u32[]{:S(2)}, u32[]{:S(2)}) %collective-permute-start.15) | collective-permute-done | bytes 32800 | tf_op jit(solution)/shard_map/ppermute | solution.py:450
  70.3 1.4 %collective-permute-done.14.refs_2_ = f32[2,32,128]{2,1,0:T(8,128)S(1)} collective-permute-done((f32[2,32,128]{2,1,0:T(8,128)S(1)}, f32[2,32,128]{2,1,0:T(8,128)S(1)}, u32[]{:S(2)}, u32[]{:S(2)}) %collective-permute-start.14) | collective-permute-done | bytes 32800 | tf_op jit(solution)/shard_map/ppermute | solution.py:450
  71.7 0.2 collective-permute-done.13.refs_1_
  71.9 3.8 %shard_map.55.refs_0_.refs_5_ = f32[2,32,128]{2,1,0:T(8,128)S(1)} custom-call(f32[2,32,128]{2,1,0:T(8,128)S(1)} %shard_map.54.refs_0_, f32[2,32,128]{2,1,0:T(8,128)S(1)} %collective-permute-done.13.refs_1_, f32[2,32,128]{2,1,0:T(8,128)S(1)} %collective-permute-done.14.refs_2_, f32[2,32,128]{2,1,0:T(8,128)S(1)} %collective-permute-done.15.refs_3_), custom_call_target="tpu_custom_call" | custom-call | tf_op jit(solution)/shard_map/pallas_call | solution.py:417
  75.7 1.6 %collective-permute-start.21 = (f32[2,32,128]{2,1,0:T(8,128)S(1)}, f32[2,32,128]{2,1,0:T(8,128)S(1)}, u32[]{:S(2)}, u32[]{:S(2)}) collective-permute-start(f32[2,32,128]{2,1,0:T(8,128)S(1)} %shard_map.55.refs_0_.refs_5_), channel_id=1, source_target_pairs={{0,3},{1,2},{2,1},{3,0},{4,7},{5,6},{6,5},{7,4},{8,11},{9,10},{10,... | collective-permute-start | bytes 98312 | tf_op jit(solution)/shard_map/ppermute | solution.py:452
  77.3 0.5 collective-permute-start.19
  77.8 1.5 %collective-permute-start.17 = (f32[2,32,128]{2,1,0:T(8,128)S(1)}, f32[2,32,128]{2,1,0:T(8,128)S(1)}, u32[]{:S(2)}, u32[]{:S(2)}) collective-permute-start(f32[2,32,128]{2,1,0:T(8,128)S(1)} %shard_map.55.refs_0_.refs_5_), channel_id=1, source_target_pairs={{0,1},{1,0},{2,3},{3,2},{4,5},{5,4},{6,7},{7,6},{8,9},{9,8},{10,11... | collective-permute-start | bytes 98312 | tf_op jit(solution)/shard_map/ppermute | solution.py:452
  79.2 0.0 collective-permute-start.16
  79.3 1.3 %collective-permute-done.21.refs_3_.refs_8_ = f32[2,32,128]{2,1,0:T(8,128)S(1)} collective-permute-done((f32[2,32,128]{2,1,0:T(8,128)S(1)}, f32[2,32,128]{2,1,0:T(8,128)S(1)}, u32[]{:S(2)}, u32[]{:S(2)}) %collective-permute-start.21) | collective-permute-done | bytes 32800 | tf_op jit(solution)/shard_map/ppermute | solution.py:452
  80.6 0.0 collective-permute-start.22
  80.6 0.6 collective-permute-done.19.refs_2_.refs_7_
  81.2 0.0 collective-permute-start.20
  81.2 0.5 collective-permute-done.17.refs_1_.refs_6_
  81.7 0.0 collective-permute-start.18
  81.7 2.3 %shard_map.56 = (f32[33,31,8,128]{3,2,1,0:T(8,128)}, f32[32,512]{1,0:T(8,128)S(1)}) custom-call(f32[2,32,128]{2,1,0:T(8,128)S(1)} %shard_map.55.refs_0_.refs_5_, f32[2,32,128]{2,1,0:T(8,128)S(1)} %collective-permute-done.17.refs_1_.refs_6_, f32[2,32,128]{2,1,0:T(8,128)S(1)} %collective-permute-done.19.refs_2_.refs_7_, ...), custom_call_target="tpu_custom_call" | custom-call | tf_op jit(solution)/shard_map/pallas_call | solution.py:417
  84.0 0.0 collective-permute-done.16.refs_0_
  84.0 0.0 collective-permute-done.22.refs_3_
  84.0 0.0 collective-permute-done.20.refs_2_
  84.0 0.0 collective-permute-done.18.refs_1_
  84.0 2.4 %shard_map.57 = (f32[33,31,8,128]{3,2,1,0:T(8,128)}, f32[2,33,31,31]{3,2,1,0:T(8,128)S(1)}) custom-call(f32[2,32,128]{2,1,0:T(8,128)S(1)} %collective-permute-done.16.refs_0_, f32[2,32,128]{2,1,0:T(8,128)S(1)} %collective-permute-done.18.refs_1_, f32[2,32,128]{2,1,0:T(8,128)S(1)} %collective-permute-done.20.refs_2_, ...), custom_call_target="tpu_custom_call", output_to_operand_aliasing={{0}: (10, {})} | custom-call | tf_op jit(solution)/shard_map/pallas_call | solution.py:417
  86.4 1.6 %copy.7 = f32[2,33,31,31]{1,0,3,2:T(2,128)} copy(f32[2,33,31,31]{3,2,1,0:T(8,128)S(1)} %get-tuple-element.29) | data formatting | bytes 507408
  (3 shorter events, 0.1 us)
Async XLA Ops:
  0.6 37.1 %copy-start.1 = (f32[512]{0:T(512)S(1)}, f32[512]{0:T(512)}, u32[]{:S(2)}) copy-start(f32[512]{0:T(512)} %param.4) | copy-start | bytes 6148
  0.6 50.0 %copy-start = (f32[64,64]{1,0:T(8,128)S(1)}, f32[64,64]{1,0:T(8,128)}, u32[]{:S(2)}) copy-start(f32[64,64]{1,0:T(8,128)} %constant.33.clone.table_ref) | copy-start | bytes 49156
  1.6 29.3 %collective-permute-start = (f32[128,512]{1,0:T(8,128)S(1)}, f32[128,512]{1,0:T(8,128)S(1)}, u32[]{:S(2)}, u32[]{:S(2)}) collective-permute-start(f32[128,512]{1,0:T(8,128)S(1)} %constant_dynamic-slice_fusion.9), channel_id=1, source_target_pairs={{0,28},{4,24},{8,20},{12,16},{16,12},{20,8},{24,4},{28,0},{1,29},{... | collective-permute-start | bytes 786440 | tf_op jit(solution)/shard_map/ppermute | solution.py:466
  7.2 23.7 %collective-permute-start.2 = (f32[128,384]{1,0:T(8,128)S(1)}, f32[128,384]{1,0:T(8,128)S(1)}, u32[]{:S(2)}, u32[]{:S(2)}) collective-permute-start(f32[128,384]{1,0:T(8,128)S(1)} %get-tuple-element.37), channel_id=1, source_target_pairs={{0,20},{4,16},{8,28},{12,24},{16,4},{20,0},{24,12},{28,8},{1,21},{... | collective-permute-start | bytes 589832 | tf_op jit(solution)/shard_map/ppermute | solution.py:466
  8.7 27.8 %collective-permute-start.6 = (f32[128,512]{1,0:T(8,128)S(1)}, f32[128,512]{1,0:T(8,128)S(1)}, u32[]{:S(2)}, u32[]{:S(2)}) collective-permute-start(f32[128,512]{1,0:T(8,128)S(1)} %get-tuple-element.33), channel_id=1, source_target_pairs={{0,4},{4,0},{8,12},{12,8},{16,20},{20,16},{24,28},{28,24},{1,5},{5... | collective-permute-start | bytes 786440 | tf_op jit(solution)/shard_map/ppermute | solution.py:466
  9.5 25.2 %collective-permute-start.1 = (f32[128,384]{1,0:T(8,128)S(1)}, f32[128,384]{1,0:T(8,128)S(1)}, u32[]{:S(2)}, u32[]{:S(2)}) collective-permute-start(f32[128,384]{1,0:T(8,128)S(1)} %get-tuple-element.38), channel_id=1, source_target_pairs={{0,24},{4,28},{8,16},{12,20},{16,8},{20,12},{24,0},{28,4},{1,25},{... | collective-permute-start | bytes 589832 | tf_op jit(solution)/shard_map/ppermute | solution.py:466
  11.0 26.8 %collective-permute-start.5 = (f32[128,512]{1,0:T(8,128)S(1)}, f32[128,512]{1,0:T(8,128)S(1)}, u32[]{:S(2)}, u32[]{:S(2)}) collective-permute-start(f32[128,512]{1,0:T(8,128)S(1)} %get-tuple-element.34), channel_id=1, source_target_pairs={{0,8},{4,12},{8,0},{12,4},{16,24},{20,28},{24,16},{28,20},{1,9},{5... | collective-permute-start | bytes 786440 | tf_op jit(solution)/shard_map/ppermute | solution.py:466
  30.9 13.2 %collective-permute-start.4 = (f32[128,512]{1,0:T(8,128)S(1)}, f32[128,512]{1,0:T(8,128)S(1)}, u32[]{:S(2)}, u32[]{:S(2)}) collective-permute-start(f32[128,512]{1,0:T(8,128)S(1)} %get-tuple-element.35), channel_id=1, source_target_pairs={{0,12},{4,8},{8,4},{12,0},{16,28},{20,24},{24,20},{28,16},{1,13},{... | collective-permute-start | bytes 786440 | tf_op jit(solution)/shard_map/ppermute | solution.py:466
  30.9 18.6 %collective-permute-start.3 = (f32[128,512]{1,0:T(8,128)S(1)}, f32[128,512]{1,0:T(8,128)S(1)}, u32[]{:S(2)}, u32[]{:S(2)}) collective-permute-start(f32[128,512]{1,0:T(8,128)S(1)} %get-tuple-element.36), channel_id=1, source_target_pairs={{0,16},{4,20},{8,24},{12,28},{16,0},{20,4},{24,8},{28,12},{1,17},{... | collective-permute-start | bytes 786440 | tf_op jit(solution)/shard_map/ppermute | solution.py:466
  34.7 15.9 %collective-permute-start.7 = (f32[128,128]{1,0:T(8,128)S(1)}, f32[128,128]{1,0:T(8,128)S(1)}, u32[]{:S(2)}, u32[]{:S(2)}) collective-permute-start(f32[128,128]{1,0:T(8,128)S(1)} %get-tuple-element.17), channel_id=1, source_target_pairs={{0,20},{4,16},{8,28},{12,24},{16,4},{20,0},{24,12},{28,8},{1,21},{... | collective-permute-start | bytes 196616 | tf_op jit(solution)/shard_map/ppermute | solution.py:466
  36.5 14.1 %collective-permute-start.8 = (f32[128,128]{1,0:T(8,128)S(1)}, f32[128,128]{1,0:T(8,128)S(1)}, u32[]{:S(2)}, u32[]{:S(2)}) collective-permute-start(f32[128,128]{1,0:T(8,128)S(1)} %get-tuple-element.18), channel_id=1, source_target_pairs={{0,24},{4,28},{8,16},{12,20},{16,8},{20,12},{24,0},{28,4},{1,25},{... | collective-permute-start | bytes 196616 | tf_op jit(solution)/shard_map/ppermute | solution.py:466
  55.0 2.1 %collective-permute-start.9 = (f32[4,2,32,128]{3,2,1,0:T(8,128)S(1)}, f32[4,2,32,128]{3,2,1,0:T(8,128)S(1)}, u32[]{:S(2)}, u32[]{:S(2)}) collective-permute-start(f32[4,2,32,128]{3,2,1,0:T(8,128)S(1)} %get-tuple-element.20), channel_id=1, source_target_pairs={{0,4},{4,0},{8,12},{12,8},{16,20},{20,16},{24,28},{28,24},{1,5},{5... | collective-permute-start | bytes 393224 | tf_op jit(solution)/shard_map/ppermute | solution.py:493
  57.1 4.9 %collective-permute-start.10 = (f32[2,32,128]{2,1,0:T(8,128)S(1)}, f32[2,32,128]{2,1,0:T(8,128)S(1)}, u32[]{:S(2)}, u32[]{:S(2)}) collective-permute-start(f32[2,32,128]{2,1,0:T(8,128)S(1)} %get-tuple-element.21), channel_id=1, source_target_pairs={{0,3},{1,2},{2,1},{3,0},{4,7},{5,6},{6,5},{7,4},{8,11},{9,10},{10,... | collective-permute-start | bytes 98312 | tf_op jit(solution)/shard_map/ppermute | solution.py:444
  59.6 3.9 %collective-permute-start.11 = (f32[2,32,128]{2,1,0:T(8,128)S(1)}, f32[2,32,128]{2,1,0:T(8,128)S(1)}, u32[]{:S(2)}, u32[]{:S(2)}) collective-permute-start(f32[2,32,128]{2,1,0:T(8,128)S(1)} %get-tuple-element.22), channel_id=1, source_target_pairs={{0,2},{1,3},{2,0},{3,1},{4,6},{5,7},{6,4},{7,5},{8,10},{9,11},{10,... | collective-permute-start | bytes 98312 | tf_op jit(solution)/shard_map/ppermute | solution.py:444
  60.2 3.9 %collective-permute-start.12 = (f32[2,32,128]{2,1,0:T(8,128)S(1)}, f32[2,32,128]{2,1,0:T(8,128)S(1)}, u32[]{:S(2)}, u32[]{:S(2)}) collective-permute-start(f32[2,32,128]{2,1,0:T(8,128)S(1)} %get-tuple-element.23), channel_id=1, source_target_pairs={{0,1},{1,0},{2,3},{3,2},{4,5},{5,4},{6,7},{7,6},{8,9},{9,8},{10,11... | collective-permute-start | bytes 98312 | tf_op jit(solution)/shard_map/ppermute | solution.py:444
  64.1 6.1 %collective-permute-start.15 = (f32[2,32,128]{2,1,0:T(8,128)S(1)}, f32[2,32,128]{2,1,0:T(8,128)S(1)}, u32[]{:S(2)}, u32[]{:S(2)}) collective-permute-start(f32[2,32,128]{2,1,0:T(8,128)S(1)} %shard_map.54.refs_0_), channel_id=1, source_target_pairs={{0,24},{4,28},{8,16},{12,20},{16,8},{20,12},{24,0},{28,4},{1,25},{... | collective-permute-start | bytes 98312 | tf_op jit(solution)/shard_map/ppermute | solution.py:450
  66.8 4.9 %collective-permute-start.14 = (f32[2,32,128]{2,1,0:T(8,128)S(1)}, f32[2,32,128]{2,1,0:T(8,128)S(1)}, u32[]{:S(2)}, u32[]{:S(2)}) collective-permute-start(f32[2,32,128]{2,1,0:T(8,128)S(1)} %shard_map.54.refs_0_), channel_id=1, source_target_pairs={{0,16},{4,20},{8,24},{12,28},{16,0},{20,4},{24,8},{28,12},{1,17},{... | collective-permute-start | bytes 98312 | tf_op jit(solution)/shard_map/ppermute | solution.py:450
  67.6 4.3 %collective-permute-start.13 = (f32[2,32,128]{2,1,0:T(8,128)S(1)}, f32[2,32,128]{2,1,0:T(8,128)S(1)}, u32[]{:S(2)}, u32[]{:S(2)}) collective-permute-start(f32[2,32,128]{2,1,0:T(8,128)S(1)} %shard_map.54.refs_0_), channel_id=1, source_target_pairs={{0,8},{4,12},{8,0},{12,4},{16,24},{20,28},{24,16},{28,20},{1,9},{5... | collective-permute-start | bytes 98312 | tf_op jit(solution)/shard_map/ppermute | solution.py:450
  75.7 4.9 %collective-permute-start.21 = (f32[2,32,128]{2,1,0:T(8,128)S(1)}, f32[2,32,128]{2,1,0:T(8,128)S(1)}, u32[]{:S(2)}, u32[]{:S(2)}) collective-permute-start(f32[2,32,128]{2,1,0:T(8,128)S(1)} %shard_map.55.refs_0_.refs_5_), channel_id=1, source_target_pairs={{0,3},{1,2},{2,1},{3,0},{4,7},{5,6},{6,5},{7,4},{8,11},{9,10},{10,... | collective-permute-start | bytes 98312 | tf_op jit(solution)/shard_map/ppermute | solution.py:452
  77.3 3.9 %collective-permute-start.19 = (f32[2,32,128]{2,1,0:T(8,128)S(1)}, f32[2,32,128]{2,1,0:T(8,128)S(1)}, u32[]{:S(2)}, u32[]{:S(2)}) collective-permute-start(f32[2,32,128]{2,1,0:T(8,128)S(1)} %shard_map.55.refs_0_.refs_5_), channel_id=1, source_target_pairs={{0,2},{1,3},{2,0},{3,1},{4,6},{5,7},{6,4},{7,5},{8,10},{9,11},{10,... | collective-permute-start | bytes 98312 | tf_op jit(solution)/shard_map/ppermute | solution.py:452
  77.8 3.9 %collective-permute-start.17 = (f32[2,32,128]{2,1,0:T(8,128)S(1)}, f32[2,32,128]{2,1,0:T(8,128)S(1)}, u32[]{:S(2)}, u32[]{:S(2)}) collective-permute-start(f32[2,32,128]{2,1,0:T(8,128)S(1)} %shard_map.55.refs_0_.refs_5_), channel_id=1, source_target_pairs={{0,1},{1,0},{2,3},{3,2},{4,5},{5,4},{6,7},{7,6},{8,9},{9,8},{10,11... | collective-permute-start | bytes 98312 | tf_op jit(solution)/shard_map/ppermute | solution.py:452
  79.2 4.7 %collective-permute-start.16 = (f32[2,32,128]{2,1,0:T(8,128)S(1)}, f32[2,32,128]{2,1,0:T(8,128)S(1)}, u32[]{:S(2)}, u32[]{:S(2)}) collective-permute-start(f32[2,32,128]{2,1,0:T(8,128)S(1)} %shard_map.55.refs_0_.refs_5_), channel_id=1, source_target_pairs={{0,4},{4,0},{8,12},{12,8},{16,20},{20,16},{24,28},{28,24},{1,5},{5... | collective-permute-start | bytes 98312 | tf_op jit(solution)/shard_map/ppermute | solution.py:453
  80.6 3.4 %collective-permute-start.22 = (f32[2,32,128]{2,1,0:T(8,128)S(1)}, f32[2,32,128]{2,1,0:T(8,128)S(1)}, u32[]{:S(2)}, u32[]{:S(2)}) collective-permute-start(f32[2,32,128]{2,1,0:T(8,128)S(1)} %collective-permute-done.21.refs_3_.refs_8_), channel_id=1, source_target_pairs={{0,4},{4,0},{8,12},{12,8},{16,20},{20,16},{24,28},{28,24},{1,5},{5... | collective-permute-start | bytes 98312 | tf_op jit(solution)/shard_map/ppermute | solution.py:453
  81.2 2.9 %collective-permute-start.20 = (f32[2,32,128]{2,1,0:T(8,128)S(1)}, f32[2,32,128]{2,1,0:T(8,128)S(1)}, u32[]{:S(2)}, u32[]{:S(2)}) collective-permute-start(f32[2,32,128]{2,1,0:T(8,128)S(1)} %collective-permute-done.19.refs_2_.refs_7_), channel_id=1, source_target_pairs={{0,4},{4,0},{8,12},{12,8},{16,20},{20,16},{24,28},{28,24},{1,5},{5... | collective-permute-start | bytes 98312 | tf_op jit(solution)/shard_map/ppermute | solution.py:453
  81.7 2.4 %collective-permute-start.18 = (f32[2,32,128]{2,1,0:T(8,128)S(1)}, f32[2,32,128]{2,1,0:T(8,128)S(1)}, u32[]{:S(2)}, u32[]{:S(2)}) collective-permute-start(f32[2,32,128]{2,1,0:T(8,128)S(1)} %collective-permute-done.17.refs_1_.refs_6_), channel_id=1, source_target_pairs={{0,4},{4,0},{8,12},{12,8},{16,20},{20,16},{24,28},{28,24},{1,5},{5... | collective-permute-start | bytes 98312 | tf_op jit(solution)/shard_map/ppermute | solution.py:453
